TPU v7x, 32 devices: a whole 2x2x4 slice. The times are simulated.
32 devices in a mesh: dp: 4 (over z), fsdp: 8 (over y, x, core).
Axes of the slice: x: 2, y: 2, z: 4, core: 2. Of those that a mesh axis runs over, the one named last changes fastest.
Arguments:
- tokens: bfloat16 [32, 1024, 1024], P(('dp', 'fsdp')), may hold values from -6 to 6
- prompt: bfloat16 [32, 128, 1024], P(('dp', 'fsdp')), may hold values from -6 to 6
- prompt_len: int32 [32], P(('dp', 'fsdp')), may hold values from 8 to 128, as said below
- cotangent: bfloat16 [32, 1024, 1024], P(('dp', 'fsdp')), may hold values from -6 to 6
- attn_master: float32 [8, 1024, 1024], P(None, ('dp', 'fsdp')), may hold values from -2 to 2
- attn_first: float32 [8, 1024, 1024], P(None, ('dp', 'fsdp')), may hold values from -0.0034179688 to 0.0034179688
- attn_second: float32 [8, 1024, 1024], P(None, ('dp', 'fsdp')), may hold values from 2.9791412e-08 to 4.766626e-07
- mlp_master: float32 [2, 1024, 4096], P(None, ('dp', 'fsdp')), may hold values from -0.1875 to 0.1875
- mlp_first: float32 [2, 1024, 4096], P(None, ('dp', 'fsdp')), may hold values from -0.0034179688 to 0.0034179688
- mlp_second: float32 [2, 1024, 4096], P(None, ('dp', 'fsdp')), may hold values from 2.9791412e-08 to 4.766626e-07
- norm_master: float32 [6, 1024], P(None, ('dp', 'fsdp')), may hold values from -1.5 to 2.6
- norm_first: float32 [6, 1024], P(None, ('dp', 'fsdp')), may hold values from -0.0068359375 to 0.0068359375
- norm_second: float32 [6, 1024], P(None, ('dp', 'fsdp')), may hold values from 1.1916565e-07 to 1.9066504e-06
Outputs:
- output: bfloat16 [32, 1024, 1024], P(('dp', 'fsdp'))
- token_grad: float32 [32, 1024, 1024], P(('dp', 'fsdp'))
- prompt_grad: float32 [32, 128, 1024], P(('dp', 'fsdp'))
- grad_norm: float32 [], replicated
- attn_first_new: float32 [8, 1024, 1024], P(None, ('dp', 'fsdp'))
- attn_second_new: float32 [8, 1024, 1024], P(None, ('dp', 'fsdp'))
- attn_new: float32 [8, 1024, 1024], P(None, ('dp', 'fsdp'))
- attn_copy: bfloat16 [8, 1024, 1024], P(None, ('dp', 'fsdp'))
- mlp_first_new: float32 [2, 1024, 4096], P(None, ('dp', 'fsdp'))
- mlp_second_new: float32 [2, 1024, 4096], P(None, ('dp', 'fsdp'))
- mlp_new: float32 [2, 1024, 4096], P(None, ('dp', 'fsdp'))
- mlp_copy: bfloat16 [2, 1024, 4096], P(None, ('dp', 'fsdp'))
- norm_first_new: float32 [6, 1024], P(None, ('dp', 'fsdp'))
- norm_second_new: float32 [6, 1024], P(None, ('dp', 'fsdp'))
- norm_new: float32 [6, 1024], P(None, ('dp', 'fsdp'))
- norm_copy: bfloat16 [6, 1024], P(None, ('dp', 'fsdp'))
Inputs may be any that keep to these rules, and one draw needn't show every extreme that they name: `prompt_len`: some item has a prompt of exactly 128 states and some of exactly 8.
All inputs are finite; a program needn't handle non-finite values.
Results may differ from a plain program's by a relative error of at most 0.022.
The roundings to bfloat16 on the way count: a program that leaves them out, or rounds other values in their place, can miss the bound.
Values may be sent and summed in bfloat16 or wider, within the bound.
No kernel may reach another device: no remote copies, remote signals or barrier semaphores. Data moves between devices by JAX's collectives and lax.ppermute only.
A program may use at most 448 MiB of HBM per device.

v0:
```python
import jax
import jax.numpy as jnp
from jax import lax
from jax.sharding import PartitionSpec as P

HD = 64
STEP = 10


EPSILON = 1e-05
CLIP_NORM = 1.0
BETA_ONE = 0.5
BETA_TWO = 0.5
MATRIX_RATE = 0.04
VECTOR_RATE = 0.3
WEIGHT_DECAY = 0.1
ADAM_EPSILON = 1e-08
SCORE_SCALE = 0.125


def layer_norm(vector, norm_gain, norm_bias):
    centre = jnp.mean(vector, axis=-1, keepdims=True)
    centred = vector - centre
    spread = jnp.mean(centred * centred, axis=-1, keepdims=True)
    return centred * lax.rsqrt(spread + EPSILON) * norm_gain + norm_bias


def exact_gelu(values_in):
    return jax.nn.gelu(values_in, approximate=False)


def reduce_owned(members):
    return lax.psum_scatter(members, ("dp", "fsdp"), scatter_dimension=1, tiled=True)


def attend(queries, keys_all, values_all, allowed):
    seq_length = queries.shape[1]
    block_rows = min(512, seq_length)
    outputs = []
    log_sums = []
    for offset in range(0, seq_length, block_rows):
        query_block = queries[:, offset : offset + block_rows]
        scores = (
            jnp.einsum("iqhe,ikhe->ihqk", query_block, keys_all, preferred_element_type=jnp.float32)
            * SCORE_SCALE
        )
        scores = jnp.where(allowed(offset, block_rows), scores, -1000000000.0)
        row_peak = jnp.max(scores, axis=-1, keepdims=True)
        exponent = jnp.exp(scores - row_peak)
        denominator = jnp.sum(exponent, axis=-1, keepdims=True)
        attn_probs = (exponent / denominator).astype(jnp.bfloat16)
        outputs.append(
            jnp.einsum(
                "ihqk,ikhe->iqhe", attn_probs, values_all, preferred_element_type=jnp.float32
            ).astype(jnp.bfloat16)
        )
        log_sums.append(row_peak + jnp.log(denominator))
    return (jnp.concatenate(outputs, axis=1), log_sums)


def attend_back(queries, keys_all, values_all, allowed, log_sums, upstream):
    seq_length = queries.shape[1]
    block_rows = min(512, seq_length)
    grad_keys = jnp.zeros(keys_all.shape, jnp.float32)
    grad_values = jnp.zeros(values_all.shape, jnp.float32)
    grad_queries = []
    for number, offset in enumerate(range(0, seq_length, block_rows)):
        query_block = queries[:, offset : offset + block_rows]
        grad_block = upstream[:, offset : offset + block_rows]
        scores = (
            jnp.einsum("iqhe,ikhe->ihqk", query_block, keys_all, preferred_element_type=jnp.float32)
            * SCORE_SCALE
        )
        scores = jnp.where(allowed(offset, block_rows), scores, -1000000000.0)
        attn_probs = jnp.exp(scores - log_sums[number])
        grad_values = grad_values + jnp.einsum(
            "ihqk,iqhe->ikhe",
            attn_probs.astype(jnp.bfloat16),
            grad_block,
            preferred_element_type=jnp.float32,
        )
        grad_probs = jnp.einsum(
            "iqhe,ikhe->ihqk", grad_block, values_all, preferred_element_type=jnp.float32
        )
        inner_sum = jnp.sum(attn_probs * grad_probs, axis=-1, keepdims=True)
        grad_scores = (attn_probs * (grad_probs - inner_sum)).astype(jnp.bfloat16)
        grad_queries.append(
            jnp.einsum("ihqk,ikhe->iqhe", grad_scores, keys_all, preferred_element_type=jnp.float32)
            * SCORE_SCALE
        )
        grad_keys = (
            grad_keys
            + jnp.einsum(
                "ihqk,iqhe->ikhe", grad_scores, query_block, preferred_element_type=jnp.float32
            )
            * SCORE_SCALE
        )
    return (jnp.concatenate(grad_queries, axis=1), grad_keys, grad_values)


def adam_update(master, first, second, gradient, factor, rate, decay):
    gradient = gradient * factor
    first_new = BETA_ONE * first + (1.0 - BETA_ONE) * gradient
    second_new = BETA_TWO * second + (1.0 - BETA_TWO) * gradient * gradient
    first_fix = 1.0 - BETA_ONE**STEP
    second_fix = 1.0 - BETA_TWO**STEP
    update = first_new / first_fix / (jnp.sqrt(second_new / second_fix) + ADAM_EPSILON)
    master_new = master - rate * (update + decay * master)
    return (first_new, second_new, master_new, master_new.astype(jnp.bfloat16))


def local(
    tokens,
    prompt,
    prompt_len,
    cotangent,
    attn_master,
    attn_first,
    attn_second,
    mlp_master,
    mlp_first,
    mlp_second,
    norm_master,
    norm_first,
    norm_second,
):
    item_count, seq_length, model_width = tokens.shape
    prompt_rows = prompt.shape[1]
    head_count = model_width // HD
    row_count = item_count * seq_length
    head_shape = (item_count, seq_length, head_count, HD)
    prompt_shape = (item_count, prompt_rows, head_count, HD)
    attn_low = attn_master.astype(jnp.bfloat16)
    mlp_low = mlp_master.astype(jnp.bfloat16)
    norm_low = norm_master.astype(jnp.bfloat16)

    def causal(offset, block_rows):
        positions = offset + jnp.arange(block_rows, dtype=jnp.int32)
        return (positions[:, None] >= jnp.arange(seq_length, dtype=jnp.int32)[None, :])[None, None]

    def padded(offset, block_rows):
        return (jnp.arange(prompt_rows, dtype=jnp.int32)[None, :] < prompt_len[:, None])[
            :, None, None, :
        ]

    self_w, norm_w = (
        lax.all_gather(attn_low[:4], ("dp", "fsdp"), axis=1, tiled=True),
        lax.all_gather(norm_low, ("dp", "fsdp"), axis=1, tiled=True),
    )
    norm_gains = norm_w.astype(jnp.float32)
    inputs = tokens.reshape(row_count, model_width).astype(jnp.float32)
    normed_one, norm_pull_one = jax.vjp(layer_norm, inputs, norm_gains[0], norm_gains[1])
    normed_one = normed_one.astype(jnp.bfloat16)
    projected = jnp.einsum(
        "rd,kde->kre", normed_one, self_w[:3], preferred_element_type=jnp.float32
    ).astype(jnp.bfloat16)
    queries = projected[0].reshape(head_shape)
    keys_self = projected[1].reshape(head_shape)
    values_self = projected[2].reshape(head_shape)
    mixed, self_sums = attend(queries, keys_self, values_self, causal)
    mixed_rows = mixed.reshape(row_count, model_width)
    after_self = inputs + jnp.dot(mixed_rows, self_w[3], preferred_element_type=jnp.float32)
    cross_w = lax.all_gather(attn_low[4:], ("dp", "fsdp"), axis=1, tiled=True)
    normed_two, norm_pull_two = jax.vjp(layer_norm, after_self, norm_gains[2], norm_gains[3])
    normed_two = normed_two.astype(jnp.bfloat16)
    cross_queries = (
        jnp.dot(normed_two, cross_w[0], preferred_element_type=jnp.float32)
        .astype(jnp.bfloat16)
        .reshape(head_shape)
    )
    states = prompt.reshape(item_count * prompt_rows, model_width)
    cross_pair = jnp.einsum(
        "rd,kde->kre", states, cross_w[1:3], preferred_element_type=jnp.float32
    ).astype(jnp.bfloat16)
    cross_keys = cross_pair[0].reshape(prompt_shape)
    cross_values = cross_pair[1].reshape(prompt_shape)
    crossed, cross_sums = attend(cross_queries, cross_keys, cross_values, padded)
    crossed_rows = crossed.reshape(row_count, model_width)
    after_cross = after_self + jnp.dot(crossed_rows, cross_w[3], preferred_element_type=jnp.float32)
    mlp_w = lax.all_gather(mlp_low, ("dp", "fsdp"), axis=1, tiled=True)
    normed_three, norm_pull_three = jax.vjp(layer_norm, after_cross, norm_gains[4], norm_gains[5])
    normed_three = normed_three.astype(jnp.bfloat16)
    hidden = jnp.dot(normed_three, mlp_w[0], preferred_element_type=jnp.float32)
    activated, gelu_pull = jax.vjp(exact_gelu, hidden)
    activated = activated.astype(jnp.bfloat16)
    result = after_cross + jnp.einsum(
        "rf,df->rd", activated, mlp_w[1], preferred_element_type=jnp.float32
    )
    output = result.astype(jnp.bfloat16).reshape(item_count, seq_length, model_width)
    mlp_w = lax.all_gather(mlp_low, ("dp", "fsdp"), axis=1, tiled=True)
    grad_out = cotangent.reshape(row_count, model_width)
    grad_down = jnp.einsum("rd,rf->df", grad_out, activated, preferred_element_type=jnp.float32)
    grad_act = jnp.einsum("rd,df->rf", grad_out, mlp_w[1], preferred_element_type=jnp.float32)
    grad_hidden = gelu_pull(grad_act)[0].astype(jnp.bfloat16)
    grad_up = jnp.einsum("rd,rf->df", normed_three, grad_hidden, preferred_element_type=jnp.float32)
    grad_normed_three = jnp.einsum(
        "rf,df->rd", grad_hidden, mlp_w[0], preferred_element_type=jnp.float32
    )
    grad_part_three, grad_gain_three, grad_bias_three = norm_pull_three(grad_normed_three)
    grad_after_cross = grad_out.astype(jnp.float32) + grad_part_three
    mlp_grads = reduce_owned((jnp.stack([grad_up, grad_down]),))[0]
    cross_w = lax.all_gather(attn_low[4:], ("dp", "fsdp"), axis=1, tiled=True)
    grad_cross_branch = grad_after_cross.astype(jnp.bfloat16)
    grad_cross_out = jnp.einsum(
        "rd,re->de", crossed_rows, grad_cross_branch, preferred_element_type=jnp.float32
    )
    grad_crossed = (
        jnp.einsum("re,de->rd", grad_cross_branch, cross_w[3], preferred_element_type=jnp.float32)
        .astype(jnp.bfloat16)
        .reshape(head_shape)
    )
    grad_cq, grad_ck, grad_cv = attend_back(
        cross_queries, cross_keys, cross_values, padded, cross_sums, grad_crossed
    )
    grad_cq = grad_cq.astype(jnp.bfloat16).reshape(row_count, model_width)
    grad_ckv = (
        jnp.stack([grad_ck, grad_cv])
        .astype(jnp.bfloat16)
        .reshape(2, item_count * prompt_rows, model_width)
    )
    grad_cross_query = jnp.einsum(
        "rd,re->de", normed_two, grad_cq, preferred_element_type=jnp.float32
    )
    grad_cross_pair = jnp.einsum(
        "rd,kre->kde", states, grad_ckv, preferred_element_type=jnp.float32
    )
    grad_states = jnp.einsum(
        "kre,kde->rd", grad_ckv, cross_w[1:3], preferred_element_type=jnp.float32
    )
    prompt_grad = grad_states.reshape(item_count, prompt_rows, model_width)
    grad_normed_two = jnp.einsum(
        "re,de->rd", grad_cq, cross_w[0], preferred_element_type=jnp.float32
    )
    grad_part_two, grad_gain_two, grad_bias_two = norm_pull_two(grad_normed_two)
    grad_after_self = grad_after_cross + grad_part_two
    cross_stack = jnp.concatenate(
        [grad_cross_query[None], grad_cross_pair, grad_cross_out[None]], axis=0
    )
    cross_grads = reduce_owned((cross_stack,))[0]
    self_w = lax.all_gather(attn_low[:4], ("dp", "fsdp"), axis=1, tiled=True)
    grad_self_branch = grad_after_self.astype(jnp.bfloat16)
    grad_self_out = jnp.einsum(
        "rd,re->de", mixed_rows, grad_self_branch, preferred_element_type=jnp.float32
    )
    grad_mixed = (
        jnp.einsum("re,de->rd", grad_self_branch, self_w[3], preferred_element_type=jnp.float32)
        .astype(jnp.bfloat16)
        .reshape(head_shape)
    )
    grad_q, grad_k, grad_v = attend_back(
        queries, keys_self, values_self, causal, self_sums, grad_mixed
    )
    grad_qkv = (
        jnp.stack([grad_q, grad_k, grad_v]).astype(jnp.bfloat16).reshape(3, row_count, model_width)
    )
    grad_projections = jnp.einsum(
        "rd,kre->kde", normed_one, grad_qkv, preferred_element_type=jnp.float32
    )
    grad_normed_one = jnp.einsum(
        "kre,kde->rd", grad_qkv, self_w[:3], preferred_element_type=jnp.float32
    )
    grad_part_one, grad_gain_one, grad_bias_one = norm_pull_one(grad_normed_one)
    token_grad = (grad_after_self + grad_part_one).reshape(item_count, seq_length, model_width)
    self_stack = jnp.concatenate([grad_projections, grad_self_out[None]], axis=0)
    norm_stack = jnp.stack(
        [
            grad_gain_one,
            grad_bias_one,
            grad_gain_two,
            grad_bias_two,
            grad_gain_three,
            grad_bias_three,
        ]
    )
    self_grads, norm_grads = reduce_owned((self_stack, norm_stack))
    attn_grads = jnp.concatenate([self_grads, cross_grads], axis=0)
    local_squares = (
        jnp.sum(attn_grads * attn_grads)
        + jnp.sum(mlp_grads * mlp_grads)
        + jnp.sum(norm_grads * norm_grads)
    )
    grad_norm = jnp.sqrt(lax.psum(local_squares, ("dp", "fsdp")))
    factor = CLIP_NORM / jnp.maximum(grad_norm, CLIP_NORM)
    attn_out = adam_update(
        attn_master, attn_first, attn_second, attn_grads, factor, MATRIX_RATE, WEIGHT_DECAY
    )
    mlp_out = adam_update(
        mlp_master, mlp_first, mlp_second, mlp_grads, factor, MATRIX_RATE, WEIGHT_DECAY
    )
    norm_out = adam_update(
        norm_master, norm_first, norm_second, norm_grads, factor, VECTOR_RATE, 0.0
    )
    return (
        output,
        token_grad,
        prompt_grad,
        grad_norm,
        attn_out[0],
        attn_out[1],
        attn_out[2],
        attn_out[3],
        mlp_out[0],
        mlp_out[1],
        mlp_out[2],
        mlp_out[3],
        norm_out[0],
        norm_out[1],
        norm_out[2],
        norm_out[3],
    )


def solution(mesh):
    return jax.shard_map(
        local,
        mesh=mesh,
        in_specs=(
            P(("dp", "fsdp"), None, None),
            P(("dp", "fsdp"), None, None),
            P(("dp", "fsdp")),
            P(("dp", "fsdp"), None, None),
            P(None, ("dp", "fsdp"), None),
            P(None, ("dp", "fsdp"), None),
            P(None, ("dp", "fsdp"), None),
            P(None, ("dp", "fsdp"), None),
            P(None, ("dp", "fsdp"), None),
            P(None, ("dp", "fsdp"), None),
            P(None, ("dp", "fsdp")),
            P(None, ("dp", "fsdp")),
            P(None, ("dp", "fsdp")),
        ),
        out_specs=(
            P(("dp", "fsdp"), None, None),
            P(("dp", "fsdp"), None, None),
            P(("dp", "fsdp"), None, None),
            P(),
            P(None, ("dp", "fsdp"), None),
            P(None, ("dp", "fsdp"), None),
            P(None, ("dp", "fsdp"), None),
            P(None, ("dp", "fsdp"), None),
            P(None, ("dp", "fsdp"), None),
            P(None, ("dp", "fsdp"), None),
            P(None, ("dp", "fsdp"), None),
            P(None, ("dp", "fsdp"), None),
            P(None, ("dp", "fsdp")),
            P(None, ("dp", "fsdp")),
            P(None, ("dp", "fsdp")),
            P(None, ("dp", "fsdp")),
        ),
        check_vma=False,
    )
```

profile of v0, /device:TPU:0, one launch (start us, length us, event | category | flops | bytes accessed | tf_op | source)
XLA Modules:
  0.0 1768.1 jit_solution(7505683509455524190)
XLA Ops:
  13.6 43.5 %all-gather = bf16[32,32,6]{1,2,0:T(8,128)(2,1)S(1)} all-gather(bf16[1,32,6]{1,2,0:T(8,128)(2,1)S(1)} %convert_bitcast_fusion.2), channel_id=1, replica_groups=mesh['dp'=4,'fsdp'=8] {'dp','fsdp'}, dimensions={0}, use_global_device_ids=true | all-gather | bytes 12672 | tf_op jit(solution)/shard_map/all_gather | solution.py:148
  67.9 23.6 %all-gather.7.cloned.1.call-done = bf16[4,1024,1024]{2,0,1:T(4,128)(2,1)} async-done(((bf16[4,32,1024]{2,0,1:T(4,128)(2,1)}), bf16[4,1024,1024]{2,0,1:T(4,128)(2,1)}) %all-gather.7.cloned.1.call-update) | async-done | bytes 8388624 | tf_op jit(solution)/shard_map/all_gather | solution.py:163
  112.8 58.3 %all-gather.5.cloned.1.call-done = bf16[4,1024,1024]{2,0,1:T(4,128)(2,1)} async-done(((bf16[4,32,1024]{2,0,1:T(4,128)(2,1)}), bf16[4,1024,1024]{2,0,1:T(4,128)(2,1)}) %all-gather.5.cloned.1.call-update) | async-done | bytes 8388624 | tf_op jit(solution)/shard_map/all_gather | solution.py:147
  205.2 14.3 fusion.115
  233.2 16.9 fusion.1
  277.2 13.9 fusion.64
  323.8 47.4 %multiply_convert_fusion.2 = (bf16[1024,4096]{1,0:T(8,128)(2,1)}, f32[1024,4096]{1,0:T(8,128)}, f32[1024,4096]{1,0:T(8,128)}) fusion(bf16[2,1024,4096]{2,1,0:T(8,128)(2,1)} %all-gather.9.cloned.1.call-done, bf16[1024,1024]{0,1:T(8,128)(2,1)S(1)} %add_convert_fusion.6.clone.5), kind=kOutput, calls=%fused_computation.26 | convolution fusion | flops 8862564352 | bytes 52428800 | tf_op jit(solution)/shard_map/dot_general | solution.py:183
  371.3 19.7 %add_convert_fusion = bf16[1024,4096]{1,0:T(8,128)(2,1)S(1)} fusion(f32[1024,4096]{1,0:T(8,128)} %get-tuple-element.119, f32[1024,4096]{1,0:T(8,128)} %get-tuple-element.147, bf16[2,1024,4096]{2,1,0:T(8,128)(2,1)} %all-gather.9.cloned.1.call-done, bf16[1,1024,1024]{2,1,0:T(8,128)(2,1)S(1)} %copy-done.51), kind=kOutput, calls=%fused_computation.25 | convolution fusion | flops 8648654848 | bytes 52428800 | tf_op jit(solution)/shard_map/rd,df->rf/dot_general | solution.py:193
  390.9 16.3 fusion.123
  475.4 15.4 fusion.5
  490.8 22.4 %multiply_reduce_fusion = (f32[16,512]{1,0:T(8,128)S(1)}, f32[16,512,1024]{2,1,0:T(8,128)}) fusion(f32[16,512,1024]{2,1,0:T(8,128)} %get-tuple-element.136, f32[16,512]{1,0:T(8,128)S(1)} %copy-done.62, bf16[1024,16,64]{0,2,1:T(8,128)(2,1)S(1)} %bitcast.313, bf16[1,1024,16,64]{1,3,2,0:T(8,128)(2,1)S(1)} %bitcast.320), kind=kOutput, calls=%fused_computation.2 | convolution fusion | flops 1098899456 | bytes 70320128 | tf_op jit(solution)/shard_map/iqhe,ikhe->ihqk/dot_general | solution.py:82
  513.3 22.3 %multiply_reduce_fusion.1 = (f32[16,512]{1,0:T(8,128)S(1)}, f32[16,512,1024]{2,1,0:T(8,128)}) fusion(f32[16,512,1024]{2,1,0:T(8,128)} %get-tuple-element.138, f32[16,512]{1,0:T(8,128)S(1)} %copy-done.63, bf16[1024,16,64]{0,2,1:T(8,128)(2,1)S(1)} %bitcast.314, bf16[1,1024,16,64]{1,3,2,0:T(8,128)(2,1)S(1)} %bitcast.321), kind=kOutput, calls=%fused_computation.5 | convolution fusion | flops 1098899456 | bytes 70320128 | tf_op jit(solution)/shard_map/iqhe,ikhe->ihqk/dot_general | solution.py:82
  535.5 28.0 %multiply_convert_fusion.1 = bf16[16,512,1024]{2,1,0:T(8,128)(2,1)} fusion(f32[16,512,1024]{2,1,0:T(8,128)} %get-tuple-element.153, f32[16,512,1024]{2,1,0:T(8,128)} %get-tuple-element.138, f32[16,512]{1,0:T(8,128)S(1)} %get-tuple-element.152, f32[16,512]{1,0:T(8,128)S(1)} %copy-done.63), kind=kLoop, calls=%fused_computation.4 | loop fusion | flops 33554432 | bytes 83951616 | tf_op jit(solution)/shard_map/convert_element_type | solution.py:86
  585.7 16.5 add_convert_fusion.1
  606.2 27.9 %multiply_convert_fusion = bf16[16,512,1024]{2,1,0:T(8,128)(2,1)} fusion(f32[16,512,1024]{2,1,0:T(8,128)} %get-tuple-element.155, f32[16,512,1024]{2,1,0:T(8,128)} %get-tuple-element.136, f32[16,512]{1,0:T(8,128)S(1)} %get-tuple-element.154, f32[16,512]{1,0:T(8,128)S(1)} %copy-done.62), kind=kLoop, calls=%fused_computation.1 | loop fusion | flops 33554432 | bytes 83951616 | tf_op jit(solution)/shard_map/convert_element_type | solution.py:86
  724.5 20.2 %copy.239 = f32[4,1024,1024]{2,0,1:T(4,128)} copy(f32[4,1024,1024]{1,2,0:T(8,128)} %pad_maximum_fusion.2) | data formatting | bytes 33554432 | tf_op jit(solution)/shard_map/concatenate | solution.py:236
  744.7 20.2 %copy.235 = f32[4,1024,1024]{2,0,1:T(4,128)} copy(f32[4,1024,1024]{1,2,0:T(8,128)} %pad_maximum_fusion.1) | data formatting | bytes 33554432 | tf_op jit(solution)/shard_map/concatenate | solution.py:264
  765.1 16.5 convolution_bitcast_fusion
  781.6 14.9 convolution_bitcast_fusion.1
  796.4 23.0 %pad_maximum_fusion = f32[2,1024,4096]{2,1,0:T(8,128)} fusion(f32[1,1024,4096]{2,1,0:T(8,128)} %convolution_bitcast_fusion, f32[1,1024,4096]{2,1,0:T(8,128)} %convolution_bitcast_fusion.1), kind=kLoop, calls=%fused_computation | loop fusion | flops 8388608 | bytes 67108864 | tf_op jit(solution)/shard_map/stack | solution.py:201
  819.5 15.4 fusion.55
  850.5 488.8 %all-reduce.5.cloned.1.call-done = (f32[4,1024,1024]{2,0,1:T(4,128)}, f32[4,1024,1024]{2,0,1:T(4,128)}) async-done(((f32[4,1024,1024]{2,0,1:T(4,128)}, f32[4,1024,1024]{2,0,1:T(4,128)}), (f32[4,1024,1024]{2,0,1:T(4,128)}, f32[4,1024,1024]{2,0,1:T(4,128)})) %all-reduce.5.cloned.1.call-update) | async-done | bytes 33554448
  1342.0 353.3 %reduce-scatter.5.cloned.1.call-done = f32[2,32,4096]{2,1,0:T(8,128)} async-done(((f32[2,1024,4096]{2,1,0:T(8,128)}), f32[2,32,4096]{2,1,0:T(8,128)}) %reduce-scatter.5.cloned.1.call-update) | async-done | bytes 1048592 | tf_op jit(solution)/shard_map/reduce_scatter | solution.py:33
  1704.9 46.9 %psum.7 = f32[]{:T(128)} all-reduce(f32[]{:T(128)S(6)} %add.253), channel_id=1, replica_groups=mesh['dp'=4,'fsdp'=8] {'dp','fsdp'}, use_global_device_ids=true, to_apply=%region_37.38 | all-reduce | flops 1 | bytes 8 | tf_op jit(solution)/shard_map/psum | solution.py:282
  (358 shorter events, 362.2 us)
Async XLA Ops:
  7.2 289.6 %copy-start = (bf16[1,128,1024]{2,1,0:T(8,128)(2,1)S(1)}, bf16[1,128,1024]{2,1,0:T(8,128)(2,1)}, u32[]{:S(2)}) copy-start(bf16[1,128,1024]{2,1,0:T(8,128)(2,1)} %param.14) | copy-start | bytes 786436
  7.2 84.3 %all-gather.7.cloned.1.call-start = ((), (), s32[]{:S(2)}) async-start(), calls=%async_computation.3 | async-start | bytes 8650752 | tf_op jit(solution)/shard_map/all_gather | solution.py:163
  10.0 161.0 %all-gather.5.cloned.1.call-start = ((), (), s32[]{:S(2)}) async-start(), calls=%async_computation.2 | async-start | bytes 8650752 | tf_op jit(solution)/shard_map/all_gather | solution.py:147
  10.8 313.0 %all-gather.9.cloned.1.call-start = ((), (), s32[]{:S(2)}) async-start(), calls=%async_computation.4 | async-start | bytes 17301504 | tf_op jit(solution)/shard_map/all_gather | solution.py:180
  12.9 836.2 %reduce-scatter.7.cloned.1.call-start = ((), (), s32[]{:S(2)}) async-start(), calls=%async_computation.6 | async-start | bytes 540672
  60.1 134.3 %copy-start.4 = (bf16[1,1024,1024]{1,2,0:T(8,128)(2,1)}, bf16[1,1024,1024]{1,2,0:T(8,128)(2,1)S(1)}, u32[]{:S(2)}) copy-start(bf16[1,1024,1024]{1,2,0:T(8,128)(2,1)S(1)} %copy.203) | copy-start | bytes 6291460
  65.7 128.7 %copy-start.71 = (f32[1024]{0:T(1024)}, f32[1024]{0:T(1024)S(1)}, u32[]{:S(2)}) copy-start(f32[1024]{0:T(1024)S(1)} %broadcast_multiply_fusion.2) | copy-start | bytes 12292
  67.0 127.5 %copy-start.88 = (f32[1024]{0:T(1024)}, f32[1024]{0:T(1024)S(1)}, u32[]{:S(2)}) copy-start(f32[1024]{0:T(1024)S(1)} %fusion.90) | copy-start | bytes 12292
  67.6 126.9 %copy-start.84 = (f32[1,1024]{1,0:T(1,128)}, f32[1,1024]{1,0:T(1,128)S(1)}, u32[]{:S(2)}) copy-start(f32[1,1024]{1,0:T(1,128)S(1)} %get-tuple-element.134) | copy-start | bytes 12292
  67.6 126.9 %copy-start.106 = (f32[1,1024]{1,0:T(1,128)}, f32[1,1024]{1,0:T(1,128)S(1)}, u32[]{:S(2)}) copy-start(f32[1,1024]{1,0:T(1,128)S(1)} %get-tuple-element.133) | copy-start | bytes 12292
  205.2 72.0 %copy-start.26 = (bf16[1,1024,1024]{1,2,0:T(8,128)(2,1)}, bf16[1,1024,1024]{1,2,0:T(8,128)(2,1)S(1)}, u32[]{:S(2)}) copy-start(bf16[1,1024,1024]{1,2,0:T(8,128)(2,1)S(1)} %get-tuple-element.124) | copy-start | bytes 6291460
  233.2 22.8 %copy-start.1 = (f32[16,512,1024]{2,1,0:T(8,128)S(1)}, f32[16,512,1024]{2,1,0:T(8,128)}, u32[]{:S(2)}) copy-start(f32[16,512,1024]{2,1,0:T(8,128)} %get-tuple-element.138) | copy-start | bytes 100663296
  263.6 37.7 %slice-start = ((s8[8388608]{0:T(1024)(128)(4,1)}), s8[4194304]{0:T(1024)(128)(4,1)S(1)}, s32[]{:S(2)}) async-start(s8[8388608]{0:T(1024)(128)(4,1)} %bitcast.316), calls=%async_computation.8 | async-start | bytes 8388608
  277.2 24.1 %slice-start.1 = ((s8[8388608]{0:T(1024)(128)(4,1)}), s8[4194304]{0:T(1024)(128)(4,1)S(1)}, s32[]{:S(2)}) async-start(s8[8388608]{0:T(1024)(128)(4,1)} %bitcast.316), calls=%async_computation.9 | async-start | bytes 8388608
  323.8 47.4 %copy-start.51 = (bf16[1,1024,1024]{2,1,0:T(8,128)(2,1)S(1)}, bf16[1,1024,1024]{2,1,0:T(8,128)(2,1)}, u32[]{:S(2)}) copy-start(bf16[1,1024,1024]{2,1,0:T(8,128)(2,1)} %param.16) | copy-start | bytes 6291460
  470.8 42.4 %copy-start.31 = (bf16[1024,1024]{0,1:T(8,128)(2,1)}, bf16[1024,1024]{0,1:T(8,128)(2,1)S(1)}, u32[]{:S(2)}) copy-start(bf16[1024,1024]{0,1:T(8,128)(2,1)S(1)} %convolution_convert_fusion) | copy-start | bytes 6291460
  535.5 28.1 %copy-start.3 = (bf16[1,1024,1024]{1,2,0:T(8,128)(2,1)S(1)}, bf16[1,1024,1024]{1,2,0:T(8,128)(2,1)}, u32[]{:S(2)}) copy-start(bf16[1,1024,1024]{1,2,0:T(8,128)(2,1)} %copy-done.2) | copy-start | bytes 6291460
  702.8 636.4 %all-reduce.5.cloned.1.call-start = ((), (), s32[]{:S(2)}) async-start(), calls=%async_computation.7 | async-start | bytes 67108864
  765.0 930.4 %reduce-scatter.5.cloned.1.call-start = ((), (), s32[]{:S(2)}) async-start(), calls=%async_computation.5 | async-start | bytes 34603008 | tf_op jit(solution)/shard_map/reduce_scatter | solution.py:33
  1699.4 53.1 %copy-start.101 = (f32[6,32]{1,0:T(8,128)S(1)}, f32[6,32]{1,0:T(8,128)}, u32[]{:S(2)}) copy-start(f32[6,32]{1,0:T(8,128)} %param.23) | copy-start | bytes 2308
  1699.4 53.1 %copy-start.104 = (f32[6,32]{1,0:T(8,128)S(1)}, f32[6,32]{1,0:T(8,128)}, u32[]{:S(2)}) copy-start(f32[6,32]{1,0:T(8,128)} %param.25) | copy-start | bytes 2308
  1699.4 53.1 %copy-start.105 = (f32[6,32]{1,0:T(8,128)S(1)}, f32[6,32]{1,0:T(8,128)}, u32[]{:S(2)}) copy-start(f32[6,32]{1,0:T(8,128)} %param.24) | copy-start | bytes 2308
  1699.4 53.8 %copy-start.34 = (f32[8,32,1024]{2,1,0:T(8,128)S(1)}, f32[8,32,1024]{2,1,0:T(8,128)}, u32[]{:S(2)}) copy-start(f32[8,32,1024]{2,1,0:T(8,128)} %param.17) | copy-start | bytes 3145732
  1704.9 52.6 %copy-start.35 = (f32[2,32,4096]{2,1,0:T(8,128)S(1)}, f32[2,32,4096]{2,1,0:T(8,128)}, u32[]{:S(2)}) copy-start(f32[2,32,4096]{2,1,0:T(8,128)} %param.20) | copy-start | bytes 3145732
  (96 other events, 664.5 us)
Sparse Core Ops, SparseCore 0:
  11.5 80.0 all-gather.6
  95.0 76.0 all-gather.4
  174.5 113.3 all-gather.8
  703.0 132.4 reduce-scatter.6
  842.9 496.3 all-reduce.4
  1341.4 353.8 reduce-scatter.4
where the time goes:
time: 1780 us; the launch traced here: 1770 us
  waiting for transfers between devices  925 us (52%)
  matrix products  392 us (22%)
  other arithmetic  178 us (10%)
  local copies, waits for them, and re-layouts  163 us (9%)
  blocking collectives  90.4 us (5%)
  between operations  20.4 us (1%)
    unnamed x8, waiting for transfers between devices  490 us
    reduce_scatter x1, waiting for transfers between devices, reduce_owned(): lax.psum_scatter(members, ('dp', 'fsdp'), scatter_dimension=1, tiled=True)  353 us
    unnamed x239, local copies, waits for them, and re-layouts  67.7 us
    convert_element_type x4, other arithmetic, attend_back(): grad_scores = (attn_probs * (grad_probs - inner_sum)).astype(jnp.bfloat16)  58.8 us
    all_gather x1, waiting for transfers between devices, local(): lax.all_gather(attn_low[:4], ('dp', 'fsdp'), axis=1, tiled=True)  58.3 us
    dot_general x1, matrix products, local(): hidden = jnp.dot(normed_three, mlp_w[0], preferred_element_type=jnp.float32)  47.4 us
    psum x1, blocking collectives, local(): grad_norm = jnp.sqrt(lax.psum(local_squares, ('dp', 'fsdp')))  46.9 us
    dot_general x4, matrix products, attend_back(): jnp.einsum('iqhe,ikhe->ihqk', grad_block, values_all, preferred_element_t...  46.8 us
  transfers between devices with their start and end apart: 6, of which 4 were waited for; matrix products, arithmetic and copies ran while one was open for 18% of the time, Pallas kernels for 0%

commit v1 on v0

v1 whole, which is shorter than its diff:
```python
import functools

import jax
import jax.numpy as jnp
from jax import lax
from jax.experimental import pallas as pl
from jax.experimental.pallas import tpu as pltpu
from jax.sharding import PartitionSpec as P

HD = 64
PAIR = 2 * HD
STEP = 10
TILE = 256

EPSILON = 1e-05
CLIP_NORM = 1.0
BETA_ONE = 0.5
BETA_TWO = 0.5
MATRIX_RATE = 0.04
VECTOR_RATE = 0.3
WEIGHT_DECAY = 0.1
ADAM_EPSILON = 1e-08
SCORE_SCALE = 0.125
MASKED = -1000000000.0
AXES = ("dp", "chip", "core")
LOW = jnp.bfloat16
FULL = jnp.float32


def dot_nn(left, right):
    return lax.dot_general(left, right, (((1,), (0,)), ((), ())), preferred_element_type=FULL)


def dot_nt(left, right):
    return lax.dot_general(left, right, (((1,), (1,)), ((), ())), preferred_element_type=FULL)


def dot_tn(left, right):
    return lax.dot_general(left, right, (((0,), (0,)), ((), ())), preferred_element_type=FULL)


def lane_masks(rows):
    lane = lax.broadcasted_iota(jnp.int32, (rows, PAIR), 1)
    return (lane < HD, lane >= HD)


def forward_pair(queries, keys, values, causal, limit):
    seq = queries.shape[0]
    span = keys.shape[0]
    block = min(TILE, seq)
    masks = lane_masks(block)
    key_masks = lane_masks(span)
    counted = [jnp.where(mask, values, jnp.ones_like(values)) for mask in key_masks]

    def score(start):
        found = []
        for head in range(2):
            query = queries[start : start + block]
            query = jnp.where(masks[head], query, jnp.zeros_like(query)) * SCORE_SCALE
            if causal:
                row = lax.broadcasted_iota(jnp.int32, (block, block), 0)
                col = lax.broadcasted_iota(jnp.int32, (block, block), 1)
                parts = [(start, start + block, col <= row)]
                if start:
                    parts.append((0, start, None))
            else:
                col = lax.broadcasted_iota(jnp.int32, (block, span), 1)
                parts = [(0, span, col < limit)]
            scores = []
            for low, high, allowed in parts:
                value = dot_nt(query, keys[low:high])
                if allowed is not None:
                    value = jnp.where(allowed, value, MASKED)
                scores.append((low, high, value))
            found.append(scores)
        return found

    results = []
    ahead = score(0)
    for start in range(0, seq, block):
        found = ahead
        if start + block < seq:
            ahead = score(start + block)
        peaks, sums = [], []
        for head in range(2):
            peak = None
            for _, _, value in found[head]:
                most = jnp.max(value, axis=1, keepdims=True)
                peak = most if peak is None else jnp.maximum(peak, most)
            peaks.append(peak)
        for head in range(2):
            mixed = None
            for low, high, value in found[head]:
                weight = jnp.exp(value - peaks[head]).astype(LOW)
                part = dot_nn(weight, counted[head][low:high])
                mixed = part if mixed is None else mixed + part
            sums.append(mixed)
        mixed = jnp.where(masks[0], sums[0], sums[1])
        total = pltpu.roll(jnp.where(masks[0], sums[1], sums[0]), HD, 1)
        level = jnp.where(masks[0], peaks[0], peaks[1]) + jnp.log(total)
        results.append((start, start + block, (mixed / total).astype(LOW), level.T))
    return results


def backward_pair(queries, keys, values, mixed, upstream, levels, causal, limit):
    seq = queries.shape[0]
    span = keys.shape[0]
    block = min(TILE, span)
    masks = lane_masks(block)
    scaled = queries * SCORE_SCALE
    inner = (upstream.astype(FULL) * mixed.astype(FULL)).T
    products = [
        jnp.sum(inner[HD * head : HD * (head + 1)], axis=0, keepdims=True) for head in range(2)
    ]
    units = []
    for low in range(0, span, block):
        for head in range(2):
            if not causal:
                units.append((low, head, 0, seq, True))
                continue
            units.append((low, head, low, low + block, True))
            if low + block < seq:
                units.append((low, head, low + block, seq, False))

    def scores(unit):
        low, head, begin, end, checked = unit
        key, value = keys[low : low + block], values[low : low + block]
        key = jnp.where(masks[head], key, jnp.zeros_like(key))
        value = jnp.where(masks[head], value, jnp.zeros_like(value))
        return dot_nt(key, scaled[begin:end]), dot_nt(value, upstream[begin:end])

    def exponents(unit, score, grad_weight):
        low, head, begin, end, checked = unit
        if checked:
            row = lax.broadcasted_iota(jnp.int32, (block, end - begin), 0) + low
            if causal:
                col = lax.broadcasted_iota(jnp.int32, (block, end - begin), 1) + begin
                allowed = row <= col
            else:
                allowed = row < limit
            score = jnp.where(allowed, score, MASKED)
        weight = jnp.exp(score - levels[8 * head : 8 * head + 1, begin:end])
        grad_score = (weight * (grad_weight - products[head][:, begin:end])).astype(LOW)
        return weight.astype(LOW), grad_score

    grad_q = [[None] * (seq // block) for _ in range(2)]
    sums_k, sums_v = {}, {}

    def gather(unit, weight, grad_score):
        low, head, begin, end, _ = unit
        part_v = dot_nn(weight, upstream[begin:end])
        part_k = dot_nn(grad_score, scaled[begin:end])
        part_q = dot_tn(grad_score, keys[low : low + block])
        for sums, part in ((sums_k, part_k), (sums_v, part_v)):
            old = sums.get((low, head))
            sums[low, head] = part if old is None else old + part
        for at in range(begin, end, block):
            piece = part_q[at - begin : at - begin + block]
            old = grad_q[head][at // block]
            grad_q[head][at // block] = piece if old is None else old + piece

    ahead = scores(units[0])
    for number, unit in enumerate(units):
        found = ahead
        if number + 1 < len(units):
            ahead = scores(units[number + 1])
        gather(unit, *exponents(unit, *found))

    grad_k, grad_v, done_q = [], [], []
    for low in range(0, span, block):
        for sums, out in ((sums_k, grad_k), (sums_v, grad_v)):
            value = jnp.where(masks[0], sums[low, 0], sums[low, 1])
            out.append((low, low + block, value.astype(LOW)))
    for number, (one, two) in enumerate(zip(grad_q[0], grad_q[1])):
        value = (jnp.where(masks[0], one, two) * SCORE_SCALE).astype(LOW)
        done_q.append((number * block, (number + 1) * block, value))
    return done_q, grad_k, grad_v


def self_forward_kernel(qkv_ref, out_ref, level_ref):
    queries = qkv_ref[:, :PAIR]
    keys = qkv_ref[:, PAIR : 2 * PAIR]
    values = qkv_ref[:, 2 * PAIR :]
    for start, stop, out, level in forward_pair(queries, keys, values, True, None):
        out_ref[start:stop, :] = out
        level_ref[0, 0:8, start:stop] = level[0:8]
        level_ref[0, 8:16, start:stop] = level[HD : HD + 8]


def self_backward_kernel(qkv_ref, mixed_ref, upstream_ref, level_ref, *rest):
    grad_ref = rest[-1]
    queries = qkv_ref[:, :PAIR]
    keys = qkv_ref[:, PAIR : 2 * PAIR]
    values = qkv_ref[:, 2 * PAIR :]
    found = backward_pair(
        queries, keys, values, mixed_ref[...], upstream_ref[...], level_ref[0], True, None
    )
    for place, rows in enumerate(found):
        for start, stop, value in rows:
            grad_ref[start:stop, place * PAIR : (place + 1) * PAIR] = value


def cross_forward_kernel(limit_ref, query_ref, kv_ref, out_ref, level_ref):
    found = forward_pair(query_ref[...], kv_ref[:, :PAIR], kv_ref[:, PAIR:], False, limit_ref[0])
    for start, stop, out, level in found:
        out_ref[start:stop, :] = out
        level_ref[0, 0:8, start:stop] = level[0:8]
        level_ref[0, 8:16, start:stop] = level[HD : HD + 8]


def cross_backward_kernel(
    limit_ref, query_ref, kv_ref, mixed_ref, upstream_ref, level_ref, grad_q_ref, grad_kv_ref
):
    found = backward_pair(
        query_ref[...],
        kv_ref[:, :PAIR],
        kv_ref[:, PAIR:],
        mixed_ref[...],
        upstream_ref[...],
        level_ref[0],
        False,
        limit_ref[0],
    )
    for start, stop, value in found[0]:
        grad_q_ref[start:stop, :] = value
    for place, rows in enumerate(found[1:]):
        for start, stop, value in rows:
            grad_kv_ref[start:stop, place * PAIR : (place + 1) * PAIR] = value


LARGE = pltpu.CompilerParams(vmem_limit_bytes=56 * 1024 * 1024)
MIDDLE = pltpu.CompilerParams(vmem_limit_bytes=42 * 1024 * 1024)
PARAMS = pltpu.CompilerParams(vmem_limit_bytes=28 * 1024 * 1024)
SCALAR = pl.BlockSpec(memory_space=pltpu.SMEM)


def columns(rows, width, offset=0):
    return pl.BlockSpec((rows, width), lambda pair: (0, pair + offset))


def planes(seq):
    return pl.BlockSpec((1, 16, seq), lambda pair: (pair, 0, 0))


SHORT = pl.CostEstimate(flops=1, bytes_accessed=1, transcendentals=0)


def self_forward(qkv):
    seq, width = qkv.shape[0], qkv.shape[1] // 3
    pairs = width // PAIR
    return pl.pallas_call(
        self_forward_kernel,
        grid=(pairs,),
        in_specs=[columns(seq, 3 * PAIR)],
        out_specs=[columns(seq, PAIR), planes(seq)],
        out_shape=[
            jax.ShapeDtypeStruct((seq, width), LOW),
            jax.ShapeDtypeStruct((pairs, 16, seq), FULL),
        ],
        compiler_params=LARGE,
        cost_estimate=SHORT,
        name="self_forward",
    )(qkv)


def self_backward(qkv, mixed, upstream, levels, start, count, total=None, at=0, old=None):
    seq = qkv.shape[0]
    total = count if total is None else total
    old = [] if old is None else [old]
    return pl.pallas_call(
        self_backward_kernel,
        grid=(count,),
        in_specs=[
            columns(seq, 3 * PAIR, start),
            columns(seq, PAIR, start),
            columns(seq, PAIR, start),
            pl.BlockSpec((1, 16, seq), lambda pair: (pair + start, 0, 0)),
        ]
        + [pl.BlockSpec(memory_space=pl.ANY)] * len(old),
        out_specs=columns(seq, 3 * PAIR, at),
        out_shape=jax.ShapeDtypeStruct((seq, 3 * PAIR * total), LOW),
        input_output_aliases={4: 0} if old else {},
        compiler_params=PARAMS,
        cost_estimate=SHORT,
        name="self_backward",
    )(qkv, mixed, upstream, levels, *old)


def cross_forward(limit, queries, pair_states):
    seq, width = queries.shape
    span = pair_states.shape[0]
    pairs = width // PAIR
    return pl.pallas_call(
        cross_forward_kernel,
        grid=(pairs,),
        in_specs=[SCALAR, columns(seq, PAIR), columns(span, 2 * PAIR)],
        out_specs=[columns(seq, PAIR), planes(seq)],
        out_shape=[
            jax.ShapeDtypeStruct((seq, width), LOW),
            jax.ShapeDtypeStruct((pairs, 16, seq), FULL),
        ],
        compiler_params=PARAMS,
        cost_estimate=SHORT,
        name="cross_forward",
    )(limit, queries, pair_states)


def cross_backward(limit, queries, pair_states, mixed, upstream, levels):
    seq, width = queries.shape
    span = pair_states.shape[0]
    pairs = width // PAIR
    return pl.pallas_call(
        cross_backward_kernel,
        grid=(pairs,),
        in_specs=[
            SCALAR,
            columns(seq, PAIR),
            columns(span, 2 * PAIR),
            columns(seq, PAIR),
            columns(seq, PAIR),
            planes(seq),
        ],
        out_specs=[columns(seq, PAIR), columns(span, 2 * PAIR)],
        out_shape=[
            jax.ShapeDtypeStruct((seq, width), LOW),
            jax.ShapeDtypeStruct((span, 2 * width), LOW),
        ],
        compiler_params=PARAMS,
        cost_estimate=SHORT,
        name="cross_backward",
    )(limit, queries, pair_states, mixed, upstream, levels)


def mlp_kernel(order, core_ref, rows_ref, grad_ref, up_ref, down_ref, *rest):
    del core_ref
    count = 2 + max(piece for _, _, piece, _ in order) * 2
    halves_refs, rest = rest[-4 - count : -4], rest[-4:]
    out_ref, back_ref, rows_turned_ref, grad_turned_ref = rest
    step = pl.program_id(0)

    @pl.when(step == 0)
    def _():
        rows_turned_ref[...] = rows_ref[...].T
        grad_turned_ref[...] = grad_ref[...].T
        back_ref[...] = jnp.zeros_like(back_ref)

    seq = rows_ref.shape[0]
    size = min(512, seq)
    width = up_ref.shape[1]

    def ahead(start):
        rows = slice(start, start + size)
        return dot_nn(rows_ref[rows, :], up_ref[...]), dot_nn(grad_ref[rows, :], down_ref[...])

    down_grad, up_grad = None, None
    found = ahead(0)
    for start in range(0, seq, size):
        hidden, grad = found
        if start + size < seq:
            found = ahead(start + size)
        rows = slice(start, start + size)
        share = 0.5 + 0.5 * lax.erf(hidden * 0.7071067811865476)
        bell = jnp.exp(hidden * hidden * -0.5)
        active = (hidden * share).astype(LOW)
        grad_hidden = (grad * (share + hidden * (bell * 0.3989422804014327))).astype(LOW)
        out_ref[rows, :] = active
        down_part = dot_nn(grad_turned_ref[:, rows], active)
        up_part = dot_nn(rows_turned_ref[:, rows], grad_hidden)
        back_ref[rows, :] += dot_nt(grad_hidden, up_ref[...])
        down_grad = down_part if start == 0 else down_grad + down_part
        up_grad = up_part if start == 0 else up_grad + up_part

    for number, half_ref in enumerate(halves_refs):
        steps = [
            at for at, (_, side, piece, _) in enumerate(order) if 2 * piece + 1 - side == number
        ]

        @pl.when((step >= steps[0]) & (step <= steps[-1]))
        def _(half_ref=half_ref):
            half_ref[:, :width] = down_grad.astype(LOW)
            half_ref[:, width:] = up_grad.astype(LOW)


def mlp(core, rows, grad, weights, up_at, down_at, order, old=None):
    seq, width = rows.shape
    block = width // 2
    pieces = 1 + max(piece for _, _, piece, _ in order)

    def chosen(j, values):
        found = values[0]
        for number, value in enumerate(values[1:], 1):
            found = jnp.where(j == number, value, found)
        return found

    def place(j, core):
        quarter = chosen(j, [quarter for quarter, _, _, _ in order])
        return 2 * quarter + (core[0] ^ chosen(j, [side for _, side, _, _ in order]))

    def strip(start):
        return pl.BlockSpec((width, block), lambda j, core: (0, start // block + place(j, core)))

    once = pl.Buffered(1)

    def strips(number):
        mine = [at for at, (_, side, piece, _) in enumerate(order) if 2 * piece + 1 - side == number]
        places = [order[min(max(at, mine[0]), mine[-1])][3] for at in range(len(order))]
        return pl.BlockSpec(
            (width, width), lambda j, core: (0, chosen(j, places)), pipeline_mode=once
        )

    old = [] if old is None else list(old)
    whole = pl.BlockSpec((seq, width), lambda j, core: (0, 0), pipeline_mode=once)
    return pl.pallas_call(
        functools.partial(mlp_kernel, order),
        grid_spec=pltpu.PrefetchScalarGridSpec(
            num_scalar_prefetch=1,
            grid=(len(order),),
            in_specs=[whole, whole, strip(up_at), strip(down_at)]
            + [pl.BlockSpec(memory_space=pl.ANY)] * len(old),
            out_specs=[strips(number) for number in range(2 * pieces)]
            + [pl.BlockSpec((seq, block), lambda j, core: (0, place(j, core))), whole],
            scratch_shapes=[pltpu.VMEM((width, seq), LOW)] * 2,
        ),
        out_shape=[jax.ShapeDtypeStruct((width, 2 * width), LOW)] * (2 * pieces)
        + [
            jax.ShapeDtypeStruct((seq, len(order) * block), LOW),
            jax.ShapeDtypeStruct((seq, width), FULL),
        ],
        input_output_aliases={5: 0, 6: 1} if old else {},
        compiler_params=MIDDLE,
        cost_estimate=SHORT,
        name="mlp",
    )(core, rows, grad, weights, weights, *old)


def matmul_kernel(left_ref, right_ref, out_ref):
    out_ref[...] = dot_nn(left_ref[...], right_ref[...]).astype(LOW)


def matmul(left, right, at, count):
    seq, depth = left.shape
    block = min(512, count)
    return pl.pallas_call(
        matmul_kernel,
        grid=(count // block,),
        in_specs=[
            pl.BlockSpec((seq, depth), lambda step: (0, 0)),
            pl.BlockSpec((depth, block), lambda step: (0, at // block + step)),
        ],
        out_specs=pl.BlockSpec((seq, block), lambda step: (0, step)),
        out_shape=jax.ShapeDtypeStruct((seq, count), LOW),
        compiler_params=PARAMS,
        cost_estimate=SHORT,
        name="matmul",
    )(left, right)


def turned_kernel(left_ref, right_ref, out_ref):
    out_ref[...] = dot_nt(left_ref[...], right_ref[...])


def matmul_turned(left, right, at):
    seq, depth = left.shape
    width = right.shape[0]
    block = min(512, width)
    return pl.pallas_call(
        turned_kernel,
        grid=(width // block,),
        in_specs=[
            pl.BlockSpec((seq, depth), lambda step: (0, 0)),
            pl.BlockSpec((block, depth), lambda step: (step, at // depth)),
        ],
        out_specs=pl.BlockSpec((seq, block), lambda step: (0, step)),
        out_shape=jax.ShapeDtypeStruct((seq, width), FULL),
        compiler_params=PARAMS,
        cost_estimate=SHORT,
        name="matmul_turned",
    )(left, right)


def product_kernel(core_ref, left_ref, sent_ref, kept_ref, *rest):
    del core_ref
    send_ref, keep_ref, turned_ref = rest[-3:]

    @pl.when(pl.program_id(0) == 0)
    def _():
        turned_ref[...] = left_ref[...].T

    send_ref[...] = dot_nn(turned_ref[...], sent_ref[...]).astype(LOW)
    keep_ref[...] = dot_nn(turned_ref[...], kept_ref[...]).astype(LOW)


def product(core, left, right, total=None, at=0, old=None):
    rows, width = left.shape
    half = right.shape[1] // 2
    block = max(b for b in (128, 256, 384, 512) if half % b == 0 and at % b == 0)
    steps, offset = half // block, at // block
    total = half if total is None else total
    old = [] if old is None else list(old)
    return pl.pallas_call(
        product_kernel,
        grid_spec=pltpu.PrefetchScalarGridSpec(
            num_scalar_prefetch=1,
            grid=(steps,),
            in_specs=[
                pl.BlockSpec((rows, width), lambda j, core: (0, 0)),
                pl.BlockSpec((rows, block), lambda j, core: (0, (1 - core[0]) * steps + j)),
                pl.BlockSpec((rows, block), lambda j, core: (0, core[0] * steps + j)),
            ]
            + [pl.BlockSpec(memory_space=pl.ANY)] * len(old),
            out_specs=[pl.BlockSpec((width, block), lambda j, core: (0, offset + j))] * 2,
            scratch_shapes=[pltpu.VMEM((width, rows), LOW)],
        ),
        out_shape=[jax.ShapeDtypeStruct((width, total), LOW)] * 2,
        input_output_aliases={4: 0, 5: 1} if old else {},
        compiler_params=PARAMS,
        cost_estimate=SHORT,
        name="product",
    )(core, left, right, right, *old)


def pack_kernel(attn_ref, mlp_ref, norm_ref, out_ref, rest_ref):
    width = attn_ref.shape[2]
    hidden = mlp_ref.shape[2]
    quarter = hidden // 4
    for pair in range(width // PAIR):
        source = slice(pair * PAIR, (pair + 1) * PAIR)
        for kind in range(3):
            place = (3 * pair + kind) * PAIR
            out_ref[:, place : place + PAIR] = attn_ref[kind, :, source].astype(LOW)
        for kind in range(2):
            place = 5 * width + (2 * pair + kind) * PAIR
            out_ref[:, place : place + PAIR] = attn_ref[5 + kind, :, source].astype(LOW)
    out_ref[:, 3 * width : 4 * width] = attn_ref[3].astype(LOW)
    out_ref[:, 4 * width : 5 * width] = attn_ref[4].astype(LOW)
    out_ref[:, 7 * width : 8 * width] = attn_ref[7].astype(LOW)
    for kind in range(2):
        place = 8 * width + kind * quarter
        out_ref[:, place : place + quarter] = mlp_ref[kind, :, :quarter].astype(LOW)
        place = kind * 3 * quarter
        rest_ref[:, place : place + 3 * quarter] = mlp_ref[kind, :, quarter:].astype(LOW)
    out_ref[:, 8 * width + 2 * quarter :] = norm_ref[...].astype(LOW)


def pack(attn_master, mlp_master, norm_columns):
    _, rows, width = attn_master.shape
    hidden = mlp_master.shape[2]
    return pl.pallas_call(
        pack_kernel,
        out_shape=[
            jax.ShapeDtypeStruct((rows, 8 * width + hidden // 2 + norm_columns.shape[1]), LOW),
            jax.ShapeDtypeStruct((rows, 3 * hidden // 2), LOW),
        ],
        compiler_params=PARAMS,
        cost_estimate=SHORT,
        name="pack",
    )(attn_master, mlp_master, norm_columns)


class Grid:
    def __init__(self, sizes):
        self.outer, self.chips = sizes
        self.inner = 2 * self.chips
        self.count = self.outer * self.inner
        self.bits = (self.count - 1).bit_length()
        self.core = lax.axis_index("core")
        self.me = lax.axis_index(AXES)
        self.plane = lax.axis_index("dp")
        near = ((self.chips - 1).bit_length() + 1) // 2
        self.x = list(range(near, 0, -1))
        self.y = list(range((self.chips - 1).bit_length(), near, -1))

    def own(self, bit):
        return lax.shift_right_logical(self.me, jnp.int32(bit)) & 1

    def turn(self, value, mask):
        return lax.ppermute(value, AXES, [(i, i ^ mask) for i in range(self.count)])

    def add_all(self, value):
        for bit in range(self.bits):
            value = value + self.turn(value, 1 << bit)
        return value

    def unpair(self, total):
        total = total.reshape(2, total.shape[0] // 2, total.shape[1])
        mine = lax.dynamic_index_in_dim(total, self.core, 0, keepdims=False)
        other = lax.dynamic_index_in_dim(total, 1 - self.core, 0, keepdims=False)
        return mine, self.turn(other, 1)


def add_kernel(counts, side_ref, *refs):
    del side_ref
    outs = refs[sum(counts) :]
    at = 0
    for count, out_ref in zip(counts, outs):
        total = refs[at][...].reshape(out_ref.shape).astype(FULL)
        for ref in refs[at + 1 : at + count]:
            total = total + ref[...].reshape(out_ref.shape).astype(FULL)
        out_ref[...] = total.astype(LOW)
        at += count


def layer_kernel(outer, steps, first, one, two, side_ref, *refs):
    ins, outs = refs[: first + one + two], refs[first + one + two :]

    def fill(parts):
        for step in range(outer):
            plane = side_ref[0] ^ step
            out_ref = outs[step]
            total = parts[0][plane].reshape(out_ref.shape).astype(FULL)
            for part in parts[1:]:
                total = total + part[plane].reshape(out_ref.shape).astype(FULL)
            out_ref[...] = total.astype(out_ref.dtype)

    @pl.when(pl.program_id(0) < steps)
    def _():
        fill(ins[:first] + ins[first : first + one])

    @pl.when(pl.program_id(0) >= steps)
    def _():
        fill(ins[:first] + ins[first + one :])


def plane_kernel(steps, first, one, two, side_ref, *refs):
    del side_ref
    ins, out_ref = refs[:-1], refs[-1]

    def fill(parts):
        total = parts[0][...].reshape(out_ref.shape).astype(FULL)
        for part in parts[1:]:
            total = total + part[...].reshape(out_ref.shape).astype(FULL)
        out_ref[...] = total.astype(LOW)

    @pl.when(pl.program_id(0) < steps)
    def _():
        fill(ins[:first] + ins[first : first + one])

    @pl.when(pl.program_id(0) >= steps)
    def _():
        fill(ins[:first] + ins[first + one :])


class Sum:
    def __init__(self, grid, keep, got):
        self.grid = grid
        self.bits = sorted(grid.x + grid.y, reverse=True)
        self.cut = keep.shape[1] // 2
        self.block = max(b for b in (128, 256, 384, 512, 640) if self.cut % b == 0)
        self.steps = self.cut // self.block
        self.base = [(keep, []), (got, [])]
        self.orders = [grid.x + grid.y, grid.y + grid.x]
        self.extra = [[], []]
        self.stages = len(self.bits)
        sides = [grid.plane] + [grid.own(bit) for bit in self.bits]
        self.sides = jnp.stack(sides).astype(jnp.int32)

    def view(self, term):
        value, done = term
        left = [bit for bit in self.bits if bit not in done]
        outer = self.grid.outer
        share = value.shape[0] // (outer << len(left))
        return value.reshape([outer] + [2] * len(left) + [share, value.shape[1]]), left

    def spec(self, view, left, flips, column):
        places = {bit: 1 + self.bits.index(bit) for bit in flips}

        def index(j, side):
            picks = [
                (side[places[bit]] ^ flips[bit]) if bit in flips else 0 for bit in left
            ]
            return (0, *picks, 0, column(j))

        shape = [view.shape[0]] + [1 if bit in flips else 2 for bit in left]
        return pl.BlockSpec((*shape, view.shape[-2], self.block), index)

    def call(self, kernel, grid, views, specs, out_specs, out_shape, name):
        return pl.pallas_call(
            kernel,
            grid_spec=pltpu.PrefetchScalarGridSpec(
                num_scalar_prefetch=1, grid=grid, in_specs=specs, out_specs=out_specs
            ),
            out_shape=out_shape,
            compiler_params=PARAMS,
            cost_estimate=SHORT,
            name=name,
        )(self.sides, *views)

    def send(self, stage):
        views, specs, counts = [], [], []
        for half, order in enumerate(self.orders):
            flips = {bit: 0 for bit in order[:stage]}
            flips[order[stage]] = 1
            terms = self.base + self.extra[half]
            counts.append(len(terms))
            for number, term in enumerate(terms):
                view, left = self.view(term)
                shift = half * self.steps if number < len(self.base) else 0
                views.append(view)
                picked = {bit: flip for bit, flip in flips.items() if bit in left}
                specs.append(self.spec(view, left, picked, lambda j, shift=shift: shift + j))
        rows = self.base[0][0].shape[0] >> (stage + 1)
        return self.call(
            functools.partial(add_kernel, counts),
            (self.steps,),
            views,
            specs,
            [pl.BlockSpec((rows, self.block), lambda j, side: (0, j))] * 2,
            [jax.ShapeDtypeStruct((rows, self.cut), LOW)] * 2,
            "add",
        )

    def swap(self, stage, out):
        return [self.grid.turn(v, 1 << order[stage]) for order, v in zip(self.orders, out)]

    def receive(self, stage, got):
        for half, value in enumerate(got):
            self.extra[half].append((value, self.orders[half][: stage + 1]))

    def between(self, main):
        for stage in range(1, self.stages - 1):
            main, sent = tie((main, self.send(stage)))
            main, got = tie((main, self.swap(stage, sent)))
            self.receive(stage, got)
        return main

    def layers(self):
        views, specs, counts = self.columns()
        outer = self.grid.outer
        share = views[0].shape[-2]
        shape = (share, 2 * self.cut)
        return self.call(
            functools.partial(layer_kernel, outer, self.steps, *counts),
            (2 * self.steps,),
            views,
            specs,
            [pl.BlockSpec((share, self.block), lambda j, side: (0, j))] * outer,
            [jax.ShapeDtypeStruct(shape, FULL)] + [jax.ShapeDtypeStruct(shape, LOW)] * (outer - 1),
            "layers",
        )

    def planes(self):
        views, specs, counts = self.columns()
        rows = views[0].shape[0] * views[0].shape[-2]
        value = self.call(
            functools.partial(plane_kernel, self.steps, *counts),
            (2 * self.steps,),
            views,
            specs,
            pl.BlockSpec((rows, self.block), lambda j, side: (0, j)),
            jax.ShapeDtypeStruct((rows, 2 * self.cut), LOW),
            "planes",
        )
        return value

    def columns(self):
        views, specs = [], []
        steps = self.steps
        groups = (
            (self.base, lambda j: j),
            (self.extra[0], lambda j: jnp.minimum(j, steps - 1)),
            (self.extra[1], lambda j: jnp.maximum(j - steps, 0)),
        )
        for terms, column in groups:
            for term in terms:
                view, left = self.view(term)
                views.append(view)
                specs.append(self.spec(view, left, {bit: 0 for bit in left}, column))
        return views, specs, [len(terms) for terms, _ in groups]

    def turn_layers(self, layers, steps=None):
        grid = self.grid
        found = [
            grid.turn(layers[step], step * grid.inner) for step in steps or range(1, grid.outer)
        ]
        return found if steps else [layers[0]] + found

    def finish(self, got):
        return sum((value.astype(FULL) for value in got[1:]), got[0])


def norm_forward(rows, gain, bias):
    centre = jnp.mean(rows, axis=-1, keepdims=True)
    centred = rows - centre
    spread = jnp.mean(centred * centred, axis=-1, keepdims=True)
    scale = lax.rsqrt(spread + EPSILON)
    return (centred * scale * gain + bias).astype(LOW)


def norm_backward_kernel(count, rows_ref, gain_ref, base_ref, *rest):
    grad_refs, out_ref, rest = rest[:count], rest[count], rest[count + 1 :]
    sums_ref = rest[-1]
    rows = rows_ref[...].astype(FULL)
    centred = rows - jnp.mean(rows, axis=1, keepdims=True)
    spread = jnp.mean(centred * centred, axis=1, keepdims=True)
    scale = lax.rsqrt(spread + EPSILON)
    plain = centred * scale
    grad = grad_refs[0][...]
    for ref in grad_refs[1:]:
        grad = grad + ref[...]
    weighted = grad * gain_ref[...]
    mean_one = jnp.mean(weighted, axis=1, keepdims=True)
    mean_two = jnp.mean(weighted * plain, axis=1, keepdims=True)
    total = base_ref[...].astype(FULL) + scale * (weighted - mean_one - plain * mean_two)
    out_ref[...] = total
    if len(rest) > 1:
        rest[0][...] = total.astype(LOW)

    @pl.when(pl.program_id(0) == 0)
    def _():
        sums_ref[...] = jnp.zeros_like(sums_ref)

    sums_ref[0:1, :] += jnp.sum(grad * plain, axis=0, keepdims=True)
    sums_ref[1:2, :] += jnp.sum(grad, axis=0, keepdims=True)


def norm_backward(rows, gain, grads, base, rounded=True):
    seq, width = rows.shape
    block = pl.BlockSpec((min(TILE, seq), width), lambda step: (step, 0))
    more = [jax.ShapeDtypeStruct((seq, width), LOW)] if rounded else []
    out = pl.pallas_call(
        functools.partial(norm_backward_kernel, len(grads)),
        grid=(max(1, seq // TILE),),
        in_specs=[block, pl.BlockSpec((1, width), lambda step: (0, 0)), block]
        + [block] * len(grads),
        out_specs=[block] * (1 + len(more)) + [pl.BlockSpec((8, width), lambda step: (0, 0))],
        out_shape=[jax.ShapeDtypeStruct((seq, width), FULL)]
        + more
        + [jax.ShapeDtypeStruct((8, width), FULL)],
        compiler_params=PARAMS,
        cost_estimate=SHORT,
        name="norm_backward",
    )(rows, gain.reshape(1, width), base, *grads)
    return *out[:-1], out[-1][:2]


def adam_update(master, first, second, gradient, factor, rate, decay):
    gradient = gradient * factor
    first_new = BETA_ONE * first + (1.0 - BETA_ONE) * gradient
    second_new = BETA_TWO * second + (1.0 - BETA_TWO) * gradient * gradient
    first_fix = 1.0 - BETA_ONE**STEP
    second_fix = 1.0 - BETA_TWO**STEP
    update = first_new / first_fix / (jnp.sqrt(second_new / second_fix) + ADAM_EPSILON)
    master_new = master - rate * (update + decay * master)
    return (first_new, second_new, master_new, master_new.astype(LOW))


def adam_places(width, hidden):
    pairs = width // PAIR
    cut, half = pairs // 2, width // 2
    places = []
    for side in range(2):
        block = hidden // 8
        for piece, part in ((0, 0), (0, 1), (1, 0), (1, 1)):
            number = 4 * piece + 2 * part + side
            for kind in range(2):
                start = (2 * part + kind) * block
                places.append((1, 1 - kind, number * block, piece, start, side, block))
        for piece, first, count in ((3, 0, cut), (4, cut, pairs - cut)):
            for pair in range(count // 2):
                column = (first + side * (count // 2) + pair) * PAIR
                for kind in range(3):
                    places.append((0, kind, column, piece, (3 * pair + kind) * PAIR, side, PAIR))
        places.append((0, 3, side * half, 3, 3 * PAIR * cut // 2, side, half))
        places.append((0, 4, side * half, 2, half, side, half))
        for pair in range(pairs // 2):
            column = (side * (pairs // 2) + pair) * PAIR
            for kind in range(2):
                start = width + (2 * pair + kind) * PAIR
                places.append((0, 5 + kind, column, 2, start, side, PAIR))
        places.append((0, 7, side * half, 2, 0, side, half))
    return places


def adam_kernel(places, factor_ref, core_ref, *refs):
    grads, olds, news = refs[:10], refs[10:16], refs[16:]
    factor = factor_ref[0]
    core = core_ref[0]
    for into, matrix, column, piece, start, side, size in places:
        mine, other = (ref[:, start : start + size] for ref in grads[2 * piece : 2 * piece + 2])
        gradient = jnp.where(core == side, mine, other)
        old = [ref[matrix, :, column : column + size] for ref in olds[3 * into : 3 * into + 3]]
        new = adam_update(*old, gradient, factor, MATRIX_RATE, WEIGHT_DECAY)
        for ref, value in zip(news[4 * into : 4 * into + 4], new):
            ref[matrix, :, column : column + size] = value


def adam(factor, core, pieces, attn, mlp):
    width, hidden = attn[0].shape[2], mlp[0].shape[2]
    shapes = []
    for group in (attn, mlp):
        shape = group[0].shape
        shapes += [jax.ShapeDtypeStruct(shape, FULL)] * 3 + [jax.ShapeDtypeStruct(shape, LOW)]
    operands = [value for pair in pieces for value in pair] + list(attn) + list(mlp)
    def whole(value):
        return pl.BlockSpec(value.shape, lambda step: (0,) * len(value.shape))

    out = pl.pallas_call(
        functools.partial(adam_kernel, adam_places(width, hidden)),
        grid=(1,),
        in_specs=[SCALAR, SCALAR] + [whole(value) for value in operands],
        out_specs=[whole(value) for value in shapes],
        out_shape=shapes,
        compiler_params=LARGE,
        cost_estimate=SHORT,
        name="adam",
    )(factor.reshape(1), core, *operands)
    return out[:4], out[4:]


def tie(values):
    return lax.optimization_barrier(values)


def local(
    sizes,
    tokens,
    prompt,
    prompt_len,
    cotangent,
    attn_master,
    attn_first,
    attn_second,
    mlp_master,
    mlp_first,
    mlp_second,
    norm_master,
    norm_first,
    norm_second,
):
    grid = Grid(sizes)
    _, seq, width = tokens.shape
    own_rows = attn_master.shape[1]
    hidden = mlp_master.shape[2]
    norm_columns = jnp.pad(norm_master.T, ((0, 0), (0, PAIR - norm_master.shape[0])))
    shard, rest_shard = pack(attn_master, mlp_master, norm_columns)
    weights = lax.all_gather(shard, AXES, axis=0, tiled=True)
    rest_w = lax.all_gather(rest_shard, AXES, axis=0, tiled=True)
    grad_out = cotangent[0]
    up_at, quarter = 8 * width, hidden // 4
    gains = weights[:, up_at + 2 * quarter :].T[: norm_master.shape[0]].astype(FULL)
    out_w, cq_w, ckv_w, cout_w = (
        weights[:, low * width : high * width] for low, high in ((3, 4), (4, 5), (5, 7), (7, 8))
    )

    inputs = tokens[0].astype(FULL)
    normed_one = norm_forward(inputs, gains[0], gains[1])
    qkv = matmul(normed_one, weights, 0, 3 * width)
    mixed, levels = self_forward(qkv)
    after_self = inputs + dot_nn(mixed, out_w)
    normed_two = norm_forward(after_self, gains[2], gains[3])
    cross_q = dot_nn(normed_two, cq_w).astype(LOW)
    states = prompt[0]
    cross_kv = dot_nn(states, ckv_w).astype(LOW)
    crossed, cross_levels = cross_forward(prompt_len, cross_q, cross_kv)
    after_cross = after_self + dot_nn(crossed, cout_w)
    normed_three = norm_forward(after_cross, gains[4], gains[5])

    core = grid.core.astype(jnp.int32).reshape(1)
    half = width // 2
    pairs = width // PAIR
    def across(value):
        return lax.psum_scatter(value, "dp", scatter_dimension=0, tiled=True)

    *one_halves, active_one, back_one = mlp(
        core,
        normed_three,
        grad_out,
        weights,
        up_at,
        up_at + quarter,
        ((0, 0, 0, 0), (0, 1, 0, 0)),
    )
    normed_three, one_halves, rest_w = tie((normed_three, one_halves, rest_w))
    *halves, active_two, back_two = mlp(
        core,
        normed_three,
        grad_out,
        rest_w,
        0,
        3 * quarter,
        ((0, 0, 0, 1), (0, 1, 0, 1), (1, 0, 1, 0), (2, 0, 1, 1), (1, 1, 1, 0), (2, 1, 1, 1)),
        one_halves,
    )
    one_halves, two_halves = halves[:2], halves[2:]
    grads, one_halves, two_halves = tie(((back_one, back_two), one_halves, two_halves))

    one_got = grid.turn(one_halves[0], 1)
    grad_after_cross, branch, norm_three = norm_backward(after_cross, gains[4], grads, grad_out)
    cross_halves = product(core, crossed, branch, 2 * width, 0)
    grad_crossed = dot_nt(branch, cout_w).astype(LOW)
    grad_crossed, one_got, cross_halves = tie((grad_crossed, one_got, cross_halves))
    one_sum = Sum(grid, one_halves[1], one_got)
    last = one_sum.stages - 1
    sent = one_sum.send(0)
    grad_crossed, sent, two_halves = tie((grad_crossed, sent, two_halves))

    one_got, two_got = one_sum.swap(0, sent), grid.turn(two_halves[0], 1)
    grad_cq, grad_ckv = cross_backward(
        prompt_len, cross_q, cross_kv, crossed, grad_crossed, cross_levels
    )
    cross_halves = product(core, normed_two, grad_cq, 2 * width, half, cross_halves)
    cross_halves = product(core, states, grad_ckv, 2 * width, width, cross_halves)
    grad_cq, cross_halves, two_got = tie((grad_cq, cross_halves, two_got))

    grad_normed = matmul_turned(grad_cq, weights, 4 * width)
    grad_after_self, branch, norm_two = norm_backward(
        after_self, gains[2], [grad_normed], grad_after_cross
    )
    branch, one_got, cross_halves = tie((branch, one_got, cross_halves))
    one_sum.receive(0, one_got)
    branch = one_sum.between(branch)
    two_sum = Sum(grid, two_halves[1], two_got)
    sent, begun = one_sum.send(last), two_sum.send(0)
    branch, sent, begun = tie((branch, sent, begun))

    cross_got = grid.turn(cross_halves[0], 1)
    one_got, two_got = one_sum.swap(last, sent), two_sum.swap(0, begun)
    cut = pairs // 2
    part_width = 3 * PAIR * cut // 2
    front_width = half + part_width
    front_halves = product(core, mixed, branch, front_width, part_width)
    grad_mixed = dot_nt(branch, out_w).astype(LOW)
    grad_front = self_backward(qkv, mixed, grad_mixed, levels, 0, cut)
    front_halves = product(core, normed_one, grad_front, front_width, 0, front_halves)
    grad_mixed, grad_front, one_got, two_got, front_halves, cross_got = tie(
        (grad_mixed, grad_front, one_got, two_got, front_halves, cross_got)
    )
    one_sum.receive(last, one_got)
    two_sum.receive(0, two_got)
    grad_mixed = two_sum.between(grad_mixed)
    cross_sum = Sum(grid, cross_halves[1], cross_got)
    sent, begun, one_total = two_sum.send(last), cross_sum.send(0), one_sum.planes()
    grad_mixed, grad_front, sent, begun, one_total = tie(
        (grad_mixed, grad_front, sent, begun, one_total)
    )

    one_total = across(one_total)
    two_got, cross_got = two_sum.swap(last, sent), cross_sum.swap(0, begun)
    front_got = grid.turn(front_halves[0], 1)
    some = (pairs - cut) // 2
    split = 3 * PAIR * cut
    grad_normed = dot_nt(grad_front, weights[:, :split])
    grad_mixed, grad_normed = tie((grad_mixed, grad_normed))
    grad_back = self_backward(qkv, mixed, grad_mixed, levels, cut, some, pairs - cut)
    grad_mixed, grad_back, two_got, front_got = tie((grad_mixed, grad_back, two_got, front_got))
    two_sum.receive(last, two_got)
    two_total = two_sum.planes()
    grad_mixed, two_total = tie((grad_mixed, two_total))

    grad_back = self_backward(
        qkv, mixed, grad_mixed, levels, cut + some, pairs - cut - some, pairs - cut, some, grad_back
    )
    back_halves = product(core, normed_one, grad_back)
    grad_back, back_halves, cross_got, one_total, two_total = tie(
        (grad_back, back_halves, cross_got, one_total, two_total)
    )
    two_total = across(two_total)
    cross_sum.receive(0, cross_got)
    grad_back = cross_sum.between(grad_back)
    front_sum = Sum(grid, front_halves[1], front_got)
    sent, begun = cross_sum.send(last), front_sum.send(0)
    grad_back, sent, begun = tie((grad_back, sent, begun))

    cross_got, front_got = cross_sum.swap(last, sent), front_sum.swap(0, begun)
    back_got = grid.turn(back_halves[0], 1)
    grad_normed = grad_normed + dot_nt(grad_back, weights[:, split : 3 * width])
    token_grad, norm_one = norm_backward(
        tokens[0], gains[0], [grad_normed], grad_after_self, False
    )
    token_grad = token_grad[None]
    token_grad, cross_got, front_got, back_got, two_total = tie(
        (token_grad, cross_got, front_got, back_got, two_total)
    )
    cross_sum.receive(last, cross_got)
    front_sum.receive(0, front_got)
    token_grad = front_sum.between(token_grad)
    back_sum = Sum(grid, back_halves[1], back_got)
    sent, begun, cross_total = front_sum.send(last), back_sum.send(0), cross_sum.planes()
    grad_ckv, sent, begun, cross_total, active = tie(
        (grad_ckv, sent, begun, cross_total, (active_one, active_two))
    )

    cross_total = across(cross_total)
    front_got, back_got = front_sum.swap(last, sent), back_sum.swap(0, begun)
    prompt_grad = dot_nt(grad_ckv, ckv_w)[None]
    down_at = up_at + quarter
    output = after_cross + dot_nt(active[0], weights[:, down_at : down_at + quarter])
    output = output + dot_nt(active[1][:, :quarter], rest_w[:, 3 * quarter : 4 * quarter])
    prompt_grad, output, front_got, back_got = tie((prompt_grad, output, front_got, back_got))
    front_sum.receive(last, front_got)
    back_sum.receive(0, back_got)
    output = back_sum.between(output)
    layers, sent = front_sum.layers(), back_sum.send(last)
    output, active, layers, sent = tie((output, active, layers, sent))

    front_layers, got = front_sum.turn_layers(layers), back_sum.swap(last, sent)
    output = output + dot_nt(active[1][:, quarter:], rest_w[:, 4 * quarter :])
    output = output.astype(LOW)[None]
    output, got = tie((output, got))
    back_sum.receive(last, got)
    layers = back_sum.layers()
    one_total, two_total, layers = tie((one_total, two_total, layers))

    back_layers = back_sum.turn_layers(layers)
    totals = [total.astype(FULL) for total in (one_total, two_total, cross_total)]
    totals.append(front_sum.finish(front_layers))
    squares = sum(jnp.sum(total * total) for total in totals)
    squares, back_layers = tie((squares, back_layers))
    totals.append(back_sum.finish(back_layers))
    squares = squares + jnp.sum(totals[-1] * totals[-1])

    norm_stack = jnp.concatenate([norm_one, norm_two, norm_three])
    payload = jnp.concatenate([norm_stack, jnp.full((2, width), squares, FULL)])
    payload = grid.add_all(payload)
    norm_grads = payload[:-2]
    grad_norm = jnp.sqrt(payload[-1, 0] + jnp.sum(norm_grads * norm_grads))
    norm_grads = lax.dynamic_slice_in_dim(norm_grads, grid.me * own_rows, own_rows, 1)
    factor = CLIP_NORM / jnp.maximum(grad_norm, CLIP_NORM)
    attn_out, mlp_out = adam(
        factor,
        core,
        [grid.unpair(total) for total in totals],
        (attn_master, attn_first, attn_second),
        (mlp_master, mlp_first, mlp_second),
    )
    norm_out = adam_update(
        norm_master, norm_first, norm_second, norm_grads, factor, VECTOR_RATE, 0.0
    )
    return (output, token_grad, prompt_grad, grad_norm, *attn_out, *mlp_out, *norm_out)


def solution(mesh):
    outer, inner = mesh.shape["dp"], mesh.shape["fsdp"]
    fine = jax.sharding.Mesh(mesh.devices.reshape(outer, inner // 2, 2), AXES)
    items = P(AXES, None, None)
    weights = P(None, AXES, None)
    vectors = P(None, AXES)
    return jax.shard_map(
        functools.partial(local, (outer, inner // 2)),
        mesh=fine,
        in_specs=(items, items, P(AXES), items) + (weights,) * 6 + (vectors,) * 3,
        out_specs=(items,) * 3 + (P(),) + (weights,) * 8 + (vectors,) * 4,
        check_vma=False,
    )
```

time: 1780 us -> 640 us (0.36)
  waiting for transfers between devices: 925 us -> 182 us
  matrix products: 392 us -> 62 us
  Pallas kernels: 0 us -> 232 us
  other arithmetic: 178 us -> 9.95 us
  blocking collectives: 90.4 us -> 0 us
  local copies, waits for them, and re-layouts: 163 us -> 84.3 us
  starting transfers between devices: 0.24 us -> 37.9 us
    unnamed x8 -> x5, waiting for transfers between devices: 490 us -> 0.76 us
    reduce_scatter x1 -> x3, waiting for transfers between devices: 353 us -> 0.02 us  [across(): return lax.psum_scatter(value, 'dp', scatter_dimension=0, tiled=True)]
    dot_general x45 -> x12, matrix products: 392 us -> 62 us  [the longest x8 44.1 us: dot_nt(): lax.dot_general(left, right, (((1,), (1,)), ((), ())), preferred_element_...]
    pallas_call x0 -> x36, Pallas kernels: none -> 232 us  [the longest x2 66.1 us: mlp(): pl.pallas_call(functools.partial(mlp_kernel, order), grid_spec=pltpu.Pref...]
    convert_element_type x11 -> x5, other arithmetic: 70.2 us -> 2.97 us  [the longest x3 2.26 us: norm_forward(): return (centred * scale * gain + bias).astype(LOW)]
    all_gather x3 -> x2, waiting for transfers between devices: 81.9 us -> 146 us  [the longest x1 137 us: local(): weights = lax.all_gather(shard, AXES, axis=0, tiled=True)]
    psum x1 -> x0, blocking collectives: 46.9 us -> none  [local(): grad_norm = jnp.sqrt(lax.psum(local_squares, ('dp', 'fsdp')))]
    reduce_sum x17 -> x8, other arithmetic: 49.8 us -> 5.98 us  [the longest x3 3.2 us: local(): squares = sum((jnp.sum(total * total) for total in totals))]
  transfers between devices with their start and end apart: 6 -> 46, of which waited for: 4 -> 12; matrix products, arithmetic and copies ran while one was open for 18% -> 12% of each run, Pallas kernels for 0% -> 26%
where the time goes in v1:
time: 640 us; the launch traced here: 630 us
  Pallas kernels  232 us (36%)
  waiting for transfers between devices  182 us (28%)
  local copies, waits for them, and re-layouts  84.3 us (13%)
  matrix products  62 us (10%)
  starting transfers between devices  37.9 us (6%)
  between operations  22.1 us (3%)
  other arithmetic  9.95 us (2%)
    all_gather x1, waiting for transfers between devices, local(): weights = lax.all_gather(shard, AXES, axis=0, tiled=True)  137 us
    unnamed x226, local copies, waits for them, and re-layouts  79.2 us
    pallas_call x2, Pallas kernels, mlp(): pl.pallas_call(functools.partial(mlp_kernel, order), grid_spec=pltpu.Pref...  66.1 us
    dot_general x8, matrix products, dot_nt(): lax.dot_general(left, right, (((1,), (1,)), ((), ())), preferred_element_...  44.1 us
    ppermute x41, starting transfers between devices, turn(): return lax.ppermute(value, AXES, [(i, i ^ mask) for i in range(self.count)])  37.7 us
    pallas_call x15, Pallas kernels, call(): pl.pallas_call(kernel, grid_spec=pltpu.PrefetchScalarGridSpec(num_scalar_...  36 us
    ppermute x41, waiting for transfers between devices, turn(): return lax.ppermute(value, AXES, [(i, i ^ mask) for i in range(self.count)])  34.8 us
    pallas_call x3, Pallas kernels, self_backward(): pl.pallas_call(self_backward_kernel, grid=(count,), in_specs=[columns(seq...  33 us
  transfers between devices with their start and end apart: 46, of which 12 were waited for; matrix products, arithmetic and copies ran while one was open for 12% of the time, Pallas kernels for 26%

profile of v1, /device:TPU:0, one launch (start us, length us, event | category | flops | bytes accessed | tf_op | source)
XLA Modules:
  0.0 630.0 jit_solution(14858380745914225790)
XLA Ops:
  13.6 136.8 %all-gather.3.cloned.1.call-done.right_ref.up_ref.down_ref = bf16[1024,10368]{1,0:T(8,128)(2,1)} async-done(((bf16[32,10368]{1,0:T(8,128)(2,1)}), bf16[1024,10368]{1,0:T(8,128)(2,1)}) %all-gather.3.cloned.1.call-update) | async-done | bytes 21233680 | tf_op jit(solution)/shard_map/all_gather | solution.py:936
  153.1 9.2 %matmul.1.qkv_ref = bf16[1024,3072]{1,0:T(8,128)(2,1)S(1)} custom-call(bf16[1024,1024]{1,0:T(8,128)(2,1)S(1)} %fusion.5.left_ref, bf16[1024,10368]{1,0:T(8,128)(2,1)} %all-gather.3.cloned.1.call-done.right_ref.up_ref.down_ref), custom_call_target="tpu_custom_call" | custom-call | flops 1 | bytes 1 | tf_op jit(solution)/shard_map/matmul/pallas_call | solution.py:443
  166.3 17.7 %self_forward.1 = (bf16[1024,1024]{1,0:T(8,128)(2,1)}, f32[8,16,1024]{2,1,0:T(8,128)}) custom-call(bf16[1024,3072]{1,0:T(8,128)(2,1)} %copy-done.4), custom_call_target="tpu_custom_call" | custom-call | flops 1 | bytes 1 | tf_op jit(solution)/shard_map/self_forward/pallas_call | solution.py:251
  184.0 4.6 fusion.59
  199.2 10.2 %cross_forward.1 = (bf16[1024,1024]{1,0:T(8,128)(2,1)S(1)}, f32[8,16,1024]{2,1,0:T(8,128)S(1)}) custom-call(s32[1]{0:T(128)S(6)} %copy.65.limit_ref, bf16[1024,1024]{1,0:T(8,128)(2,1)S(1)} %fusion.34.query_ref, bf16[128,2048]{1,0:T(8,128)(2,1)S(1)} %fusion.20.kv_ref), custom_call_target="tpu_custom_call" | custom-call | flops 1 | bytes 1 | tf_op jit(solution)/shard_map/cross_forward/pallas_call | solution.py:293
  209.5 6.0 fusion.60
  218.6 18.6 %mlp.2 = (bf16[1024,2048]{1,0:T(8,128)(2,1)}, bf16[1024,2048]{1,0:T(8,128)(2,1)}, bf16[1024,1024]{1,0:T(8,128)(2,1)S(1)}, f32[1024,1024]{1,0:T(8,128)}) custom-call(s32[1]{0:T(128)} %bitcast.10.core_ref, bf16[1024,1024]{1,0:T(8,128)(2,1)S(1)} %add_convert_fusion.1.rows_ref, bf16[1024,1024]{1,0:T(8,128)(2,1)S(1)} %bitcast.135, ...), custom_call_target="tpu_custom_call" | custom-call | flops 1 | bytes 1 | tf_op jit(solution)/shard_map/mlp/pallas_call | solution.py:413
  238.6 9.4 %all-gather.5.cloned.1.call-done.up_ref.down_ref = bf16[1024,6144]{1,0:T(8,128)(2,1)} async-done(((bf16[32,6144]{1,0:T(8,128)(2,1)}), bf16[1024,6144]{1,0:T(8,128)(2,1)}) %all-gather.5.cloned.1.call-update) | async-done | bytes 12582928 | tf_op jit(solution)/shard_map/all_gather | solution.py:937
  249.6 47.5 %mlp.3 = (bf16[1024,2048]{1,0:T(8,128)(2,1)}, bf16[1024,2048]{1,0:T(8,128)(2,1)}, bf16[1024,2048]{1,0:T(8,128)(2,1)}, bf16[1024,2048]{1,0:T(8,128)(2,1)}, bf16[1...) custom-call(s32[1]{0:T(128)} %bitcast.10.core_ref, ...), custom_call_target="tpu_custom_call", output_to_operand_aliasing={{0}: (5, {}), {1}: (6, {})} | custom-call | flops 1 | bytes 1 | tf_op jit(solution)/shard_map/mlp/pallas_call | solution.py:413
  324.0 10.0 %cross_backward.1 = (bf16[1024,1024]{1,0:T(8,128)(2,1)S(1)}, bf16[128,2048]{1,0:T(8,128)(2,1)S(1)}) custom-call(s32[1]{0:T(128)S(6)} %copy.65.limit_ref, bf16[1024,1024]{1,0:T(8,128)(2,1)S(1)} %copy-done.50, bf16[128,2048]{1,0:T(8,128)(2,1)S(1)} %fusion.20.kv_ref, bf16[1024,1024]{1,0:T(8,128)(2,1)S(1)} %copy-done.48, ...), custom_call_target="tpu_custom_call" | custom-call | flops 1 | bytes 1 | tf_op jit(solution)/shard_map/cross_backward/pallas_call | solution.py:312
  338.5 5.0 matmul_turned.1.rest_0_
  370.8 16.6 %self_backward.3.sent_ref.kept_ref = bf16[1024,1536]{1,0:T(8,128)(2,1)S(1)} custom-call(bf16[1024,3072]{1,0:T(8,128)(2,1)S(1)} %bitcast.103, bf16[1024,1024]{1,0:T(8,128)(2,1)S(1)} %copy-done.33, bf16[1024,1024]{1,0:T(8,128)(2,1)S(1)} %convolution_convert_fusion.upstream_ref, f32[8,16,1024]{2,1,0:T(8,128)S(1)} %copy-done.51), custom_call_target="tpu_custom_call" | custom-call | flops 1 | bytes 1 | tf_op jit(solution)/shard_map/self_backward/pallas_call | solution.py:270
  387.5 6.8 %product.10 = (bf16[1024,1280]{1,0:T(8,128)(2,1)}, bf16[1024,1280]{1,0:T(8,128)(2,1)S(1)}) custom-call(s32[1]{0:T(128)} %bitcast.10.core_ref, bf16[1024,1024]{1,0:T(8,128)(2,1)S(1)} %copy-done.31, bf16[1024,1536]{1,0:T(8,128)(2,1)S(1)} %self_backward.3.sent_ref.kept_ref, ...), custom_call_target="tpu_custom_call", output_to_operand_aliasing={{0}: (4, {}), {1}: (5, {})} | custom-call | flops 1 | bytes 1 | tf_op jit(solution)/shard_map/product/pallas_call | solution.py:500
  422.1 8.3 %fusion.15 = f32[1024,1024]{1,0:T(8,128)} fusion(bf16[1024,1536]{1,0:T(8,128)(2,1)} %copy-done.38, bf16[1024,10368]{1,0:T(8,128)(2,1)} %all-gather.3.cloned.1.call-done.right_ref.up_ref.down_ref), kind=kOutput, calls=%fused_computation.24 | convolution fusion | flops 3221225472 | bytes 10485760 | tf_op jit(solution)/shard_map/dot_general | solution.py:35
  433.2 8.3 %self_backward.4.rest_0_ = bf16[1024,1536]{1,0:T(8,128)(2,1)S(1)} custom-call(bf16[1024,3072]{1,0:T(8,128)(2,1)S(1)} %copy-done.5, bf16[1024,1024]{1,0:T(8,128)(2,1)S(1)} %copy-done.34, bf16[1024,1024]{1,0:T(8,128)(2,1)S(1)} %copy-done.40, f32[8,16,1024]{2,1,0:T(8,128)S(1)} %copy-done.51), custom_call_target="tpu_custom_call" | custom-call | flops 1 | bytes 1 | tf_op jit(solution)/shard_map/self_backward/pallas_call | solution.py:270
  443.2 12.1 %collective-permute-done.9 = bf16[256,1024]{1,0:T(8,128)(2,1)S(1)} collective-permute-done((bf16[256,1024]{1,0:T(8,128)(2,1)}, bf16[256,1024]{1,0:T(8,128)(2,1)S(1)}, u32[]{:S(2)}, u32[]{:S(2)}) %collective-permute-start.9) | collective-permute-done | bytes 524320 | tf_op jit(solution)/shard_map/ppermute | solution.py:577
  466.0 8.1 %self_backward.5.sent_ref.kept_ref = bf16[1024,1536]{1,0:T(8,128)(2,1)S(1)} custom-call(bf16[1024,3072]{1,0:T(8,128)(2,1)S(1)} %copy-done.6, bf16[1024,1024]{1,0:T(8,128)(2,1)S(1)} %copy-done.35, bf16[1024,1024]{1,0:T(8,128)(2,1)S(1)} %copy-done.41, f32[8,16,1024]{2,1,0:T(8,128)S(1)} %copy-done.51, ...), custom_call_target="tpu_custom_call", output_to_operand_aliasing={{}: (4, {})} | custom-call | flops 1 | bytes 1 | tf_op jit(solution)/shard_map/self_backward/pallas_call | solution.py:270
  474.2 6.0 product.11
  496.3 5.4 fusion.31.rest_0_
  501.7 4.7 norm_backward.5
  509.2 12.5 %collective-permute-done.16 = bf16[512,640]{1,0:T(8,128)(2,1)S(1)} collective-permute-done((bf16[512,640]{1,0:T(8,128)(2,1)S(1)}, bf16[512,640]{1,0:T(8,128)(2,1)S(1)}, u32[]{:S(2)}, u32[]{:S(2)}) %collective-permute-start.16) | collective-permute-done | bytes 655392 | tf_op jit(solution)/shard_map/ppermute | solution.py:577
  548.7 4.8 add_add_fusion
  569.0 8.2 %fusion.23 = bf16[1,1024,1024]{2,1,0:T(8,128)(2,1)} fusion(f32[1024,1024]{1,0:T(8,128)S(1)} %add_add_fusion, bf16[1024,6144]{1,0:T(8,128)(2,1)} %all-gather.5.cloned.1.call-done.up_ref.down_ref, bf16[1024,3072]{1,0:T(8,128)(2,1)S(1)} %bitcast.179), kind=kOutput, calls=%fused_computation.28 | convolution fusion | flops 4297064448 | bytes 14680064 | tf_op jit(solution)/shard_map/dot_general | solution.py:35
  614.2 7.7 %adam.1 = (f32[8,32,1024]{2,1,0:T(8,128)}, f32[8,32,1024]{2,1,0:T(8,128)}, f32[8,32,1024]{2,1,0:T(8,128)}, bf16[8,32,1024]{2,1,0:T(8,128)(2,1)}, f32[2,32,4096]{...) custom-call(f32[1]{0:T(128)} %bitcast.50.factor_ref, ...), custom_call_target="tpu_custom_call" | custom-call | flops 1 | bytes 1 | tf_op jit(solution)/shard_map/adam/pallas_call | solution.py:897
  (393 shorter events, 223.3 us)
Async XLA Ops:
  7.2 143.2 %all-gather.3.cloned.1.call-start = ((), (), s32[]{:S(2)}) async-start(), calls=%async_computation.3 | async-start | bytes 21897216 | tf_op jit(solution)/shard_map/all_gather | solution.py:936
  11.7 236.3 %all-gather.5.cloned.1.call-start = ((), (), s32[]{:S(2)}) async-start(), calls=%async_computation.4 | async-start | bytes 12976128 | tf_op jit(solution)/shard_map/all_gather | solution.py:937
  12.5 470.1 %reduce-scatter.4.cloned.1.call-start = ((), (), s32[]{:S(2)}) async-start(), calls=%async_computation.5 | async-start | bytes 1310720 | tf_op jit(solution)/shard_map/reduce_scatter | solution.py:962
  297.1 20.8 %collective-permute-start = (bf16[1024,2048]{1,0:T(8,128)(2,1)}, bf16[1024,2048]{1,0:T(8,128)(2,1)}, u32[]{:S(2)}, u32[]{:S(2)}) collective-permute-start(bf16[1024,2048]{1,0:T(8,128)(2,1)} %get-tuple-element.222), channel_id=1, source_target_pairs={{0,1},{1,0},{2,3},{3,2},{4,5},{5,4},{6,7},{7,6},{8,9},{9,8},{10,11... | collective-permute-start | bytes 12582920 | tf_op jit(solution)/shard_map/ppermute | solution.py:577
  322.0 30.0 %collective-permute-start.2 = (bf16[512,1024]{1,0:T(8,128)(2,1)}, bf16[512,1024]{1,0:T(8,128)(2,1)S(1)}, u32[]{:S(2)}, u32[]{:S(2)}) collective-permute-start(bf16[512,1024]{1,0:T(8,128)(2,1)} %get-tuple-element.246), channel_id=1, source_target_pairs={{0,2},{1,3},{2,0},{3,1},{4,6},{5,7},{6,4},{7,5},{8,10},{9,11},{10,... | collective-permute-start | bytes 3145736 | tf_op jit(solution)/shard_map/ppermute | solution.py:577
  323.5 28.5 %collective-permute-start.3 = (bf16[512,1024]{1,0:T(8,128)(2,1)}, bf16[512,1024]{1,0:T(8,128)(2,1)S(1)}, u32[]{:S(2)}, u32[]{:S(2)}) collective-permute-start(bf16[512,1024]{1,0:T(8,128)(2,1)} %get-tuple-element.247), channel_id=1, source_target_pairs={{0,4},{1,5},{2,6},{3,7},{4,0},{5,1},{6,2},{7,3},{8,12},{9,13},{10,... | collective-permute-start | bytes 3145736 | tf_op jit(solution)/shard_map/ppermute | solution.py:577
  352.0 45.3 %collective-permute-start.8 = (bf16[1024,2048]{1,0:T(8,128)(2,1)S(1)}, bf16[1024,2048]{1,0:T(8,128)(2,1)S(1)}, u32[]{:S(2)}, u32[]{:S(2)}) collective-permute-start(bf16[1024,2048]{1,0:T(8,128)(2,1)S(1)} %get-tuple-element.269), channel_id=1, source_target_pairs={{0,1},{1,0},{2,3},{3,2},{4,5},{5,4},{6,7},{7,6},{8,9},{9,8},{10,11... | collective-permute-start | bytes 12582920 | tf_op jit(solution)/shard_map/ppermute | solution.py:577
  358.1 37.3 %collective-permute-start.6 = (bf16[512,1024]{1,0:T(8,128)(2,1)}, bf16[512,1024]{1,0:T(8,128)(2,1)S(1)}, u32[]{:S(2)}, u32[]{:S(2)}) collective-permute-start(bf16[512,1024]{1,0:T(8,128)(2,1)} %get-tuple-element.263), channel_id=1, source_target_pairs={{0,2},{1,3},{2,0},{3,1},{4,6},{5,7},{6,4},{7,5},{8,10},{9,11},{10,... | collective-permute-start | bytes 3145736 | tf_op jit(solution)/shard_map/ppermute | solution.py:577
  359.5 36.8 %collective-permute-start.7 = (bf16[512,1024]{1,0:T(8,128)(2,1)S(1)}, bf16[512,1024]{1,0:T(8,128)(2,1)S(1)}, u32[]{:S(2)}, u32[]{:S(2)}) collective-permute-start(bf16[512,1024]{1,0:T(8,128)(2,1)S(1)} %get-tuple-element.264), channel_id=1, source_target_pairs={{0,4},{1,5},{2,6},{3,7},{4,0},{5,1},{6,2},{7,3},{8,12},{9,13},{10,... | collective-permute-start | bytes 3145736 | tf_op jit(solution)/shard_map/ppermute | solution.py:577
  360.1 35.3 %collective-permute-start.4 = (bf16[256,1024]{1,0:T(8,128)(2,1)}, bf16[256,1024]{1,0:T(8,128)(2,1)S(1)}, u32[]{:S(2)}, u32[]{:S(2)}) collective-permute-start(bf16[256,1024]{1,0:T(8,128)(2,1)} %get-tuple-element.261), channel_id=1, source_target_pairs={{0,4},{1,5},{2,6},{3,7},{4,0},{5,1},{6,2},{7,3},{8,12},{9,13},{10,... | collective-permute-start | bytes 1572872 | tf_op jit(solution)/shard_map/ppermute | solution.py:577
  361.6 33.8 %collective-permute-start.5 = (bf16[256,1024]{1,0:T(8,128)(2,1)}, bf16[256,1024]{1,0:T(8,128)(2,1)S(1)}, u32[]{:S(2)}, u32[]{:S(2)}) collective-permute-start(bf16[256,1024]{1,0:T(8,128)(2,1)} %get-tuple-element.262), channel_id=1, source_target_pairs={{0,2},{1,3},{2,0},{3,1},{4,6},{5,7},{6,4},{7,5},{8,10},{9,11},{10,... | collective-permute-start | bytes 1572872 | tf_op jit(solution)/shard_map/ppermute | solution.py:577
  399.4 55.9 %collective-permute-start.11 = (bf16[1024,1280]{1,0:T(8,128)(2,1)}, bf16[1024,1280]{1,0:T(8,128)(2,1)}, u32[]{:S(2)}, u32[]{:S(2)}) collective-permute-start(bf16[1024,1280]{1,0:T(8,128)(2,1)} %get-tuple-element.288), channel_id=1, source_target_pairs={{0,1},{1,0},{2,3},{3,2},{4,5},{5,4},{6,7},{7,6},{8,9},{9,8},{10,11... | collective-permute-start | bytes 7864328 | tf_op jit(solution)/shard_map/ppermute | solution.py:577
  417.9 104.8 %reduce-scatter.6.cloned.1.call-start = ((), (), s32[]{:S(2)}) async-start(), calls=%async_computation.6 | async-start | bytes 1310720 | tf_op jit(solution)/shard_map/reduce_scatter | solution.py:962
  417.9 64.6 %collective-permute-start.12 = (bf16[512,1024]{1,0:T(8,128)(2,1)}, bf16[512,1024]{1,0:T(8,128)(2,1)}, u32[]{:S(2)}, u32[]{:S(2)}) collective-permute-start(bf16[512,1024]{1,0:T(8,128)(2,1)} %copy-done.88), channel_id=1, source_target_pairs={{0,2},{1,3},{2,0},{3,1},{4,6},{5,7},{6,4},{7,5},{8,10},{9,11},{10,... | collective-permute-start | bytes 3145736 | tf_op jit(solution)/shard_map/ppermute | solution.py:577
  418.6 64.0 %collective-permute-start.13 = (bf16[512,1024]{1,0:T(8,128)(2,1)}, bf16[512,1024]{1,0:T(8,128)(2,1)}, u32[]{:S(2)}, u32[]{:S(2)}) collective-permute-start(bf16[512,1024]{1,0:T(8,128)(2,1)} %copy-done.87), channel_id=1, source_target_pairs={{0,4},{1,5},{2,6},{3,7},{4,0},{5,1},{6,2},{7,3},{8,12},{9,13},{10,... | collective-permute-start | bytes 3145736 | tf_op jit(solution)/shard_map/ppermute | solution.py:577
  420.1 35.2 %collective-permute-start.9 = (bf16[256,1024]{1,0:T(8,128)(2,1)}, bf16[256,1024]{1,0:T(8,128)(2,1)S(1)}, u32[]{:S(2)}, u32[]{:S(2)}) collective-permute-start(bf16[256,1024]{1,0:T(8,128)(2,1)} %copy-done.90), channel_id=1, source_target_pairs={{0,4},{1,5},{2,6},{3,7},{4,0},{5,1},{6,2},{7,3},{8,12},{9,13},{10,... | collective-permute-start | bytes 1572872 | tf_op jit(solution)/shard_map/ppermute | solution.py:577
  420.6 34.7 %collective-permute-start.10 = (bf16[256,1024]{1,0:T(8,128)(2,1)}, bf16[256,1024]{1,0:T(8,128)(2,1)S(1)}, u32[]{:S(2)}, u32[]{:S(2)}) collective-permute-start(bf16[256,1024]{1,0:T(8,128)(2,1)} %copy-done.89), channel_id=1, source_target_pairs={{0,2},{1,3},{2,0},{3,1},{4,6},{5,7},{6,4},{7,5},{8,10},{9,11},{10,... | collective-permute-start | bytes 1572872 | tf_op jit(solution)/shard_map/ppermute | solution.py:577
  482.6 104.0 %reduce-scatter.8.cloned.1.call-start = ((), (), s32[]{:S(2)}) async-start(), calls=%async_computation.7 | async-start | bytes 1310720 | tf_op jit(solution)/shard_map/reduce_scatter | solution.py:962
  482.6 40.0 %collective-permute-start.18 = (bf16[1024,768]{1,0:T(8,128)(2,1)}, bf16[1024,768]{1,0:T(8,128)(2,1)}, u32[]{:S(2)}, u32[]{:S(2)}) collective-permute-start(bf16[1024,768]{1,0:T(8,128)(2,1)} %copy-done.86), channel_id=1, source_target_pairs={{0,1},{1,0},{2,3},{3,2},{4,5},{5,4},{6,7},{7,6},{8,9},{9,8},{10,11... | collective-permute-start | bytes 4718600 | tf_op jit(solution)/shard_map/ppermute | solution.py:577
  494.2 27.6 %collective-permute-start.16 = (bf16[512,640]{1,0:T(8,128)(2,1)S(1)}, bf16[512,640]{1,0:T(8,128)(2,1)S(1)}, u32[]{:S(2)}, u32[]{:S(2)}) collective-permute-start(bf16[512,640]{1,0:T(8,128)(2,1)S(1)} %get-tuple-element.314), channel_id=1, source_target_pairs={{0,2},{1,3},{2,0},{3,1},{4,6},{5,7},{6,4},{7,5},{8,10},{9,11},{10,... | collective-permute-start | bytes 1966088 | tf_op jit(solution)/shard_map/ppermute | solution.py:577
  495.7 26.1 %collective-permute-start.17 = (bf16[512,640]{1,0:T(8,128)(2,1)S(1)}, bf16[512,640]{1,0:T(8,128)(2,1)S(1)}, u32[]{:S(2)}, u32[]{:S(2)}) collective-permute-start(bf16[512,640]{1,0:T(8,128)(2,1)S(1)} %get-tuple-element.315), channel_id=1, source_target_pairs={{0,4},{1,5},{2,6},{3,7},{4,0},{5,1},{6,2},{7,3},{8,12},{9,13},{10,... | collective-permute-start | bytes 1966088 | tf_op jit(solution)/shard_map/ppermute | solution.py:577
  539.9 18.2 %collective-permute-start.19 = (bf16[256,640]{1,0:T(8,128)(2,1)}, bf16[256,640]{1,0:T(8,128)(2,1)S(1)}, u32[]{:S(2)}, u32[]{:S(2)}) collective-permute-start(bf16[256,640]{1,0:T(8,128)(2,1)} %copy-done.94), channel_id=1, source_target_pairs={{0,4},{1,5},{2,6},{3,7},{4,0},{5,1},{6,2},{7,3},{8,12},{9,13},{10,... | collective-permute-start | bytes 983048 | tf_op jit(solution)/shard_map/ppermute | solution.py:577
  592.8 20.5 %collective-permute-start.39 = (f32[32,1280]{1,0:T(8,128)S(1)}, f32[32,1280]{1,0:T(8,128)S(1)}, u32[]{:S(2)}, u32[]{:S(2)}) collective-permute-start(f32[32,1280]{1,0:T(8,128)S(1)} %get-tuple-element.404), channel_id=1, source_target_pairs={{0,1},{1,0},{2,3},{3,2},{4,5},{5,4},{6,7},{7,6},{8,9},{9,8},{10,11... | collective-permute-start | bytes 491528 | tf_op jit(solution)/shard_map/ppermute | solution.py:577
  595.5 17.8 %collective-permute-start.37 = (f32[32,2048]{1,0:T(8,128)S(1)}, f32[32,2048]{1,0:T(8,128)S(1)}, u32[]{:S(2)}, u32[]{:S(2)}) collective-permute-start(f32[32,2048]{1,0:T(8,128)S(1)} %get-tuple-element.400), channel_id=1, source_target_pairs={{0,1},{1,0},{2,3},{3,2},{4,5},{5,4},{6,7},{7,6},{8,9},{9,8},{10,11... | collective-permute-start | bytes 786440 | tf_op jit(solution)/shard_map/ppermute | solution.py:577
  (134 other events, 856.7 us)
Sparse Core Ops, SparseCore 0:
  11.8 138.5 all-gather.2
  153.8 94.1 all-gather.4
  418.0 25.5 reduce-scatter.3
  482.7 25.4 reduce-scatter.5
  540.0 25.3 reduce-scatter.7

commit v2 on v1

--- a/solution.py
+++ b/solution.py
@@ -234,6 +234,10 @@
 SCALAR = pl.BlockSpec(memory_space=pltpu.SMEM)
 
 
+def streamed(value):
+    return pltpu.with_memory_space_constraint(value, pltpu.HBM)
+
+
 def columns(rows, width, offset=0):
     return pl.BlockSpec((rows, width), lambda pair: (0, pair + offset))
 
@@ -260,7 +264,7 @@
         compiler_params=LARGE,
         cost_estimate=SHORT,
         name="self_forward",
-    )(qkv)
+    )(streamed(qkv))
 
 
 def self_backward(qkv, mixed, upstream, levels, start, count, total=None, at=0, old=None):
@@ -283,7 +287,7 @@
         compiler_params=PARAMS,
         cost_estimate=SHORT,
         name="self_backward",
-    )(qkv, mixed, upstream, levels, *old)
+    )(streamed(qkv), streamed(mixed), upstream, levels, *old)
 
 
 def cross_forward(limit, queries, pair_states):
@@ -516,7 +520,7 @@
         compiler_params=PARAMS,
         cost_estimate=SHORT,
         name="product",
-    )(core, left, right, right, *old)
+    )(core, streamed(left), right, right, *old)
 
 
 def pack_kernel(attn_ref, mlp_ref, norm_ref, out_ref, rest_ref):
@@ -683,7 +687,7 @@
             compiler_params=PARAMS,
             cost_estimate=SHORT,
             name=name,
-        )(self.sides, *views)
+        )(self.sides, *(streamed(view) for view in views))
 
     def send(self, stage):
         views, specs, counts = [], [], []
@@ -829,7 +833,7 @@
         compiler_params=PARAMS,
         cost_estimate=SHORT,
         name="norm_backward",
-    )(rows, gain.reshape(1, width), base, *grads)
+    )(streamed(rows), gain.reshape(1, width), streamed(base), *grads)
     return *out[:-1], out[-1][:2]
 
 
@@ -1035,18 +1039,19 @@
     )
 
     one_total = across(one_total)
-    two_got, cross_got = two_sum.swap(last, sent), cross_sum.swap(0, begun)
-    front_got = grid.turn(front_halves[0], 1)
-    some = (pairs - cut) // 2
+    two_got, front_got = two_sum.swap(last, sent), grid.turn(front_halves[0], 1)
     split = 3 * PAIR * cut
     grad_normed = dot_nt(grad_front, weights[:, :split])
-    grad_mixed, grad_normed = tie((grad_mixed, grad_normed))
-    grad_back = self_backward(qkv, mixed, grad_mixed, levels, cut, some, pairs - cut)
-    grad_mixed, grad_back, two_got, front_got = tie((grad_mixed, grad_back, two_got, front_got))
+    grad_mixed, grad_normed, two_got, front_got, begun = tie(
+        (grad_mixed, grad_normed, two_got, front_got, begun)
+    )
+
+    cross_got = cross_sum.swap(0, begun)
     two_sum.receive(last, two_got)
     two_total = two_sum.planes()
-    grad_mixed, two_total = tie((grad_mixed, two_total))
-
+    some = (pairs - cut) // 2
+    grad_back = self_backward(qkv, mixed, grad_mixed, levels, cut, some, pairs - cut)
+    grad_mixed, grad_back, two_total = tie((grad_mixed, grad_back, two_total))
     grad_back = self_backward(
         qkv, mixed, grad_mixed, levels, cut + some, pairs - cut - some, pairs - cut, some, grad_back
     )
@@ -1068,33 +1073,33 @@
         tokens[0], gains[0], [grad_normed], grad_after_self, False
     )
     token_grad = token_grad[None]
-    token_grad, cross_got, front_got, back_got, two_total = tie(
-        (token_grad, cross_got, front_got, back_got, two_total)
+    prompt_grad = dot_nt(grad_ckv, ckv_w)[None]
+    down_at = up_at + quarter
+    output = after_cross + dot_nt(active_one, weights[:, down_at : down_at + quarter])
+    token_grad, prompt_grad, output, cross_got, front_got, back_got, two_total = tie(
+        (token_grad, prompt_grad, output, cross_got, front_got, back_got, two_total)
     )
     cross_sum.receive(last, cross_got)
     front_sum.receive(0, front_got)
     token_grad = front_sum.between(token_grad)
     back_sum = Sum(grid, back_halves[1], back_got)
     sent, begun, cross_total = front_sum.send(last), back_sum.send(0), cross_sum.planes()
-    grad_ckv, sent, begun, cross_total, active = tie(
-        (grad_ckv, sent, begun, cross_total, (active_one, active_two))
+    output, sent, begun, cross_total, active_two = tie(
+        (output, sent, begun, cross_total, active_two)
     )
 
     cross_total = across(cross_total)
     front_got, back_got = front_sum.swap(last, sent), back_sum.swap(0, begun)
-    prompt_grad = dot_nt(grad_ckv, ckv_w)[None]
-    down_at = up_at + quarter
-    output = after_cross + dot_nt(active[0], weights[:, down_at : down_at + quarter])
-    output = output + dot_nt(active[1][:, :quarter], rest_w[:, 3 * quarter : 4 * quarter])
-    prompt_grad, output, front_got, back_got = tie((prompt_grad, output, front_got, back_got))
+    output = output + dot_nt(active_two[:, : 2 * quarter], rest_w[:, 3 * quarter : 5 * quarter])
+    output, front_got, back_got = tie((output, front_got, back_got))
     front_sum.receive(last, front_got)
     back_sum.receive(0, back_got)
     output = back_sum.between(output)
     layers, sent = front_sum.layers(), back_sum.send(last)
-    output, active, layers, sent = tie((output, active, layers, sent))
+    output, active_two, layers, sent = tie((output, active_two, layers, sent))
 
     front_layers, got = front_sum.turn_layers(layers), back_sum.swap(last, sent)
-    output = output + dot_nt(active[1][:, quarter:], rest_w[:, 4 * quarter :])
+    output = output + dot_nt(active_two[:, 2 * quarter :], rest_w[:, 5 * quarter :])
     output = output.astype(LOW)[None]
     output, got = tie((output, got))
     back_sum.receive(last, got)

time: 640 us -> 628 us (0.981)
  local copies, waits for them, and re-layouts: 84.3 us -> 41.6 us
  Pallas kernels: 232 us -> 260 us
    unnamed x226 -> x152, local copies, waits for them, and re-layouts: 79.2 us -> 36.4 us
    pallas_call x15, Pallas kernels: 36 us -> 46.8 us  [call(): pl.pallas_call(kernel, grid_spec=pltpu.PrefetchScalarGridSpec(num_scalar_...]
    pallas_call x6, Pallas kernels: 24 us -> 33.4 us  [product(): pl.pallas_call(product_kernel, grid_spec=pltpu.PrefetchScalarGridSpec(num...]
  transfers between devices with their start and end apart: 46 -> 46, of which waited for: 12 -> 12; matrix products, arithmetic and copies ran while one was open for 12% -> 13% of each run, Pallas kernels for 26% -> 31%
where the time goes in v2:
time: 628 us; the launch traced here: 618 us
  Pallas kernels  260 us (41%)
  waiting for transfers between devices  181 us (29%)
  matrix products  65.3 us (10%)
  local copies, waits for them, and re-layouts  41.6 us (7%)
  starting transfers between devices  36.8 us (6%)
  between operations  21.9 us (3%)
  other arithmetic  10.9 us (2%)
    all_gather x1, waiting for transfers between devices, local(): weights = lax.all_gather(shard, AXES, axis=0, tiled=True)  137 us
    pallas_call x2, Pallas kernels, mlp(): pl.pallas_call(functools.partial(mlp_kernel, order), grid_spec=pltpu.Pref...  65.8 us
    dot_general x8, matrix products, dot_nt(): lax.dot_general(left, right, (((1,), (1,)), ((), ())), preferred_element_...  47.4 us
    pallas_call x15, Pallas kernels, call(): pl.pallas_call(kernel, grid_spec=pltpu.PrefetchScalarGridSpec(num_scalar_...  46.8 us
    unnamed x152, local copies, waits for them, and re-layouts  36.4 us
    ppermute x41, starting transfers between devices, turn(): return lax.ppermute(value, AXES, [(i, i ^ mask) for i in range(self.count)])  36.4 us
    pallas_call x3, Pallas kernels, self_backward(): pl.pallas_call(self_backward_kernel, grid=(count,), in_specs=[columns(seq...  34.9 us
    ppermute x41, waiting for transfers between devices, turn(): return lax.ppermute(value, AXES, [(i, i ^ mask) for i in range(self.count)])  34.4 us
  transfers between devices with their start and end apart: 46, of which 12 were waited for; matrix products, arithmetic and copies ran while one was open for 13% of the time, Pallas kernels for 31%

profile of v2, /device:TPU:0, one launch (start us, length us, event | category | flops | bytes accessed | tf_op | source)
XLA Modules:
  0.0 617.8 jit_solution(4086521290549205150)
XLA Ops:
  13.5 136.8 %all-gather.3.cloned.1.call-done.right_ref.up_ref.down_ref = bf16[1024,10368]{1,0:T(8,128)(2,1)} async-done(((bf16[32,10368]{1,0:T(8,128)(2,1)}), bf16[1024,10368]{1,0:T(8,128)(2,1)}) %all-gather.3.cloned.1.call-update) | async-done | bytes 21233680 | tf_op jit(solution)/shard_map/all_gather | solution.py:940
  152.9 9.2 %matmul.1.qkv_ref = bf16[1024,3072]{1,0:T(8,128)(2,1)S(1)} custom-call(bf16[1024,1024]{1,0:T(8,128)(2,1)S(1)} %fusion.5.left_ref, bf16[1024,10368]{1,0:T(8,128)(2,1)} %all-gather.3.cloned.1.call-done.right_ref.up_ref.down_ref), custom_call_target="tpu_custom_call" | custom-call | flops 1 | bytes 1 | tf_op jit(solution)/shard_map/matmul/pallas_call | solution.py:447
  166.3 17.7 %self_forward.1 = (bf16[1024,1024]{1,0:T(8,128)(2,1)}, f32[8,16,1024]{2,1,0:T(8,128)}) custom-call(bf16[1024,3072]{1,0:T(8,128)(2,1)} %copy-done.1), custom_call_target="tpu_custom_call" | custom-call | flops 1 | bytes 1 | tf_op jit(solution)/shard_map/self_forward/pallas_call | solution.py:255
  199.1 10.3 %cross_forward.1 = (bf16[1024,1024]{1,0:T(8,128)(2,1)S(1)}, f32[8,16,1024]{2,1,0:T(8,128)S(1)}) custom-call(s32[1]{0:T(128)S(6)} %copy.65.limit_ref, bf16[1024,1024]{1,0:T(8,128)(2,1)S(1)} %fusion.39.query_ref, bf16[128,2048]{1,0:T(8,128)(2,1)S(1)} %fusion.20.kv_ref), custom_call_target="tpu_custom_call" | custom-call | flops 1 | bytes 1 | tf_op jit(solution)/shard_map/cross_forward/pallas_call | solution.py:297
  209.4 6.0 fusion.61
  218.6 18.4 %mlp.2 = (bf16[1024,2048]{1,0:T(8,128)(2,1)}, bf16[1024,2048]{1,0:T(8,128)(2,1)}, bf16[1024,1024]{1,0:T(8,128)(2,1)S(1)}, f32[1024,1024]{1,0:T(8,128)}) custom-call(s32[1]{0:T(128)} %bitcast.10.core_ref, bf16[1024,1024]{1,0:T(8,128)(2,1)S(1)} %add_convert_fusion.1.rows_ref, bf16[1024,1024]{1,0:T(8,128)(2,1)S(1)} %bitcast.113, ...), custom_call_target="tpu_custom_call" | custom-call | flops 1 | bytes 1 | tf_op jit(solution)/shard_map/mlp/pallas_call | solution.py:417
  238.3 9.5 %all-gather.5.cloned.1.call-done.up_ref.down_ref = bf16[1024,6144]{1,0:T(8,128)(2,1)} async-done(((bf16[32,6144]{1,0:T(8,128)(2,1)}), bf16[1024,6144]{1,0:T(8,128)(2,1)}) %all-gather.5.cloned.1.call-update) | async-done | bytes 12582928 | tf_op jit(solution)/shard_map/all_gather | solution.py:941
  249.4 47.3 %mlp.3 = (bf16[1024,2048]{1,0:T(8,128)(2,1)}, bf16[1024,2048]{1,0:T(8,128)(2,1)}, bf16[1024,2048]{1,0:T(8,128)(2,1)}, bf16[1024,2048]{1,0:T(8,128)(2,1)}, bf16[1...) custom-call(s32[1]{0:T(128)} %bitcast.10.core_ref, ...), custom_call_target="tpu_custom_call", output_to_operand_aliasing={{0}: (5, {}), {1}: (6, {})} | custom-call | flops 1 | bytes 1 | tf_op jit(solution)/shard_map/mlp/pallas_call | solution.py:417
  301.5 5.6 norm_backward.3
  323.0 10.0 %cross_backward.1 = (bf16[1024,1024]{1,0:T(8,128)(2,1)S(1)}, bf16[128,2048]{1,0:T(8,128)(2,1)S(1)}) custom-call(s32[1]{0:T(128)S(6)} %copy.65.limit_ref, bf16[1024,1024]{1,0:T(8,128)(2,1)S(1)} %copy-done.15, bf16[128,2048]{1,0:T(8,128)(2,1)S(1)} %fusion.20.kv_ref, bf16[1024,1024]{1,0:T(8,128)(2,1)S(1)} %copy-done.13, ...), custom_call_target="tpu_custom_call" | custom-call | flops 1 | bytes 1 | tf_op jit(solution)/shard_map/cross_backward/pallas_call | solution.py:316
  345.0 6.0 norm_backward.4
  362.4 5.9 product.9
  372.3 17.3 %self_backward.3.sent_ref.kept_ref = bf16[1024,1536]{1,0:T(8,128)(2,1)S(1)} custom-call(bf16[1024,3072]{1,0:T(8,128)(2,1)} %copy-done.1, bf16[1024,1024]{1,0:T(8,128)(2,1)} %get-tuple-element.205.mixed_ref.left_ref, bf16[1024,1024]{1,0:T(8,128)(2,1)S(1)} %convolution_convert_fusion.upstream_ref, f32[8,16,1024]{2,1,0:T(8,128)S(1)} %copy-done.16), custom_call_target="tpu_custom_call" | custom-call | flops 1 | bytes 1 | tf_op jit(solution)/shard_map/self_backward/pallas_call | solution.py:274
  389.6 9.1 %product.10 = (bf16[1024,1280]{1,0:T(8,128)(2,1)}, bf16[1024,1280]{1,0:T(8,128)(2,1)S(1)}) custom-call(s32[1]{0:T(128)} %bitcast.10.core_ref, bf16[1024,1024]{1,0:T(8,128)(2,1)} %copy-done.4, bf16[1024,1536]{1,0:T(8,128)(2,1)S(1)} %self_backward.3.sent_ref.kept_ref, ...), custom_call_target="tpu_custom_call", output_to_operand_aliasing={{0}: (4, {}), {1}: (5, {})} | custom-call | flops 1 | bytes 1 | tf_op jit(solution)/shard_map/product/pallas_call | solution.py:504
  417.3 7.0 %fusion.15 = f32[1024,1024]{1,0:T(8,128)} fusion(bf16[1024,1536]{1,0:T(8,128)(2,1)S(1)} %copy-done.6, bf16[1024,10368]{1,0:T(8,128)(2,1)} %all-gather.3.cloned.1.call-done.right_ref.up_ref.down_ref), kind=kOutput, calls=%fused_computation.23 | convolution fusion | flops 3221225472 | bytes 10485760 | tf_op jit(solution)/shard_map/dot_general | solution.py:35
  431.1 8.8 %self_backward.4.rest_0_ = bf16[1024,1536]{1,0:T(8,128)(2,1)S(1)} custom-call(bf16[1024,3072]{1,0:T(8,128)(2,1)} %copy-done.1, bf16[1024,1024]{1,0:T(8,128)(2,1)} %get-tuple-element.205.mixed_ref.left_ref, bf16[1024,1024]{1,0:T(8,128)(2,1)S(1)} %copy-done.8, f32[8,16,1024]{2,1,0:T(8,128)S(1)} %copy-done.17), custom_call_target="tpu_custom_call" | custom-call | flops 1 | bytes 1 | tf_op jit(solution)/shard_map/self_backward/pallas_call | solution.py:274
  447.5 8.8 %self_backward.5.sent_ref.kept_ref = bf16[1024,1536]{1,0:T(8,128)(2,1)S(1)} custom-call(bf16[1024,3072]{1,0:T(8,128)(2,1)} %copy-done.1, bf16[1024,1024]{1,0:T(8,128)(2,1)} %get-tuple-element.205.mixed_ref.left_ref, bf16[1024,1024]{1,0:T(8,128)(2,1)S(1)} %copy-done.9, f32[8,16,1024]{2,1,0:T(8,128)S(1)} %copy-done.18, ...), custom_call_target="tpu_custom_call", output_to_operand_aliasing={{}: (4, {})} | custom-call | flops 1 | bytes 1 | tf_op jit(solution)/shard_map/self_backward/pallas_call | solution.py:274
  456.3 7.4 %product.11 = (bf16[1024,768]{1,0:T(8,128)(2,1)S(1)}, bf16[1024,768]{1,0:T(8,128)(2,1)S(1)}) custom-call(s32[1]{0:T(128)} %bitcast.10.core_ref, bf16[1024,1024]{1,0:T(8,128)(2,1)} %copy-done.4, bf16[1024,1536]{1,0:T(8,128)(2,1)S(1)} %self_backward.5.sent_ref.kept_ref, bf16[1024,1536]{1,0:T(8,128)(2,1)S(1)} %self_backward.5.sent_ref.kept_ref), custom_call_target="tpu_custom_call" | custom-call | flops 1 | bytes 1 | tf_op jit(solution)/shard_map/product/pallas_call | solution.py:504
  466.5 8.0 %fusion.31 = f32[1024,1024]{1,0:T(8,128)} fusion(f32[1024,1024]{1,0:T(8,128)} %copy-done.38, bf16[1024,1024]{1,0:T(8,128)(2,1)} %copy-done.31, bf16[1024,10368]{1,0:T(8,128)(2,1)} %all-gather.3.cloned.1.call-done.right_ref.up_ref.down_ref), kind=kOutput, calls=%fused_computation.35 | convolution fusion | flops 2148532224 | bytes 12582912 | tf_op jit(solution)/shard_map/dot_general | solution.py:35
  488.5 5.3 fusion.13
  494.8 6.6 %norm_backward.5 = (f32[1024,1024]{1,0:T(8,128)}, f32[8,1024]{1,0:T(8,128)S(1)}) custom-call(bf16[1024,1024]{1,0:T(8,128)(2,1)} %bitcast.138, f32[1,1024]{1,0:T(1,128)S(1)} %copy-done.30, f32[1024,1024]{1,0:T(8,128)} %copy-done.19, f32[1024,1024]{1,0:T(8,128)S(1)} %add.196.rest_0_), custom_call_target="tpu_custom_call" | custom-call | flops 1 | bytes 1 | tf_op jit(solution)/shard_map/norm_backward/pallas_call | solution.py:824
  501.5 11.5 %collective-permute-done.16 = bf16[512,640]{1,0:T(8,128)(2,1)S(1)} collective-permute-done((bf16[512,640]{1,0:T(8,128)(2,1)S(1)}, bf16[512,640]{1,0:T(8,128)(2,1)S(1)}, u32[]{:S(2)}, u32[]{:S(2)}) %collective-permute-start.16) | collective-permute-done | bytes 655392 | tf_op jit(solution)/shard_map/ppermute | solution.py:581
  528.1 9.2 %fusion.34 = f32[1024,1024]{1,0:T(8,128)S(1)} fusion(f32[1024,1024]{1,0:T(8,128)} %fusion.31, bf16[1024,6144]{1,0:T(8,128)(2,1)} %all-gather.5.cloned.1.call-done.up_ref.down_ref, bf16[1024,3072]{1,0:T(8,128)(2,1)} %get-tuple-element.351), kind=kOutput, calls=%fused_computation.36 | convolution fusion | flops 4296015872 | bytes 16777216 | tf_op jit(solution)/shard_map/dot_general | solution.py:35
  602.0 7.7 %adam.1 = (f32[8,32,1024]{2,1,0:T(8,128)}, f32[8,32,1024]{2,1,0:T(8,128)}, f32[8,32,1024]{2,1,0:T(8,128)}, bf16[8,32,1024]{2,1,0:T(8,128)(2,1)}, f32[2,32,4096]{...) custom-call(f32[1]{0:T(128)} %bitcast.50.factor_ref, ...), custom_call_target="tpu_custom_call" | custom-call | flops 1 | bytes 1 | tf_op jit(solution)/shard_map/adam/pallas_call | solution.py:901
  (319 shorter events, 206.3 us)
Async XLA Ops:
  7.2 143.1 %all-gather.3.cloned.1.call-start = ((), (), s32[]{:S(2)}) async-start(), calls=%async_computation.3 | async-start | bytes 21897216 | tf_op jit(solution)/shard_map/all_gather | solution.py:940
  11.6 236.2 %all-gather.5.cloned.1.call-start = ((), (), s32[]{:S(2)}) async-start(), calls=%async_computation.4 | async-start | bytes 12976128 | tf_op jit(solution)/shard_map/all_gather | solution.py:941
  12.3 453.8 %reduce-scatter.4.cloned.1.call-start = ((), (), s32[]{:S(2)}) async-start(), calls=%async_computation.5 | async-start | bytes 1310720 | tf_op jit(solution)/shard_map/reduce_scatter | solution.py:966
  296.7 20.2 %collective-permute-start = (bf16[1024,2048]{1,0:T(8,128)(2,1)}, bf16[1024,2048]{1,0:T(8,128)(2,1)}, u32[]{:S(2)}, u32[]{:S(2)}) collective-permute-start(bf16[1024,2048]{1,0:T(8,128)(2,1)} %get-tuple-element.224), channel_id=1, source_target_pairs={{0,1},{1,0},{2,3},{3,2},{4,5},{5,4},{6,7},{7,6},{8,9},{9,8},{10,11... | collective-permute-start | bytes 12582920 | tf_op jit(solution)/shard_map/ppermute | solution.py:581
  320.6 19.5 %collective-permute-start.1 = (bf16[1024,2048]{1,0:T(8,128)(2,1)S(1)}, bf16[1024,2048]{1,0:T(8,128)(2,1)S(1)}, u32[]{:S(2)}, u32[]{:S(2)}) collective-permute-start(bf16[1024,2048]{1,0:T(8,128)(2,1)S(1)} %copy-done.72), channel_id=1, source_target_pairs={{0,1},{1,0},{2,3},{3,2},{4,5},{5,4},{6,7},{7,6},{8,9},{9,8},{10,11... | collective-permute-start | bytes 12582920 | tf_op jit(solution)/shard_map/ppermute | solution.py:581
  320.9 30.1 %collective-permute-start.2 = (bf16[512,1024]{1,0:T(8,128)(2,1)S(1)}, bf16[512,1024]{1,0:T(8,128)(2,1)S(1)}, u32[]{:S(2)}, u32[]{:S(2)}) collective-permute-start(bf16[512,1024]{1,0:T(8,128)(2,1)S(1)} %get-tuple-element.248), channel_id=1, source_target_pairs={{0,2},{1,3},{2,0},{3,1},{4,6},{5,7},{6,4},{7,5},{8,10},{9,11},{10,... | collective-permute-start | bytes 3145736 | tf_op jit(solution)/shard_map/ppermute | solution.py:581
  322.4 28.7 %collective-permute-start.3 = (bf16[512,1024]{1,0:T(8,128)(2,1)S(1)}, bf16[512,1024]{1,0:T(8,128)(2,1)S(1)}, u32[]{:S(2)}, u32[]{:S(2)}) collective-permute-start(bf16[512,1024]{1,0:T(8,128)(2,1)S(1)} %get-tuple-element.249), channel_id=1, source_target_pairs={{0,4},{1,5},{2,6},{3,7},{4,0},{5,1},{6,2},{7,3},{8,12},{9,13},{10,... | collective-permute-start | bytes 3145736 | tf_op jit(solution)/shard_map/ppermute | solution.py:581
  351.0 47.8 %collective-permute-start.8 = (bf16[1024,2048]{1,0:T(8,128)(2,1)S(1)}, bf16[1024,2048]{1,0:T(8,128)(2,1)S(1)}, u32[]{:S(2)}, u32[]{:S(2)}) collective-permute-start(bf16[1024,2048]{1,0:T(8,128)(2,1)S(1)} %get-tuple-element.271), channel_id=1, source_target_pairs={{0,1},{1,0},{2,3},{3,2},{4,5},{5,4},{6,7},{7,6},{8,9},{9,8},{10,11... | collective-permute-start | bytes 12582920 | tf_op jit(solution)/shard_map/ppermute | solution.py:581
  358.3 40.5 %collective-permute-start.6 = (bf16[512,1024]{1,0:T(8,128)(2,1)S(1)}, bf16[512,1024]{1,0:T(8,128)(2,1)S(1)}, u32[]{:S(2)}, u32[]{:S(2)}) collective-permute-start(bf16[512,1024]{1,0:T(8,128)(2,1)S(1)} %get-tuple-element.265), channel_id=1, source_target_pairs={{0,2},{1,3},{2,0},{3,1},{4,6},{5,7},{6,4},{7,5},{8,10},{9,11},{10,... | collective-permute-start | bytes 3145736 | tf_op jit(solution)/shard_map/ppermute | solution.py:581
  359.8 39.0 %collective-permute-start.7 = (bf16[512,1024]{1,0:T(8,128)(2,1)S(1)}, bf16[512,1024]{1,0:T(8,128)(2,1)S(1)}, u32[]{:S(2)}, u32[]{:S(2)}) collective-permute-start(bf16[512,1024]{1,0:T(8,128)(2,1)S(1)} %get-tuple-element.266), channel_id=1, source_target_pairs={{0,4},{1,5},{2,6},{3,7},{4,0},{5,1},{6,2},{7,3},{8,12},{9,13},{10,... | collective-permute-start | bytes 3145736 | tf_op jit(solution)/shard_map/ppermute | solution.py:581
  360.4 38.4 %collective-permute-start.4 = (bf16[256,1024]{1,0:T(8,128)(2,1)S(1)}, bf16[256,1024]{1,0:T(8,128)(2,1)S(1)}, u32[]{:S(2)}, u32[]{:S(2)}) collective-permute-start(bf16[256,1024]{1,0:T(8,128)(2,1)S(1)} %get-tuple-element.263), channel_id=1, source_target_pairs={{0,4},{1,5},{2,6},{3,7},{4,0},{5,1},{6,2},{7,3},{8,12},{9,13},{10,... | collective-permute-start | bytes 1572872 | tf_op jit(solution)/shard_map/ppermute | solution.py:581
  361.9 36.9 %collective-permute-start.5 = (bf16[256,1024]{1,0:T(8,128)(2,1)S(1)}, bf16[256,1024]{1,0:T(8,128)(2,1)S(1)}, u32[]{:S(2)}, u32[]{:S(2)}) collective-permute-start(bf16[256,1024]{1,0:T(8,128)(2,1)S(1)} %get-tuple-element.264), channel_id=1, source_target_pairs={{0,2},{1,3},{2,0},{3,1},{4,6},{5,7},{6,4},{7,5},{8,10},{9,11},{10,... | collective-permute-start | bytes 1572872 | tf_op jit(solution)/shard_map/ppermute | solution.py:581
  398.9 30.2 %collective-permute-start.11 = (bf16[1024,1280]{1,0:T(8,128)(2,1)}, bf16[1024,1280]{1,0:T(8,128)(2,1)}, u32[]{:S(2)}, u32[]{:S(2)}) collective-permute-start(bf16[1024,1280]{1,0:T(8,128)(2,1)} %get-tuple-element.288), channel_id=1, source_target_pairs={{0,1},{1,0},{2,3},{3,2},{4,5},{5,4},{6,7},{7,6},{8,9},{9,8},{10,11... | collective-permute-start | bytes 7864328 | tf_op jit(solution)/shard_map/ppermute | solution.py:581
  415.1 99.6 %reduce-scatter.6.cloned.1.call-start = ((), (), s32[]{:S(2)}) async-start(), calls=%async_computation.6 | async-start | bytes 1310720 | tf_op jit(solution)/shard_map/reduce_scatter | solution.py:966
  429.0 37.1 %collective-permute-start.12 = (bf16[512,1024]{1,0:T(8,128)(2,1)}, bf16[512,1024]{1,0:T(8,128)(2,1)}, u32[]{:S(2)}, u32[]{:S(2)}) collective-permute-start(bf16[512,1024]{1,0:T(8,128)(2,1)} %get-tuple-element.299), channel_id=1, source_target_pairs={{0,2},{1,3},{2,0},{3,1},{4,6},{5,7},{6,4},{7,5},{8,10},{9,11},{10,... | collective-permute-start | bytes 3145736 | tf_op jit(solution)/shard_map/ppermute | solution.py:581
  429.6 36.5 %collective-permute-start.13 = (bf16[512,1024]{1,0:T(8,128)(2,1)}, bf16[512,1024]{1,0:T(8,128)(2,1)}, u32[]{:S(2)}, u32[]{:S(2)}) collective-permute-start(bf16[512,1024]{1,0:T(8,128)(2,1)} %get-tuple-element.300), channel_id=1, source_target_pairs={{0,4},{1,5},{2,6},{3,7},{4,0},{5,1},{6,2},{7,3},{8,12},{9,13},{10,... | collective-permute-start | bytes 3145736 | tf_op jit(solution)/shard_map/ppermute | solution.py:581
  466.1 107.7 %reduce-scatter.8.cloned.1.call-start = ((), (), s32[]{:S(2)}) async-start(), calls=%async_computation.7 | async-start | bytes 1310720 | tf_op jit(solution)/shard_map/reduce_scatter | solution.py:966
  466.4 48.3 %collective-permute-start.18 = (bf16[1024,768]{1,0:T(8,128)(2,1)}, bf16[1024,768]{1,0:T(8,128)(2,1)}, u32[]{:S(2)}, u32[]{:S(2)}) collective-permute-start(bf16[1024,768]{1,0:T(8,128)(2,1)} %copy-done.32), channel_id=1, source_target_pairs={{0,1},{1,0},{2,3},{3,2},{4,5},{5,4},{6,7},{7,6},{8,9},{9,8},{10,11... | collective-permute-start | bytes 4718600 | tf_op jit(solution)/shard_map/ppermute | solution.py:581
  484.3 17.1 %collective-permute-start.14 = (bf16[256,1024]{1,0:T(8,128)(2,1)S(1)}, bf16[256,1024]{1,0:T(8,128)(2,1)S(1)}, u32[]{:S(2)}, u32[]{:S(2)}) collective-permute-start(bf16[256,1024]{1,0:T(8,128)(2,1)S(1)} %get-tuple-element.315), channel_id=1, source_target_pairs={{0,4},{1,5},{2,6},{3,7},{4,0},{5,1},{6,2},{7,3},{8,12},{9,13},{10,... | collective-permute-start | bytes 1572872 | tf_op jit(solution)/shard_map/ppermute | solution.py:581
  485.0 16.5 %collective-permute-start.15 = (bf16[256,1024]{1,0:T(8,128)(2,1)S(1)}, bf16[256,1024]{1,0:T(8,128)(2,1)S(1)}, u32[]{:S(2)}, u32[]{:S(2)}) collective-permute-start(bf16[256,1024]{1,0:T(8,128)(2,1)S(1)} %get-tuple-element.316), channel_id=1, source_target_pairs={{0,2},{1,3},{2,0},{3,1},{4,6},{5,7},{6,4},{7,5},{8,10},{9,11},{10,... | collective-permute-start | bytes 1572872 | tf_op jit(solution)/shard_map/ppermute | solution.py:581
  486.4 26.7 %collective-permute-start.16 = (bf16[512,640]{1,0:T(8,128)(2,1)S(1)}, bf16[512,640]{1,0:T(8,128)(2,1)S(1)}, u32[]{:S(2)}, u32[]{:S(2)}) collective-permute-start(bf16[512,640]{1,0:T(8,128)(2,1)S(1)} %get-tuple-element.317), channel_id=1, source_target_pairs={{0,2},{1,3},{2,0},{3,1},{4,6},{5,7},{6,4},{7,5},{8,10},{9,11},{10,... | collective-permute-start | bytes 1966088 | tf_op jit(solution)/shard_map/ppermute | solution.py:581
  487.0 26.1 %collective-permute-start.17 = (bf16[512,640]{1,0:T(8,128)(2,1)S(1)}, bf16[512,640]{1,0:T(8,128)(2,1)S(1)}, u32[]{:S(2)}, u32[]{:S(2)}) collective-permute-start(bf16[512,640]{1,0:T(8,128)(2,1)S(1)} %get-tuple-element.318), channel_id=1, source_target_pairs={{0,4},{1,5},{2,6},{3,7},{4,0},{5,1},{6,2},{7,3},{8,12},{9,13},{10,... | collective-permute-start | bytes 1966088 | tf_op jit(solution)/shard_map/ppermute | solution.py:581
  580.5 20.5 %collective-permute-start.39 = (f32[32,1280]{1,0:T(8,128)S(1)}, f32[32,1280]{1,0:T(8,128)S(1)}, u32[]{:S(2)}, u32[]{:S(2)}) collective-permute-start(f32[32,1280]{1,0:T(8,128)S(1)} %get-tuple-element.406), channel_id=1, source_target_pairs={{0,1},{1,0},{2,3},{3,2},{4,5},{5,4},{6,7},{7,6},{8,9},{9,8},{10,11... | collective-permute-start | bytes 491528 | tf_op jit(solution)/shard_map/ppermute | solution.py:581
  582.5 18.5 %collective-permute-start.37 = (f32[32,2048]{1,0:T(8,128)S(1)}, f32[32,2048]{1,0:T(8,128)S(1)}, u32[]{:S(2)}, u32[]{:S(2)}) collective-permute-start(f32[32,2048]{1,0:T(8,128)S(1)} %get-tuple-element.402), channel_id=1, source_target_pairs={{0,1},{1,0},{2,3},{3,2},{4,5},{5,4},{6,7},{7,6},{8,9},{9,8},{10,11... | collective-permute-start | bytes 786440 | tf_op jit(solution)/shard_map/ppermute | solution.py:581
  (97 other events, 631.7 us)
Sparse Core Ops, SparseCore 0:
  11.7 138.5 all-gather.2
  153.7 94.0 all-gather.4
  415.3 25.3 reduce-scatter.3
  466.3 25.3 reduce-scatter.5
  524.1 25.3 reduce-scatter.7

commit v3 on v2

--- a/solution.py
+++ b/solution.py
@@ -833,7 +833,7 @@
         compiler_params=PARAMS,
         cost_estimate=SHORT,
         name="norm_backward",
-    )(streamed(rows), gain.reshape(1, width), streamed(base), *grads)
+    )(streamed(rows), gain.reshape(1, width), streamed(base), *(map(streamed, grads) if len(grads) > 1 else grads))
     return *out[:-1], out[-1][:2]
 
 
@@ -1029,23 +1029,25 @@
     grad_mixed, grad_front, one_got, two_got, front_halves, cross_got = tie(
         (grad_mixed, grad_front, one_got, two_got, front_halves, cross_got)
     )
-    one_sum.receive(last, one_got)
     two_sum.receive(0, two_got)
     grad_mixed = two_sum.between(grad_mixed)
+    sent = two_sum.send(last)
+    grad_mixed, grad_front, sent, one_got, cross_got = tie(
+        (grad_mixed, grad_front, sent, one_got, cross_got)
+    )
+
+    two_got, front_got = two_sum.swap(last, sent), grid.turn(front_halves[0], 1)
+    one_sum.receive(last, one_got)
+    one_total = one_sum.planes()
     cross_sum = Sum(grid, cross_halves[1], cross_got)
-    sent, begun, one_total = two_sum.send(last), cross_sum.send(0), one_sum.planes()
-    grad_mixed, grad_front, sent, begun, one_total = tie(
-        (grad_mixed, grad_front, sent, begun, one_total)
-    )
-
-    one_total = across(one_total)
-    two_got, front_got = two_sum.swap(last, sent), grid.turn(front_halves[0], 1)
+    begun = cross_sum.send(0)
     split = 3 * PAIR * cut
     grad_normed = dot_nt(grad_front, weights[:, :split])
-    grad_mixed, grad_normed, two_got, front_got, begun = tie(
-        (grad_mixed, grad_normed, two_got, front_got, begun)
-    )
-
+    grad_mixed, grad_normed, two_got, front_got, begun, one_total = tie(
+        (grad_mixed, grad_normed, two_got, front_got, begun, one_total)
+    )
+
+    one_total = across(one_total)
     cross_got = cross_sum.swap(0, begun)
     two_sum.receive(last, two_got)
     two_total = two_sum.planes()
@@ -1064,7 +1066,9 @@
     grad_back = cross_sum.between(grad_back)
     front_sum = Sum(grid, front_halves[1], front_got)
     sent, begun = cross_sum.send(last), front_sum.send(0)
-    grad_back, sent, begun = tie((grad_back, sent, begun))
+    grad_back, sent, begun, grad_ckv, active_one = tie(
+        (grad_back, sent, begun, grad_ckv, active_one)
+    )
 
     cross_got, front_got = cross_sum.swap(last, sent), front_sum.swap(0, begun)
     back_got = grid.turn(back_halves[0], 1)
@@ -1079,19 +1083,20 @@
     token_grad, prompt_grad, output, cross_got, front_got, back_got, two_total = tie(
         (token_grad, prompt_grad, output, cross_got, front_got, back_got, two_total)
     )
-    cross_sum.receive(last, cross_got)
     front_sum.receive(0, front_got)
     token_grad = front_sum.between(token_grad)
     back_sum = Sum(grid, back_halves[1], back_got)
-    sent, begun, cross_total = front_sum.send(last), back_sum.send(0), cross_sum.planes()
-    output, sent, begun, cross_total, active_two = tie(
-        (output, sent, begun, cross_total, active_two)
-    )
-
-    cross_total = across(cross_total)
+    sent, begun = front_sum.send(last), back_sum.send(0)
+    output, sent, begun, cross_got, active_two = tie(
+        (output, sent, begun, cross_got, active_two)
+    )
+
+    cross_sum.receive(last, cross_got)
+    cross_total = cross_sum.planes()
     front_got, back_got = front_sum.swap(last, sent), back_sum.swap(0, begun)
     output = output + dot_nt(active_two[:, : 2 * quarter], rest_w[:, 3 * quarter : 5 * quarter])
-    output, front_got, back_got = tie((output, front_got, back_got))
+    output, front_got, back_got, cross_total = tie((output, front_got, back_got, cross_total))
+    cross_total = across(cross_total)
     front_sum.receive(last, front_got)
     back_sum.receive(0, back_got)
     output = back_sum.between(output)

time: 628 us -> 621 us (0.989)
  waiting for transfers between devices: 181 us -> 172 us
    ppermute x41, waiting for transfers between devices: 34.4 us -> 25.4 us  [turn(): return lax.ppermute(value, AXES, [(i, i ^ mask) for i in range(self.count)])]
    unnamed x152 -> x156, local copies, waits for them, and re-layouts: 36.4 us -> 31.1 us
  transfers between devices with their start and end apart: 46 -> 46, of which waited for: 12 -> 11; matrix products, arithmetic and copies ran while one was open for 13% -> 13% of each run, Pallas kernels for 31% -> 33%
where the time goes in v3:
time: 621 us; the launch traced here: 611 us
  Pallas kernels  264 us (43%)
  waiting for transfers between devices  172 us (28%)
  matrix products  63.1 us (10%)
  starting transfers between devices  42.7 us (7%)
  local copies, waits for them, and re-layouts  36.2 us (6%)
  between operations  21.9 us (4%)
  other arithmetic  10.9 us (2%)
    all_gather x1, waiting for transfers between devices, local(): weights = lax.all_gather(shard, AXES, axis=0, tiled=True)  137 us
    pallas_call x2, Pallas kernels, mlp(): pl.pallas_call(functools.partial(mlp_kernel, order), grid_spec=pltpu.Pref...  66 us
    pallas_call x15, Pallas kernels, call(): pl.pallas_call(kernel, grid_spec=pltpu.PrefetchScalarGridSpec(num_scalar_...  50 us
    dot_general x8, matrix products, dot_nt(): lax.dot_general(left, right, (((1,), (1,)), ((), ())), preferred_element_...  45.2 us
    ppermute x41, starting transfers between devices, turn(): return lax.ppermute(value, AXES, [(i, i ^ mask) for i in range(self.count)])  42.5 us
    pallas_call x3, Pallas kernels, self_backward(): pl.pallas_call(self_backward_kernel, grid=(count,), in_specs=[columns(seq...  35 us
    pallas_call x6, Pallas kernels, product(): pl.pallas_call(product_kernel, grid_spec=pltpu.PrefetchScalarGridSpec(num...  32 us
    unnamed x156, local copies, waits for them, and re-layouts  31.1 us
  transfers between devices with their start and end apart: 46, of which 11 were waited for; matrix products, arithmetic and copies ran while one was open for 13% of the time, Pallas kernels for 33%

profile of v3, /device:TPU:0, one launch (start us, length us, event | category | flops | bytes accessed | tf_op | source)
XLA Modules:
  0.0 611.0 jit_solution(5189748155402569885)
XLA Ops:
  13.5 136.8 %all-gather.3.cloned.1.call-done.right_ref.up_ref.down_ref = bf16[1024,10368]{1,0:T(8,128)(2,1)} async-done(((bf16[32,10368]{1,0:T(8,128)(2,1)}), bf16[1024,10368]{1,0:T(8,128)(2,1)}) %all-gather.3.cloned.1.call-update) | async-done | bytes 21233680 | tf_op jit(solution)/shard_map/all_gather | solution.py:940
  152.9 9.2 %matmul.1.qkv_ref = bf16[1024,3072]{1,0:T(8,128)(2,1)S(1)} custom-call(bf16[1024,1024]{1,0:T(8,128)(2,1)S(1)} %fusion.5.left_ref, bf16[1024,10368]{1,0:T(8,128)(2,1)} %all-gather.3.cloned.1.call-done.right_ref.up_ref.down_ref), custom_call_target="tpu_custom_call" | custom-call | flops 1 | bytes 1 | tf_op jit(solution)/shard_map/matmul/pallas_call | solution.py:447
  166.2 17.7 %self_forward.1 = (bf16[1024,1024]{1,0:T(8,128)(2,1)}, f32[8,16,1024]{2,1,0:T(8,128)}) custom-call(bf16[1024,3072]{1,0:T(8,128)(2,1)} %copy-done.1), custom_call_target="tpu_custom_call" | custom-call | flops 1 | bytes 1 | tf_op jit(solution)/shard_map/self_forward/pallas_call | solution.py:255
  199.1 10.3 %cross_forward.1 = (bf16[1024,1024]{1,0:T(8,128)(2,1)S(1)}, f32[8,16,1024]{2,1,0:T(8,128)S(1)}) custom-call(s32[1]{0:T(128)S(6)} %copy.65.limit_ref, bf16[1024,1024]{1,0:T(8,128)(2,1)S(1)} %fusion.39.query_ref, bf16[128,2048]{1,0:T(8,128)(2,1)S(1)} %fusion.20.kv_ref), custom_call_target="tpu_custom_call" | custom-call | flops 1 | bytes 1 | tf_op jit(solution)/shard_map/cross_forward/pallas_call | solution.py:297
  209.4 6.0 fusion.61
  218.6 18.6 %mlp.2 = (bf16[1024,2048]{1,0:T(8,128)(2,1)}, bf16[1024,2048]{1,0:T(8,128)(2,1)}, bf16[1024,1024]{1,0:T(8,128)(2,1)S(1)}, f32[1024,1024]{1,0:T(8,128)}) custom-call(s32[1]{0:T(128)} %bitcast.10.core_ref, bf16[1024,1024]{1,0:T(8,128)(2,1)S(1)} %add_convert_fusion.1.rows_ref, bf16[1024,1024]{1,0:T(8,128)(2,1)S(1)} %bitcast.113, ...), custom_call_target="tpu_custom_call" | custom-call | flops 1 | bytes 1 | tf_op jit(solution)/shard_map/mlp/pallas_call | solution.py:417
  238.5 9.4 %all-gather.5.cloned.1.call-done.up_ref.down_ref = bf16[1024,6144]{1,0:T(8,128)(2,1)} async-done(((bf16[32,6144]{1,0:T(8,128)(2,1)}), bf16[1024,6144]{1,0:T(8,128)(2,1)}) %all-gather.5.cloned.1.call-update) | async-done | bytes 12582928 | tf_op jit(solution)/shard_map/all_gather | solution.py:941
  249.5 47.3 %mlp.3 = (bf16[1024,2048]{1,0:T(8,128)(2,1)}, bf16[1024,2048]{1,0:T(8,128)(2,1)}, bf16[1024,2048]{1,0:T(8,128)(2,1)}, bf16[1024,2048]{1,0:T(8,128)(2,1)}, bf16[1...) custom-call(s32[1]{0:T(128)} %bitcast.10.core_ref, ...), custom_call_target="tpu_custom_call", output_to_operand_aliasing={{0}: (5, {}), {1}: (6, {})} | custom-call | flops 1 | bytes 1 | tf_op jit(solution)/shard_map/mlp/pallas_call | solution.py:417
  297.0 7.2 %norm_backward.3 = (f32[1024,1024]{1,0:T(8,128)S(1)}, bf16[1024,1024]{1,0:T(8,128)(2,1)S(1)}, f32[8,1024]{1,0:T(8,128)S(1)}) custom-call(f32[1024,1024]{1,0:T(8,128)} %copy-done.37, f32[1,1024]{1,0:T(1,128)S(1)} %get-tuple-element.423.gain_ref, bf16[1024,1024]{1,0:T(8,128)(2,1)} %bitcast.112, f32[1024,1024]{1,0:T(8,128)} %get-tuple-element.225.rest_0_, ...), custom_call_target="tpu_custom_call" | custom-call | flops 1 | bytes 1 | tf_op jit(solution)/shard_map/norm_backward/pallas_call | solution.py:824
  320.4 10.0 %cross_backward.1 = (bf16[1024,1024]{1,0:T(8,128)(2,1)S(1)}, bf16[128,2048]{1,0:T(8,128)(2,1)S(1)}) custom-call(s32[1]{0:T(128)S(6)} %copy.65.limit_ref, bf16[1024,1024]{1,0:T(8,128)(2,1)S(1)} %copy-done.15, bf16[128,2048]{1,0:T(8,128)(2,1)S(1)} %fusion.20.kv_ref, bf16[1024,1024]{1,0:T(8,128)(2,1)S(1)} %copy-done.13, ...), custom_call_target="tpu_custom_call" | custom-call | flops 1 | bytes 1 | tf_op jit(solution)/shard_map/cross_backward/pallas_call | solution.py:316
  342.4 6.0 norm_backward.4
  369.0 17.3 %self_backward.3.sent_ref.kept_ref = bf16[1024,1536]{1,0:T(8,128)(2,1)S(1)} custom-call(bf16[1024,3072]{1,0:T(8,128)(2,1)} %copy-done.1, bf16[1024,1024]{1,0:T(8,128)(2,1)} %get-tuple-element.210.mixed_ref.left_ref, bf16[1024,1024]{1,0:T(8,128)(2,1)S(1)} %convolution_convert_fusion.upstream_ref, f32[8,16,1024]{2,1,0:T(8,128)S(1)} %copy-done.16), custom_call_target="tpu_custom_call" | custom-call | flops 1 | bytes 1 | tf_op jit(solution)/shard_map/self_backward/pallas_call | solution.py:274
  386.3 8.6 %product.10 = (bf16[1024,1280]{1,0:T(8,128)(2,1)S(1)}, bf16[1024,1280]{1,0:T(8,128)(2,1)S(1)}) custom-call(s32[1]{0:T(128)} %bitcast.10.core_ref, bf16[1024,1024]{1,0:T(8,128)(2,1)} %copy-done.4, bf16[1024,1536]{1,0:T(8,128)(2,1)S(1)} %self_backward.3.sent_ref.kept_ref, ...), custom_call_target="tpu_custom_call", output_to_operand_aliasing={{0}: (4, {}), {1}: (5, {})} | custom-call | flops 1 | bytes 1 | tf_op jit(solution)/shard_map/product/pallas_call | solution.py:504
  411.1 7.6 %fusion.15 = f32[1024,1024]{1,0:T(8,128)} fusion(bf16[1024,1536]{1,0:T(8,128)(2,1)S(1)} %copy-done.6, bf16[1024,10368]{1,0:T(8,128)(2,1)} %all-gather.3.cloned.1.call-done.right_ref.up_ref.down_ref), kind=kOutput, calls=%fused_computation.23 | convolution fusion | flops 3221225472 | bytes 10485760 | tf_op jit(solution)/shard_map/dot_general | solution.py:35
  423.7 9.0 %self_backward.4.rest_0_ = bf16[1024,1536]{1,0:T(8,128)(2,1)S(1)} custom-call(bf16[1024,3072]{1,0:T(8,128)(2,1)} %copy-done.1, bf16[1024,1024]{1,0:T(8,128)(2,1)} %get-tuple-element.210.mixed_ref.left_ref, bf16[1024,1024]{1,0:T(8,128)(2,1)S(1)} %copy-done.8, f32[8,16,1024]{2,1,0:T(8,128)S(1)} %copy-done.17), custom_call_target="tpu_custom_call" | custom-call | flops 1 | bytes 1 | tf_op jit(solution)/shard_map/self_backward/pallas_call | solution.py:274
  440.2 8.8 %self_backward.5.sent_ref.kept_ref = bf16[1024,1536]{1,0:T(8,128)(2,1)S(1)} custom-call(bf16[1024,3072]{1,0:T(8,128)(2,1)} %copy-done.1, bf16[1024,1024]{1,0:T(8,128)(2,1)} %get-tuple-element.210.mixed_ref.left_ref, bf16[1024,1024]{1,0:T(8,128)(2,1)S(1)} %copy-done.9, f32[8,16,1024]{2,1,0:T(8,128)S(1)} %copy-done.18, ...), custom_call_target="tpu_custom_call", output_to_operand_aliasing={{}: (4, {})} | custom-call | flops 1 | bytes 1 | tf_op jit(solution)/shard_map/self_backward/pallas_call | solution.py:274
  449.0 7.4 %product.11 = (bf16[1024,768]{1,0:T(8,128)(2,1)S(1)}, bf16[1024,768]{1,0:T(8,128)(2,1)S(1)}) custom-call(s32[1]{0:T(128)} %bitcast.10.core_ref, bf16[1024,1024]{1,0:T(8,128)(2,1)} %copy-done.4, bf16[1024,1536]{1,0:T(8,128)(2,1)S(1)} %self_backward.5.sent_ref.kept_ref, bf16[1024,1536]{1,0:T(8,128)(2,1)S(1)} %self_backward.5.sent_ref.kept_ref), custom_call_target="tpu_custom_call" | custom-call | flops 1 | bytes 1 | tf_op jit(solution)/shard_map/product/pallas_call | solution.py:504
  468.7 5.3 fusion.13
  474.1 6.1 %fusion.31 = f32[1024,1024]{1,0:T(8,128)} fusion(f32[1024,1024]{1,0:T(8,128)S(1)} %copy-done.38, bf16[1024,1024]{1,0:T(8,128)(2,1)S(1)} %copy-done.29, bf16[1024,10368]{1,0:T(8,128)(2,1)} %all-gather.3.cloned.1.call-done.right_ref.up_ref.down_ref), kind=kOutput, calls=%fused_computation.35 | convolution fusion | flops 2148532224 | bytes 12582912 | tf_op jit(solution)/shard_map/dot_general | solution.py:35
  481.2 6.7 %norm_backward.5 = (f32[1024,1024]{1,0:T(8,128)}, f32[8,1024]{1,0:T(8,128)S(1)}) custom-call(bf16[1024,1024]{1,0:T(8,128)(2,1)} %bitcast.138, f32[1,1024]{1,0:T(1,128)S(1)} %copy-done.27, f32[1024,1024]{1,0:T(8,128)} %copy-done.19, f32[1024,1024]{1,0:T(8,128)S(1)} %add.196.rest_0_), custom_call_target="tpu_custom_call" | custom-call | flops 1 | bytes 1 | tf_op jit(solution)/shard_map/norm_backward/pallas_call | solution.py:824
  503.5 8.3 %fusion.34 = f32[1024,1024]{1,0:T(8,128)} fusion(f32[1024,1024]{1,0:T(8,128)S(1)} %copy-done.71, bf16[1024,6144]{1,0:T(8,128)(2,1)} %all-gather.5.cloned.1.call-done.up_ref.down_ref, bf16[1024,3072]{1,0:T(8,128)(2,1)S(1)} %bitcast.175), kind=kOutput, calls=%fused_computation.36 | convolution fusion | flops 4296015872 | bytes 16777216 | tf_op jit(solution)/shard_map/dot_general | solution.py:35
  536.9 5.6 collective-permute-done.25
  553.8 7.9 %collective-permute-start.28 = (bf16[64,768]{1,0:T(8,128)(2,1)S(1)}, bf16[64,768]{1,0:T(8,128)(2,1)S(1)}, u32[]{:S(2)}, u32[]{:S(2)}) collective-permute-start(bf16[64,768]{1,0:T(8,128)(2,1)S(1)} %get-tuple-element.386), channel_id=1, source_target_pairs={{0,8},{1,9},{2,10},{3,11},{4,12},{5,13},{6,14},{7,15},{8,0},{9,1},... | collective-permute-start | bytes 294920 | tf_op jit(solution)/shard_map/ppermute | solution.py:581
  595.2 7.7 %adam.1 = (f32[8,32,1024]{2,1,0:T(8,128)}, f32[8,32,1024]{2,1,0:T(8,128)}, f32[8,32,1024]{2,1,0:T(8,128)}, bf16[8,32,1024]{2,1,0:T(8,128)(2,1)}, f32[2,32,4096]{...) custom-call(f32[1]{0:T(128)} %bitcast.50.factor_ref, ...), custom_call_target="tpu_custom_call" | custom-call | flops 1 | bytes 1 | tf_op jit(solution)/shard_map/adam/pallas_call | solution.py:901
  (324 shorter events, 204.3 us)
Async XLA Ops:
  7.2 143.1 %all-gather.3.cloned.1.call-start = ((), (), s32[]{:S(2)}) async-start(), calls=%async_computation.3 | async-start | bytes 21897216 | tf_op jit(solution)/shard_map/all_gather | solution.py:940
  11.6 236.3 %all-gather.5.cloned.1.call-start = ((), (), s32[]{:S(2)}) async-start(), calls=%async_computation.4 | async-start | bytes 12976128 | tf_op jit(solution)/shard_map/all_gather | solution.py:941
  12.3 446.5 %reduce-scatter.4.cloned.1.call-start = ((), (), s32[]{:S(2)}) async-start(), calls=%async_computation.5 | async-start | bytes 1310720 | tf_op jit(solution)/shard_map/reduce_scatter | solution.py:966
  318.3 30.0 %collective-permute-start.2 = (bf16[512,1024]{1,0:T(8,128)(2,1)S(1)}, bf16[512,1024]{1,0:T(8,128)(2,1)S(1)}, u32[]{:S(2)}, u32[]{:S(2)}) collective-permute-start(bf16[512,1024]{1,0:T(8,128)(2,1)S(1)} %get-tuple-element.253), channel_id=1, source_target_pairs={{0,2},{1,3},{2,0},{3,1},{4,6},{5,7},{6,4},{7,5},{8,10},{9,11},{10,... | collective-permute-start | bytes 3145736 | tf_op jit(solution)/shard_map/ppermute | solution.py:581
  319.8 28.6 %collective-permute-start.3 = (bf16[512,1024]{1,0:T(8,128)(2,1)S(1)}, bf16[512,1024]{1,0:T(8,128)(2,1)S(1)}, u32[]{:S(2)}, u32[]{:S(2)}) collective-permute-start(bf16[512,1024]{1,0:T(8,128)(2,1)S(1)} %get-tuple-element.254), channel_id=1, source_target_pairs={{0,4},{1,5},{2,6},{3,7},{4,0},{5,1},{6,2},{7,3},{8,12},{9,13},{10,... | collective-permute-start | bytes 3145736 | tf_op jit(solution)/shard_map/ppermute | solution.py:581
  348.4 46.6 %collective-permute-start.8 = (bf16[1024,2048]{1,0:T(8,128)(2,1)S(1)}, bf16[1024,2048]{1,0:T(8,128)(2,1)S(1)}, u32[]{:S(2)}, u32[]{:S(2)}) collective-permute-start(bf16[1024,2048]{1,0:T(8,128)(2,1)S(1)} %get-tuple-element.276), channel_id=1, source_target_pairs={{0,1},{1,0},{2,3},{3,2},{4,5},{5,4},{6,7},{7,6},{8,9},{9,8},{10,11... | collective-permute-start | bytes 12582920 | tf_op jit(solution)/shard_map/ppermute | solution.py:581
  355.8 39.2 %collective-permute-start.6 = (bf16[512,1024]{1,0:T(8,128)(2,1)S(1)}, bf16[512,1024]{1,0:T(8,128)(2,1)S(1)}, u32[]{:S(2)}, u32[]{:S(2)}) collective-permute-start(bf16[512,1024]{1,0:T(8,128)(2,1)S(1)} %get-tuple-element.270), channel_id=1, source_target_pairs={{0,2},{1,3},{2,0},{3,1},{4,6},{5,7},{6,4},{7,5},{8,10},{9,11},{10,... | collective-permute-start | bytes 3145736 | tf_op jit(solution)/shard_map/ppermute | solution.py:581
  357.2 37.7 %collective-permute-start.7 = (bf16[512,1024]{1,0:T(8,128)(2,1)S(1)}, bf16[512,1024]{1,0:T(8,128)(2,1)S(1)}, u32[]{:S(2)}, u32[]{:S(2)}) collective-permute-start(bf16[512,1024]{1,0:T(8,128)(2,1)S(1)} %get-tuple-element.271), channel_id=1, source_target_pairs={{0,4},{1,5},{2,6},{3,7},{4,0},{5,1},{6,2},{7,3},{8,12},{9,13},{10,... | collective-permute-start | bytes 3145736 | tf_op jit(solution)/shard_map/ppermute | solution.py:581
  357.8 37.1 %collective-permute-start.4 = (bf16[256,1024]{1,0:T(8,128)(2,1)S(1)}, bf16[256,1024]{1,0:T(8,128)(2,1)S(1)}, u32[]{:S(2)}, u32[]{:S(2)}) collective-permute-start(bf16[256,1024]{1,0:T(8,128)(2,1)S(1)} %get-tuple-element.268), channel_id=1, source_target_pairs={{0,4},{1,5},{2,6},{3,7},{4,0},{5,1},{6,2},{7,3},{8,12},{9,13},{10,... | collective-permute-start | bytes 1572872 | tf_op jit(solution)/shard_map/ppermute | solution.py:581
  359.3 35.7 %collective-permute-start.5 = (bf16[256,1024]{1,0:T(8,128)(2,1)S(1)}, bf16[256,1024]{1,0:T(8,128)(2,1)S(1)}, u32[]{:S(2)}, u32[]{:S(2)}) collective-permute-start(bf16[256,1024]{1,0:T(8,128)(2,1)S(1)} %get-tuple-element.269), channel_id=1, source_target_pairs={{0,2},{1,3},{2,0},{3,1},{4,6},{5,7},{6,4},{7,5},{8,10},{9,11},{10,... | collective-permute-start | bytes 1572872 | tf_op jit(solution)/shard_map/ppermute | solution.py:581
  395.0 23.8 %collective-permute-start.11 = (bf16[1024,1280]{1,0:T(8,128)(2,1)S(1)}, bf16[1024,1280]{1,0:T(8,128)(2,1)}, u32[]{:S(2)}, u32[]{:S(2)}) collective-permute-start(bf16[1024,1280]{1,0:T(8,128)(2,1)S(1)} %get-tuple-element.290), channel_id=1, source_target_pairs={{0,1},{1,0},{2,3},{3,2},{4,5},{5,4},{6,7},{7,6},{8,9},{9,8},{10,11... | collective-permute-start | bytes 7864328 | tf_op jit(solution)/shard_map/ppermute | solution.py:581
  418.8 75.7 %reduce-scatter.6.cloned.1.call-start = ((), (), s32[]{:S(2)}) async-start(), calls=%async_computation.6 | async-start | bytes 1310720 | tf_op jit(solution)/shard_map/reduce_scatter | solution.py:966
  418.8 40.0 %collective-permute-start.12 = (bf16[512,1024]{1,0:T(8,128)(2,1)}, bf16[512,1024]{1,0:T(8,128)(2,1)}, u32[]{:S(2)}, u32[]{:S(2)}) collective-permute-start(bf16[512,1024]{1,0:T(8,128)(2,1)} %copy-done.33), channel_id=1, source_target_pairs={{0,2},{1,3},{2,0},{3,1},{4,6},{5,7},{6,4},{7,5},{8,10},{9,11},{10,... | collective-permute-start | bytes 3145736 | tf_op jit(solution)/shard_map/ppermute | solution.py:581
  420.4 38.4 %collective-permute-start.13 = (bf16[512,1024]{1,0:T(8,128)(2,1)}, bf16[512,1024]{1,0:T(8,128)(2,1)}, u32[]{:S(2)}, u32[]{:S(2)}) collective-permute-start(bf16[512,1024]{1,0:T(8,128)(2,1)} %copy-done.32), channel_id=1, source_target_pairs={{0,4},{1,5},{2,6},{3,7},{4,0},{5,1},{6,2},{7,3},{8,12},{9,13},{10,... | collective-permute-start | bytes 3145736 | tf_op jit(solution)/shard_map/ppermute | solution.py:581
  458.8 107.4 %reduce-scatter.8.cloned.1.call-start = ((), (), s32[]{:S(2)}) async-start(), calls=%async_computation.7 | async-start | bytes 1310720 | tf_op jit(solution)/shard_map/reduce_scatter | solution.py:966
  464.6 27.8 %collective-permute-start.14 = (bf16[256,1024]{1,0:T(8,128)(2,1)S(1)}, bf16[256,1024]{1,0:T(8,128)(2,1)S(1)}, u32[]{:S(2)}, u32[]{:S(2)}) collective-permute-start(bf16[256,1024]{1,0:T(8,128)(2,1)S(1)} %get-tuple-element.323), channel_id=1, source_target_pairs={{0,4},{1,5},{2,6},{3,7},{4,0},{5,1},{6,2},{7,3},{8,12},{9,13},{10,... | collective-permute-start | bytes 1572872 | tf_op jit(solution)/shard_map/ppermute | solution.py:581
  466.1 26.4 %collective-permute-start.15 = (bf16[256,1024]{1,0:T(8,128)(2,1)S(1)}, bf16[256,1024]{1,0:T(8,128)(2,1)S(1)}, u32[]{:S(2)}, u32[]{:S(2)}) collective-permute-start(bf16[256,1024]{1,0:T(8,128)(2,1)S(1)} %get-tuple-element.324), channel_id=1, source_target_pairs={{0,2},{1,3},{2,0},{3,1},{4,6},{5,7},{6,4},{7,5},{8,10},{9,11},{10,... | collective-permute-start | bytes 1572872 | tf_op jit(solution)/shard_map/ppermute | solution.py:581
  466.6 25.9 %collective-permute-start.16 = (bf16[512,640]{1,0:T(8,128)(2,1)S(1)}, bf16[512,640]{1,0:T(8,128)(2,1)S(1)}, u32[]{:S(2)}, u32[]{:S(2)}) collective-permute-start(bf16[512,640]{1,0:T(8,128)(2,1)S(1)} %get-tuple-element.325), channel_id=1, source_target_pairs={{0,2},{1,3},{2,0},{3,1},{4,6},{5,7},{6,4},{7,5},{8,10},{9,11},{10,... | collective-permute-start | bytes 1966088 | tf_op jit(solution)/shard_map/ppermute | solution.py:581
  468.1 24.4 %collective-permute-start.17 = (bf16[512,640]{1,0:T(8,128)(2,1)S(1)}, bf16[512,640]{1,0:T(8,128)(2,1)S(1)}, u32[]{:S(2)}, u32[]{:S(2)}) collective-permute-start(bf16[512,640]{1,0:T(8,128)(2,1)S(1)} %get-tuple-element.326), channel_id=1, source_target_pairs={{0,4},{1,5},{2,6},{3,7},{4,0},{5,1},{6,2},{7,3},{8,12},{9,13},{10,... | collective-permute-start | bytes 1966088 | tf_op jit(solution)/shard_map/ppermute | solution.py:581
  468.7 25.7 %collective-permute-start.18 = (bf16[1024,768]{1,0:T(8,128)(2,1)S(1)}, bf16[1024,768]{1,0:T(8,128)(2,1)}, u32[]{:S(2)}, u32[]{:S(2)}) collective-permute-start(bf16[1024,768]{1,0:T(8,128)(2,1)S(1)} %copy-done.31), channel_id=1, source_target_pairs={{0,1},{1,0},{2,3},{3,2},{4,5},{5,4},{6,7},{7,6},{8,9},{9,8},{10,11... | collective-permute-start | bytes 4718600 | tf_op jit(solution)/shard_map/ppermute | solution.py:581
  525.9 21.2 %collective-permute-start.26 = (bf16[64,1280]{1,0:T(8,128)(2,1)S(1)}, bf16[64,1280]{1,0:T(8,128)(2,1)S(1)}, u32[]{:S(2)}, u32[]{:S(2)}) collective-permute-start(bf16[64,1280]{1,0:T(8,128)(2,1)S(1)} %get-tuple-element.383), channel_id=1, source_target_pairs={{0,16},{1,17},{2,18},{3,19},{4,20},{5,21},{6,22},{7,23},{8,24},{9,... | collective-permute-start | bytes 491528 | tf_op jit(solution)/shard_map/ppermute | solution.py:581
  527.0 23.0 %collective-permute-start.27 = (bf16[64,1280]{1,0:T(8,128)(2,1)S(1)}, bf16[64,1280]{1,0:T(8,128)(2,1)S(1)}, u32[]{:S(2)}, u32[]{:S(2)}) collective-permute-start(bf16[64,1280]{1,0:T(8,128)(2,1)S(1)} %get-tuple-element.384), channel_id=1, source_target_pairs={{0,24},{1,25},{2,26},{3,27},{4,28},{5,29},{6,30},{7,31},{8,16},{9,... | collective-permute-start | bytes 491528 | tf_op jit(solution)/shard_map/ppermute | solution.py:581
  529.6 21.1 %collective-permute-start.23 = (bf16[256,384]{1,0:T(8,128)(2,1)S(1)}, bf16[256,384]{1,0:T(8,128)(2,1)S(1)}, u32[]{:S(2)}, u32[]{:S(2)}) collective-permute-start(bf16[256,384]{1,0:T(8,128)(2,1)S(1)} %get-tuple-element.362), channel_id=1, source_target_pairs={{0,4},{1,5},{2,6},{3,7},{4,0},{5,1},{6,2},{7,3},{8,12},{9,13},{10,... | collective-permute-start | bytes 589832 | tf_op jit(solution)/shard_map/ppermute | solution.py:581
  530.2 20.5 %collective-permute-start.24 = (bf16[256,384]{1,0:T(8,128)(2,1)S(1)}, bf16[256,384]{1,0:T(8,128)(2,1)S(1)}, u32[]{:S(2)}, u32[]{:S(2)}) collective-permute-start(bf16[256,384]{1,0:T(8,128)(2,1)S(1)} %get-tuple-element.363), channel_id=1, source_target_pairs={{0,2},{1,3},{2,0},{3,1},{4,6},{5,7},{6,4},{7,5},{8,10},{9,11},{10,... | collective-permute-start | bytes 589832 | tf_op jit(solution)/shard_map/ppermute | solution.py:581
  (99 other events, 719.7 us)
Sparse Core Ops, SparseCore 0:
  11.7 138.5 all-gather.2
  153.7 94.1 all-gather.4
  418.9 25.4 reduce-scatter.3
  459.0 25.3 reduce-scatter.5
  519.3 35.8 reduce-scatter.7

commit v4 on v3

--- a/solution.py
+++ b/solution.py
@@ -581,9 +581,19 @@
         return lax.ppermute(value, AXES, [(i, i ^ mask) for i in range(self.count)])
 
     def add_all(self, value):
-        for bit in range(self.bits):
-            value = value + self.turn(value, 1 << bit)
+        low = 1
+        for size in (2, self.chips, self.outer):
+            found = [value] + [self.turn(value, step * low) for step in range(1, size)]
+            place = (self.me // low) % size
+            if size > 2:
+                stack = jnp.stack(found)
+                found = [self.pick(stack, place ^ step) for step in range(size)]
+            value = sum(found[1:], found[0])
+            low *= size
         return value
+
+    def pick(self, stack, index):
+        return lax.dynamic_index_in_dim(stack, index, 0, keepdims=False)
 
     def unpair(self, total):
         total = total.reshape(2, total.shape[0] // 2, total.shape[1])
@@ -1057,46 +1067,48 @@
     grad_back = self_backward(
         qkv, mixed, grad_mixed, levels, cut + some, pairs - cut - some, pairs - cut, some, grad_back
     )
+    grad_back, one_total, two_total = tie((grad_back, one_total, two_total))
+
+    two_total = across(two_total)
     back_halves = product(core, normed_one, grad_back)
-    grad_back, back_halves, cross_got, one_total, two_total = tie(
-        (grad_back, back_halves, cross_got, one_total, two_total)
-    )
-    two_total = across(two_total)
+    grad_back, back_halves, cross_got = tie((grad_back, back_halves, cross_got))
     cross_sum.receive(0, cross_got)
     grad_back = cross_sum.between(grad_back)
+    sent = cross_sum.send(last)
+    grad_back, sent, grad_ckv, active_one, front_got = tie(
+        (grad_back, sent, grad_ckv, active_one, front_got)
+    )
+
+    cross_got, back_got = cross_sum.swap(last, sent), grid.turn(back_halves[0], 1)
     front_sum = Sum(grid, front_halves[1], front_got)
-    sent, begun = cross_sum.send(last), front_sum.send(0)
-    grad_back, sent, begun, grad_ckv, active_one = tie(
-        (grad_back, sent, begun, grad_ckv, active_one)
-    )
-
-    cross_got, front_got = cross_sum.swap(last, sent), front_sum.swap(0, begun)
-    back_got = grid.turn(back_halves[0], 1)
+    begun = front_sum.send(0)
     grad_normed = grad_normed + dot_nt(grad_back, weights[:, split : 3 * width])
+    prompt_grad = dot_nt(grad_ckv, ckv_w)[None]
+    grad_normed, prompt_grad, cross_got, back_got, two_total, begun = tie(
+        (grad_normed, prompt_grad, cross_got, back_got, two_total, begun)
+    )
+
+    front_got = front_sum.swap(0, begun)
+    cross_sum.receive(last, cross_got)
+    cross_total = cross_sum.planes()
+    grad_normed, cross_total = tie((grad_normed, cross_total))
+    cross_total = across(cross_total)
     token_grad, norm_one = norm_backward(
         tokens[0], gains[0], [grad_normed], grad_after_self, False
     )
     token_grad = token_grad[None]
-    prompt_grad = dot_nt(grad_ckv, ckv_w)[None]
     down_at = up_at + quarter
     output = after_cross + dot_nt(active_one, weights[:, down_at : down_at + quarter])
-    token_grad, prompt_grad, output, cross_got, front_got, back_got, two_total = tie(
-        (token_grad, prompt_grad, output, cross_got, front_got, back_got, two_total)
-    )
+    token_grad, output, front_got = tie((token_grad, output, front_got))
     front_sum.receive(0, front_got)
     token_grad = front_sum.between(token_grad)
     back_sum = Sum(grid, back_halves[1], back_got)
     sent, begun = front_sum.send(last), back_sum.send(0)
-    output, sent, begun, cross_got, active_two = tie(
-        (output, sent, begun, cross_got, active_two)
-    )
-
-    cross_sum.receive(last, cross_got)
-    cross_total = cross_sum.planes()
+    output, sent, begun, active_two = tie((output, sent, begun, active_two))
+
     front_got, back_got = front_sum.swap(last, sent), back_sum.swap(0, begun)
     output = output + dot_nt(active_two[:, : 2 * quarter], rest_w[:, 3 * quarter : 5 * quarter])
     output, front_got, back_got, cross_total = tie((output, front_got, back_got, cross_total))
-    cross_total = across(cross_total)
     front_sum.receive(last, front_got)
     back_sum.receive(0, back_got)
     output = back_sum.between(output)

time: 621 us -> 609 us (0.981)
  waiting for transfers between devices: 172 us -> 163 us
    ppermute x41 -> x43, waiting for transfers between devices: 25.4 us -> 16.4 us  [turn(): return lax.ppermute(value, AXES, [(i, i ^ mask) for i in range(self.count)])]
    ppermute x41 -> x43, starting transfers between devices: 42.5 us -> 38.9 us  [turn(): return lax.ppermute(value, AXES, [(i, i ^ mask) for i in range(self.count)])]
    unnamed x156 -> x150, local copies, waits for them, and re-layouts: 31.1 us -> 30.6 us
  transfers between devices with their start and end apart: 46 -> 48, of which waited for: 11 -> 13; matrix products, arithmetic and copies ran while one was open for 13% -> 13% of each run, Pallas kernels for 33% -> 32%
where the time goes in v4:
time: 609 us; the launch traced here: 599 us
  Pallas kernels  264 us (43%)
  waiting for transfers between devices  163 us (27%)
  matrix products  62.7 us (10%)
  starting transfers between devices  39.1 us (6%)
  local copies, waits for them, and re-layouts  35.8 us (6%)
  between operations  22 us (4%)
  other arithmetic  11.9 us (2%)
    all_gather x1, waiting for transfers between devices, local(): weights = lax.all_gather(shard, AXES, axis=0, tiled=True)  137 us
    pallas_call x2, Pallas kernels, mlp(): pl.pallas_call(functools.partial(mlp_kernel, order), grid_spec=pltpu.Pref...  66.5 us
    pallas_call x15, Pallas kernels, call(): pl.pallas_call(kernel, grid_spec=pltpu.PrefetchScalarGridSpec(num_scalar_...  49.3 us
    dot_general x8, matrix products, dot_nt(): lax.dot_general(left, right, (((1,), (1,)), ((), ())), preferred_element_...  44.7 us
    ppermute x43, starting transfers between devices, turn(): return lax.ppermute(value, AXES, [(i, i ^ mask) for i in range(self.count)])  38.9 us
    pallas_call x3, Pallas kernels, self_backward(): pl.pallas_call(self_backward_kernel, grid=(count,), in_specs=[columns(seq...  35.1 us
    pallas_call x6, Pallas kernels, product(): pl.pallas_call(product_kernel, grid_spec=pltpu.PrefetchScalarGridSpec(num...  32.2 us
    unnamed x150, local copies, waits for them, and re-layouts  30.6 us
  transfers between devices with their start and end apart: 48, of which 13 were waited for; matrix products, arithmetic and copies ran while one was open for 13% of the time, Pallas kernels for 32%

profile of v4, /device:TPU:0, one launch (start us, length us, event | category | flops | bytes accessed | tf_op | source)
XLA Modules:
  0.0 598.7 jit_solution(819640342267026552)
XLA Ops:
  13.5 136.8 %all-gather.3.cloned.1.call-done.right_ref.up_ref.down_ref = bf16[1024,10368]{1,0:T(8,128)(2,1)} async-done(((bf16[32,10368]{1,0:T(8,128)(2,1)}), bf16[1024,10368]{1,0:T(8,128)(2,1)}) %all-gather.3.cloned.1.call-update) | async-done | bytes 21233680 | tf_op jit(solution)/shard_map/all_gather | solution.py:950
  152.9 9.2 %matmul.1.qkv_ref = bf16[1024,3072]{1,0:T(8,128)(2,1)S(1)} custom-call(bf16[1024,1024]{1,0:T(8,128)(2,1)S(1)} %fusion.5.left_ref, bf16[1024,10368]{1,0:T(8,128)(2,1)} %all-gather.3.cloned.1.call-done.right_ref.up_ref.down_ref), custom_call_target="tpu_custom_call" | custom-call | flops 1 | bytes 1 | tf_op jit(solution)/shard_map/matmul/pallas_call | solution.py:447
  166.3 17.7 %self_forward.1 = (bf16[1024,1024]{1,0:T(8,128)(2,1)}, f32[8,16,1024]{2,1,0:T(8,128)}) custom-call(bf16[1024,3072]{1,0:T(8,128)(2,1)} %copy-done.1), custom_call_target="tpu_custom_call" | custom-call | flops 1 | bytes 1 | tf_op jit(solution)/shard_map/self_forward/pallas_call | solution.py:255
  199.1 10.3 %cross_forward.1 = (bf16[1024,1024]{1,0:T(8,128)(2,1)S(1)}, f32[8,16,1024]{2,1,0:T(8,128)S(1)}) custom-call(s32[1]{0:T(128)S(6)} %copy.65.limit_ref, bf16[1024,1024]{1,0:T(8,128)(2,1)S(1)} %fusion.39.query_ref, bf16[128,2048]{1,0:T(8,128)(2,1)S(1)} %fusion.20.kv_ref), custom_call_target="tpu_custom_call" | custom-call | flops 1 | bytes 1 | tf_op jit(solution)/shard_map/cross_forward/pallas_call | solution.py:297
  209.4 6.1 %fusion.63 = (f32[1024]{0:T(1024)S(1)}, f32[1024,1024]{1,0:T(8,128)S(1)}) fusion(f32[1024,1024]{1,0:T(8,128)} %copy-done.35, bf16[1024,1024]{1,0:T(8,128)(2,1)S(1)} %get-tuple-element.214.left_ref.mixed_ref, bf16[1024,10368]{1,0:T(8,128)(2,1)} %all-gather.3.cloned.1.call-done.right_ref.up_ref.down_ref), kind=kOutput, calls=%fused_computation.90 | convolution fusion | flops 2149579776 | bytes 12587008 | tf_op jit(solution)/shard_map/dot_general | solution.py:31
  218.6 18.7 %mlp.2 = (bf16[1024,2048]{1,0:T(8,128)(2,1)}, bf16[1024,2048]{1,0:T(8,128)(2,1)}, bf16[1024,1024]{1,0:T(8,128)(2,1)S(1)}, f32[1024,1024]{1,0:T(8,128)}) custom-call(s32[1]{0:T(128)} %bitcast.10.core_ref, bf16[1024,1024]{1,0:T(8,128)(2,1)S(1)} %add_convert_fusion.1.rows_ref, bf16[1024,1024]{1,0:T(8,128)(2,1)S(1)} %bitcast.132, ...), custom_call_target="tpu_custom_call" | custom-call | flops 1 | bytes 1 | tf_op jit(solution)/shard_map/mlp/pallas_call | solution.py:417
  238.7 9.2 %all-gather.5.cloned.1.call-done.up_ref.down_ref = bf16[1024,6144]{1,0:T(8,128)(2,1)} async-done(((bf16[32,6144]{1,0:T(8,128)(2,1)}), bf16[1024,6144]{1,0:T(8,128)(2,1)}) %all-gather.5.cloned.1.call-update) | async-done | bytes 12582928 | tf_op jit(solution)/shard_map/all_gather | solution.py:951
  249.4 47.7 %mlp.3 = (bf16[1024,2048]{1,0:T(8,128)(2,1)}, bf16[1024,2048]{1,0:T(8,128)(2,1)}, bf16[1024,2048]{1,0:T(8,128)(2,1)}, bf16[1024,2048]{1,0:T(8,128)(2,1)}, bf16[1...) custom-call(s32[1]{0:T(128)} %bitcast.10.core_ref, ...), custom_call_target="tpu_custom_call", output_to_operand_aliasing={{0}: (5, {}), {1}: (6, {})} | custom-call | flops 1 | bytes 1 | tf_op jit(solution)/shard_map/mlp/pallas_call | solution.py:417
  297.5 7.2 %norm_backward.3 = (f32[1024,1024]{1,0:T(8,128)S(1)}, bf16[1024,1024]{1,0:T(8,128)(2,1)S(1)}, f32[8,1024]{1,0:T(8,128)S(1)}) custom-call(f32[1024,1024]{1,0:T(8,128)} %copy-done.36, f32[1,1024]{1,0:T(1,128)S(1)} %get-tuple-element.429.gain_ref, bf16[1024,1024]{1,0:T(8,128)(2,1)} %bitcast.131, f32[1024,1024]{1,0:T(8,128)} %get-tuple-element.228.rest_0_, ...), custom_call_target="tpu_custom_call" | custom-call | flops 1 | bytes 1 | tf_op jit(solution)/shard_map/norm_backward/pallas_call | solution.py:834
  320.6 10.0 %cross_backward.1 = (bf16[1024,1024]{1,0:T(8,128)(2,1)S(1)}, bf16[128,2048]{1,0:T(8,128)(2,1)S(1)}) custom-call(s32[1]{0:T(128)S(6)} %copy.65.limit_ref, bf16[1024,1024]{1,0:T(8,128)(2,1)S(1)} %copy-done.16, bf16[128,2048]{1,0:T(8,128)(2,1)S(1)} %fusion.20.kv_ref, bf16[1024,1024]{1,0:T(8,128)(2,1)S(1)} %copy-done.14, ...), custom_call_target="tpu_custom_call" | custom-call | flops 1 | bytes 1 | tf_op jit(solution)/shard_map/cross_backward/pallas_call | solution.py:316
  342.7 6.0 norm_backward.4
  369.2 17.3 %self_backward.3.sent_ref.kept_ref = bf16[1024,1536]{1,0:T(8,128)(2,1)S(1)} custom-call(bf16[1024,3072]{1,0:T(8,128)(2,1)} %copy-done.1, bf16[1024,1024]{1,0:T(8,128)(2,1)} %get-tuple-element.213.mixed_ref.left_ref, bf16[1024,1024]{1,0:T(8,128)(2,1)S(1)} %convolution_convert_fusion.upstream_ref, f32[8,16,1024]{2,1,0:T(8,128)S(1)} %copy-done.17), custom_call_target="tpu_custom_call" | custom-call | flops 1 | bytes 1 | tf_op jit(solution)/shard_map/self_backward/pallas_call | solution.py:274
  386.5 8.6 %product.10 = (bf16[1024,1280]{1,0:T(8,128)(2,1)S(1)}, bf16[1024,1280]{1,0:T(8,128)(2,1)S(1)}) custom-call(s32[1]{0:T(128)} %bitcast.10.core_ref, bf16[1024,1024]{1,0:T(8,128)(2,1)} %copy-done.4, bf16[1024,1536]{1,0:T(8,128)(2,1)S(1)} %self_backward.3.sent_ref.kept_ref, ...), custom_call_target="tpu_custom_call", output_to_operand_aliasing={{0}: (4, {}), {1}: (5, {})} | custom-call | flops 1 | bytes 1 | tf_op jit(solution)/shard_map/product/pallas_call | solution.py:504
  411.4 7.6 %fusion.15 = f32[1024,1024]{1,0:T(8,128)} fusion(bf16[1024,1536]{1,0:T(8,128)(2,1)S(1)} %copy-done.6, bf16[1024,10368]{1,0:T(8,128)(2,1)} %all-gather.3.cloned.1.call-done.right_ref.up_ref.down_ref), kind=kOutput, calls=%fused_computation.23 | convolution fusion | flops 3221225472 | bytes 10485760 | tf_op jit(solution)/shard_map/dot_general | solution.py:35
  423.9 9.0 %self_backward.4.rest_0_ = bf16[1024,1536]{1,0:T(8,128)(2,1)S(1)} custom-call(bf16[1024,3072]{1,0:T(8,128)(2,1)} %copy-done.1, bf16[1024,1024]{1,0:T(8,128)(2,1)} %get-tuple-element.213.mixed_ref.left_ref, bf16[1024,1024]{1,0:T(8,128)(2,1)S(1)} %copy-done.8, f32[8,16,1024]{2,1,0:T(8,128)S(1)} %copy-done.18), custom_call_target="tpu_custom_call" | custom-call | flops 1 | bytes 1 | tf_op jit(solution)/shard_map/self_backward/pallas_call | solution.py:274
  440.5 8.8 %self_backward.5.sent_ref.kept_ref = bf16[1024,1536]{1,0:T(8,128)(2,1)S(1)} custom-call(bf16[1024,3072]{1,0:T(8,128)(2,1)} %copy-done.1, bf16[1024,1024]{1,0:T(8,128)(2,1)} %get-tuple-element.213.mixed_ref.left_ref, bf16[1024,1024]{1,0:T(8,128)(2,1)S(1)} %copy-done.9, f32[8,16,1024]{2,1,0:T(8,128)S(1)} %copy-done.19, ...), custom_call_target="tpu_custom_call", output_to_operand_aliasing={{}: (4, {})} | custom-call | flops 1 | bytes 1 | tf_op jit(solution)/shard_map/self_backward/pallas_call | solution.py:274
  449.4 7.6 %product.11 = (bf16[1024,768]{1,0:T(8,128)(2,1)S(1)}, bf16[1024,768]{1,0:T(8,128)(2,1)S(1)}) custom-call(s32[1]{0:T(128)} %bitcast.10.core_ref, bf16[1024,1024]{1,0:T(8,128)(2,1)} %copy-done.4, bf16[1024,1536]{1,0:T(8,128)(2,1)S(1)} %self_backward.5.sent_ref.kept_ref, bf16[1024,1536]{1,0:T(8,128)(2,1)S(1)} %self_backward.5.sent_ref.kept_ref), custom_call_target="tpu_custom_call" | custom-call | flops 1 | bytes 1 | tf_op jit(solution)/shard_map/product/pallas_call | solution.py:504
  463.2 5.4 fusion.13
  487.7 5.4 fusion.31
  495.8 6.8 %norm_backward.5 = (f32[1024,1024]{1,0:T(8,128)}, f32[8,1024]{1,0:T(8,128)S(1)}) custom-call(bf16[1024,1024]{1,0:T(8,128)(2,1)} %bitcast.157, f32[1,1024]{1,0:T(1,128)S(1)} %copy-done.28, f32[1024,1024]{1,0:T(8,128)} %copy-done.20, f32[1024,1024]{1,0:T(8,128)S(1)} %copy-done.12), custom_call_target="tpu_custom_call" | custom-call | flops 1 | bytes 1 | tf_op jit(solution)/shard_map/norm_backward/pallas_call | solution.py:834
  510.6 8.6 %fusion.34 = f32[1024,1024]{1,0:T(8,128)} fusion(f32[1024,1024]{1,0:T(8,128)S(1)} %fusion.31, bf16[1024,6144]{1,0:T(8,128)(2,1)} %all-gather.5.cloned.1.call-done.up_ref.down_ref, bf16[1024,3072]{1,0:T(8,128)(2,1)S(1)} %bitcast.201), kind=kOutput, calls=%fused_computation.36 | convolution fusion | flops 4296015872 | bytes 16777216 | tf_op jit(solution)/shard_map/dot_general | solution.py:35
  519.2 5.2 collective-permute-done.21
  536.6 5.3 fusion.23
  582.9 7.7 %adam.1 = (f32[8,32,1024]{2,1,0:T(8,128)}, f32[8,32,1024]{2,1,0:T(8,128)}, f32[8,32,1024]{2,1,0:T(8,128)}, bf16[8,32,1024]{2,1,0:T(8,128)(2,1)}, f32[2,32,4096]{...) custom-call(f32[1]{0:T(128)} %bitcast.59.factor_ref, ...), custom_call_target="tpu_custom_call" | custom-call | flops 1 | bytes 1 | tf_op jit(solution)/shard_map/adam/pallas_call | solution.py:911
  (324 shorter events, 194.6 us)
Async XLA Ops:
  7.2 143.1 %all-gather.3.cloned.1.call-start = ((), (), s32[]{:S(2)}) async-start(), calls=%async_computation.3 | async-start | bytes 21897216 | tf_op jit(solution)/shard_map/all_gather | solution.py:950
  11.6 236.3 %all-gather.5.cloned.1.call-start = ((), (), s32[]{:S(2)}) async-start(), calls=%async_computation.4 | async-start | bytes 12976128 | tf_op jit(solution)/shard_map/all_gather | solution.py:951
  12.3 437.0 %reduce-scatter.4.cloned.1.call-start = ((), (), s32[]{:S(2)}) async-start(), calls=%async_computation.5 | async-start | bytes 1310720 | tf_op jit(solution)/shard_map/reduce_scatter | solution.py:976
  297.2 17.4 %collective-permute-start = (bf16[1024,2048]{1,0:T(8,128)(2,1)}, bf16[1024,2048]{1,0:T(8,128)(2,1)}, u32[]{:S(2)}, u32[]{:S(2)}) collective-permute-start(bf16[1024,2048]{1,0:T(8,128)(2,1)} %get-tuple-element.232), channel_id=1, source_target_pairs={{0,1},{1,0},{2,3},{3,2},{4,5},{5,4},{6,7},{7,6},{8,9},{9,8},{10,11... | collective-permute-start | bytes 12582920 | tf_op jit(solution)/shard_map/ppermute | solution.py:581
  318.3 19.5 %collective-permute-start.1 = (bf16[1024,2048]{1,0:T(8,128)(2,1)S(1)}, bf16[1024,2048]{1,0:T(8,128)(2,1)S(1)}, u32[]{:S(2)}, u32[]{:S(2)}) collective-permute-start(bf16[1024,2048]{1,0:T(8,128)(2,1)S(1)} %copy-done.68), channel_id=1, source_target_pairs={{0,1},{1,0},{2,3},{3,2},{4,5},{5,4},{6,7},{7,6},{8,9},{9,8},{10,11... | collective-permute-start | bytes 12582920 | tf_op jit(solution)/shard_map/ppermute | solution.py:581
  318.6 30.0 %collective-permute-start.2 = (bf16[512,1024]{1,0:T(8,128)(2,1)S(1)}, bf16[512,1024]{1,0:T(8,128)(2,1)S(1)}, u32[]{:S(2)}, u32[]{:S(2)}) collective-permute-start(bf16[512,1024]{1,0:T(8,128)(2,1)S(1)} %get-tuple-element.256), channel_id=1, source_target_pairs={{0,2},{1,3},{2,0},{3,1},{4,6},{5,7},{6,4},{7,5},{8,10},{9,11},{10,... | collective-permute-start | bytes 3145736 | tf_op jit(solution)/shard_map/ppermute | solution.py:581
  320.0 28.7 %collective-permute-start.3 = (bf16[512,1024]{1,0:T(8,128)(2,1)S(1)}, bf16[512,1024]{1,0:T(8,128)(2,1)S(1)}, u32[]{:S(2)}, u32[]{:S(2)}) collective-permute-start(bf16[512,1024]{1,0:T(8,128)(2,1)S(1)} %get-tuple-element.257), channel_id=1, source_target_pairs={{0,4},{1,5},{2,6},{3,7},{4,0},{5,1},{6,2},{7,3},{8,12},{9,13},{10,... | collective-permute-start | bytes 3145736 | tf_op jit(solution)/shard_map/ppermute | solution.py:581
  348.7 46.5 %collective-permute-start.8 = (bf16[1024,2048]{1,0:T(8,128)(2,1)S(1)}, bf16[1024,2048]{1,0:T(8,128)(2,1)S(1)}, u32[]{:S(2)}, u32[]{:S(2)}) collective-permute-start(bf16[1024,2048]{1,0:T(8,128)(2,1)S(1)} %get-tuple-element.279), channel_id=1, source_target_pairs={{0,1},{1,0},{2,3},{3,2},{4,5},{5,4},{6,7},{7,6},{8,9},{9,8},{10,11... | collective-permute-start | bytes 12582920 | tf_op jit(solution)/shard_map/ppermute | solution.py:581
  356.0 39.2 %collective-permute-start.6 = (bf16[512,1024]{1,0:T(8,128)(2,1)S(1)}, bf16[512,1024]{1,0:T(8,128)(2,1)S(1)}, u32[]{:S(2)}, u32[]{:S(2)}) collective-permute-start(bf16[512,1024]{1,0:T(8,128)(2,1)S(1)} %get-tuple-element.273), channel_id=1, source_target_pairs={{0,2},{1,3},{2,0},{3,1},{4,6},{5,7},{6,4},{7,5},{8,10},{9,11},{10,... | collective-permute-start | bytes 3145736 | tf_op jit(solution)/shard_map/ppermute | solution.py:581
  357.5 37.7 %collective-permute-start.7 = (bf16[512,1024]{1,0:T(8,128)(2,1)S(1)}, bf16[512,1024]{1,0:T(8,128)(2,1)S(1)}, u32[]{:S(2)}, u32[]{:S(2)}) collective-permute-start(bf16[512,1024]{1,0:T(8,128)(2,1)S(1)} %get-tuple-element.274), channel_id=1, source_target_pairs={{0,4},{1,5},{2,6},{3,7},{4,0},{5,1},{6,2},{7,3},{8,12},{9,13},{10,... | collective-permute-start | bytes 3145736 | tf_op jit(solution)/shard_map/ppermute | solution.py:581
  358.1 37.1 %collective-permute-start.4 = (bf16[256,1024]{1,0:T(8,128)(2,1)S(1)}, bf16[256,1024]{1,0:T(8,128)(2,1)S(1)}, u32[]{:S(2)}, u32[]{:S(2)}) collective-permute-start(bf16[256,1024]{1,0:T(8,128)(2,1)S(1)} %get-tuple-element.271), channel_id=1, source_target_pairs={{0,4},{1,5},{2,6},{3,7},{4,0},{5,1},{6,2},{7,3},{8,12},{9,13},{10,... | collective-permute-start | bytes 1572872 | tf_op jit(solution)/shard_map/ppermute | solution.py:581
  359.5 35.6 %collective-permute-start.5 = (bf16[256,1024]{1,0:T(8,128)(2,1)S(1)}, bf16[256,1024]{1,0:T(8,128)(2,1)S(1)}, u32[]{:S(2)}, u32[]{:S(2)}) collective-permute-start(bf16[256,1024]{1,0:T(8,128)(2,1)S(1)} %get-tuple-element.272), channel_id=1, source_target_pairs={{0,2},{1,3},{2,0},{3,1},{4,6},{5,7},{6,4},{7,5},{8,10},{9,11},{10,... | collective-permute-start | bytes 1572872 | tf_op jit(solution)/shard_map/ppermute | solution.py:581
  395.2 23.8 %collective-permute-start.11 = (bf16[1024,1280]{1,0:T(8,128)(2,1)S(1)}, bf16[1024,1280]{1,0:T(8,128)(2,1)}, u32[]{:S(2)}, u32[]{:S(2)}) collective-permute-start(bf16[1024,1280]{1,0:T(8,128)(2,1)S(1)} %get-tuple-element.293), channel_id=1, source_target_pairs={{0,1},{1,0},{2,3},{3,2},{4,5},{5,4},{6,7},{7,6},{8,9},{9,8},{10,11... | collective-permute-start | bytes 7864328 | tf_op jit(solution)/shard_map/ppermute | solution.py:581
  401.1 18.0 %collective-permute-start.9 = (bf16[256,1024]{1,0:T(8,128)(2,1)}, bf16[256,1024]{1,0:T(8,128)(2,1)}, u32[]{:S(2)}, u32[]{:S(2)}) collective-permute-start(bf16[256,1024]{1,0:T(8,128)(2,1)} %get-tuple-element.291), channel_id=1, source_target_pairs={{0,4},{1,5},{2,6},{3,7},{4,0},{5,1},{6,2},{7,3},{8,12},{9,13},{10,... | collective-permute-start | bytes 1572872 | tf_op jit(solution)/shard_map/ppermute | solution.py:581
  419.1 61.5 %reduce-scatter.6.cloned.1.call-start = ((), (), s32[]{:S(2)}) async-start(), calls=%async_computation.6 | async-start | bytes 1310720 | tf_op jit(solution)/shard_map/reduce_scatter | solution.py:976
  419.1 39.1 %collective-permute-start.12 = (bf16[512,1024]{1,0:T(8,128)(2,1)}, bf16[512,1024]{1,0:T(8,128)(2,1)}, u32[]{:S(2)}, u32[]{:S(2)}) collective-permute-start(bf16[512,1024]{1,0:T(8,128)(2,1)} %copy-done.32), channel_id=1, source_target_pairs={{0,2},{1,3},{2,0},{3,1},{4,6},{5,7},{6,4},{7,5},{8,10},{9,11},{10,... | collective-permute-start | bytes 3145736 | tf_op jit(solution)/shard_map/ppermute | solution.py:581
  420.6 37.7 %collective-permute-start.13 = (bf16[512,1024]{1,0:T(8,128)(2,1)}, bf16[512,1024]{1,0:T(8,128)(2,1)}, u32[]{:S(2)}, u32[]{:S(2)}) collective-permute-start(bf16[512,1024]{1,0:T(8,128)(2,1)} %copy-done.31), channel_id=1, source_target_pairs={{0,4},{1,5},{2,6},{3,7},{4,0},{5,1},{6,2},{7,3},{8,12},{9,13},{10,... | collective-permute-start | bytes 3145736 | tf_op jit(solution)/shard_map/ppermute | solution.py:581
  449.4 75.0 %reduce-scatter.8.cloned.1.call-start = ((), (), s32[]{:S(2)}) async-start(), calls=%async_computation.7 | async-start | bytes 1310720 | tf_op jit(solution)/shard_map/reduce_scatter | solution.py:976
  458.3 22.4 %collective-permute-start.16 = (bf16[1024,768]{1,0:T(8,128)(2,1)S(1)}, bf16[1024,768]{1,0:T(8,128)(2,1)}, u32[]{:S(2)}, u32[]{:S(2)}) collective-permute-start(bf16[1024,768]{1,0:T(8,128)(2,1)S(1)} %get-tuple-element.324), channel_id=1, source_target_pairs={{0,1},{1,0},{2,3},{3,2},{4,5},{5,4},{6,7},{7,6},{8,9},{9,8},{10,11... | collective-permute-start | bytes 4718600 | tf_op jit(solution)/shard_map/ppermute | solution.py:581
  461.0 18.0 %collective-permute-start.14 = (bf16[256,1024]{1,0:T(8,128)(2,1)S(1)}, bf16[256,1024]{1,0:T(8,128)(2,1)S(1)}, u32[]{:S(2)}, u32[]{:S(2)}) collective-permute-start(bf16[256,1024]{1,0:T(8,128)(2,1)S(1)} %get-tuple-element.322), channel_id=1, source_target_pairs={{0,4},{1,5},{2,6},{3,7},{4,0},{5,1},{6,2},{7,3},{8,12},{9,13},{10,... | collective-permute-start | bytes 1572872 | tf_op jit(solution)/shard_map/ppermute | solution.py:581
  462.5 16.6 %collective-permute-start.15 = (bf16[256,1024]{1,0:T(8,128)(2,1)S(1)}, bf16[256,1024]{1,0:T(8,128)(2,1)S(1)}, u32[]{:S(2)}, u32[]{:S(2)}) collective-permute-start(bf16[256,1024]{1,0:T(8,128)(2,1)S(1)} %get-tuple-element.323), channel_id=1, source_target_pairs={{0,2},{1,3},{2,0},{3,1},{4,6},{5,7},{6,4},{7,5},{8,10},{9,11},{10,... | collective-permute-start | bytes 1572872 | tf_op jit(solution)/shard_map/ppermute | solution.py:581
  485.6 16.9 %collective-permute-start.17 = (bf16[512,640]{1,0:T(8,128)(2,1)S(1)}, bf16[512,640]{1,0:T(8,128)(2,1)S(1)}, u32[]{:S(2)}, u32[]{:S(2)}) collective-permute-start(bf16[512,640]{1,0:T(8,128)(2,1)S(1)} %get-tuple-element.336), channel_id=1, source_target_pairs={{0,2},{1,3},{2,0},{3,1},{4,6},{5,7},{6,4},{7,5},{8,10},{9,11},{10,... | collective-permute-start | bytes 1966088 | tf_op jit(solution)/shard_map/ppermute | solution.py:581
  543.4 38.5 %collective-permute-start.40 = (f32[32,2048]{1,0:T(8,128)S(1)}, f32[32,2048]{1,0:T(8,128)S(1)}, u32[]{:S(2)}, u32[]{:S(2)}) collective-permute-start(f32[32,2048]{1,0:T(8,128)S(1)} %get-tuple-element.416), channel_id=1, source_target_pairs={{0,1},{1,0},{2,3},{3,2},{4,5},{5,4},{6,7},{7,6},{8,9},{9,8},{10,11... | collective-permute-start | bytes 786440 | tf_op jit(solution)/shard_map/ppermute | solution.py:581
  546.1 35.8 %collective-permute-start.41 = (f32[32,1280]{1,0:T(8,128)S(1)}, f32[32,1280]{1,0:T(8,128)S(1)}, u32[]{:S(2)}, u32[]{:S(2)}) collective-permute-start(f32[32,1280]{1,0:T(8,128)S(1)} %get-tuple-element.422), channel_id=1, source_target_pairs={{0,1},{1,0},{2,3},{3,2},{4,5},{5,4},{6,7},{7,6},{8,9},{9,8},{10,11... | collective-permute-start | bytes 491528 | tf_op jit(solution)/shard_map/ppermute | solution.py:581
  (98 other events, 616.0 us)
Sparse Core Ops, SparseCore 0:
  11.7 138.5 all-gather.2
  153.7 94.0 all-gather.4
  419.2 25.4 reduce-scatter.3
  449.5 25.4 reduce-scatter.5
  485.6 25.3 reduce-scatter.7

commit v5 on v4

--- a/solution.py
+++ b/solution.py
@@ -1089,17 +1089,16 @@
     )
 
     front_got = front_sum.swap(0, begun)
+    token_grad, norm_one = norm_backward(
+        tokens[0], gains[0], [grad_normed], grad_after_self, False
+    )
+    token_grad, cross_got = tie((token_grad[None], cross_got))
     cross_sum.receive(last, cross_got)
     cross_total = cross_sum.planes()
-    grad_normed, cross_total = tie((grad_normed, cross_total))
-    cross_total = across(cross_total)
-    token_grad, norm_one = norm_backward(
-        tokens[0], gains[0], [grad_normed], grad_after_self, False
-    )
-    token_grad = token_grad[None]
     down_at = up_at + quarter
     output = after_cross + dot_nt(active_one, weights[:, down_at : down_at + quarter])
-    token_grad, output, front_got = tie((token_grad, output, front_got))
+    token_grad, output, front_got, cross_total = tie((token_grad, output, front_got, cross_total))
+    cross_total = across(cross_total)
     front_sum.receive(0, front_got)
     token_grad = front_sum.between(token_grad)
     back_sum = Sum(grid, back_halves[1], back_got)

time: 609 us -> 613 us (level)
    unnamed x150 -> x148, local copies, waits for them, and re-layouts: 30.6 us -> 29.5 us
  transfers between devices with their start and end apart: 48 -> 48, of which waited for: 13 -> 13; matrix products, arithmetic and copies ran while one was open for 13% -> 14% of each run, Pallas kernels for 32% -> 33%
where the time goes in v5:
time: 613 us; the launch traced here: 603 us
  Pallas kernels  264 us (43%)
  waiting for transfers between devices  166 us (27%)
  matrix products  64.7 us (11%)
  starting transfers between devices  40.5 us (7%)
  local copies, waits for them, and re-layouts  34.7 us (6%)
  between operations  22 us (4%)
  other arithmetic  11.9 us (2%)
    all_gather x1, waiting for transfers between devices, local(): weights = lax.all_gather(shard, AXES, axis=0, tiled=True)  137 us
    pallas_call x2, Pallas kernels, mlp(): pl.pallas_call(functools.partial(mlp_kernel, order), grid_spec=pltpu.Pref...  66.4 us
    pallas_call x15, Pallas kernels, call(): pl.pallas_call(kernel, grid_spec=pltpu.PrefetchScalarGridSpec(num_scalar_...  49.4 us
    dot_general x8, matrix products, dot_nt(): lax.dot_general(left, right, (((1,), (1,)), ((), ())), preferred_element_...  46.7 us
    ppermute x43, starting transfers between devices, turn(): return lax.ppermute(value, AXES, [(i, i ^ mask) for i in range(self.count)])  40.3 us
    pallas_call x3, Pallas kernels, self_backward(): pl.pallas_call(self_backward_kernel, grid=(count,), in_specs=[columns(seq...  35.1 us
    pallas_call x6, Pallas kernels, product(): pl.pallas_call(product_kernel, grid_spec=pltpu.PrefetchScalarGridSpec(num...  32.2 us
    unnamed x148, local copies, waits for them, and re-layouts  29.5 us
  transfers between devices with their start and end apart: 48, of which 13 were waited for; matrix products, arithmetic and copies ran while one was open for 14% of the time, Pallas kernels for 33%

profile of v5, /device:TPU:0, one launch (start us, length us, event | category | flops | bytes accessed | tf_op | source)
XLA Modules:
  0.0 603.2 jit_solution(10890525769842840835)
XLA Ops:
  13.5 136.8 %all-gather.3.cloned.1.call-done.right_ref.up_ref.down_ref = bf16[1024,10368]{1,0:T(8,128)(2,1)} async-done(((bf16[32,10368]{1,0:T(8,128)(2,1)}), bf16[1024,10368]{1,0:T(8,128)(2,1)}) %all-gather.3.cloned.1.call-update) | async-done | bytes 21233680 | tf_op jit(solution)/shard_map/all_gather | solution.py:950
  152.9 9.3 %matmul.1.qkv_ref = bf16[1024,3072]{1,0:T(8,128)(2,1)S(1)} custom-call(bf16[1024,1024]{1,0:T(8,128)(2,1)S(1)} %fusion.5.left_ref, bf16[1024,10368]{1,0:T(8,128)(2,1)} %all-gather.3.cloned.1.call-done.right_ref.up_ref.down_ref), custom_call_target="tpu_custom_call" | custom-call | flops 1 | bytes 1 | tf_op jit(solution)/shard_map/matmul/pallas_call | solution.py:447
  166.2 17.7 %self_forward.1 = (bf16[1024,1024]{1,0:T(8,128)(2,1)}, f32[8,16,1024]{2,1,0:T(8,128)}) custom-call(bf16[1024,3072]{1,0:T(8,128)(2,1)} %copy-done.1), custom_call_target="tpu_custom_call" | custom-call | flops 1 | bytes 1 | tf_op jit(solution)/shard_map/self_forward/pallas_call | solution.py:255
  199.1 10.3 %cross_forward.1 = (bf16[1024,1024]{1,0:T(8,128)(2,1)S(1)}, f32[8,16,1024]{2,1,0:T(8,128)S(1)}) custom-call(s32[1]{0:T(128)S(6)} %copy.65.limit_ref, bf16[1024,1024]{1,0:T(8,128)(2,1)S(1)} %fusion.39.query_ref, bf16[128,2048]{1,0:T(8,128)(2,1)S(1)} %fusion.20.kv_ref), custom_call_target="tpu_custom_call" | custom-call | flops 1 | bytes 1 | tf_op jit(solution)/shard_map/cross_forward/pallas_call | solution.py:297
  209.4 6.1 %fusion.63 = (f32[1024]{0:T(1024)S(1)}, f32[1024,1024]{1,0:T(8,128)S(1)}) fusion(f32[1024,1024]{1,0:T(8,128)} %copy-done.35, bf16[1024,1024]{1,0:T(8,128)(2,1)S(1)} %get-tuple-element.216.left_ref.mixed_ref, bf16[1024,10368]{1,0:T(8,128)(2,1)} %all-gather.3.cloned.1.call-done.right_ref.up_ref.down_ref), kind=kOutput, calls=%fused_computation.90 | convolution fusion | flops 2149579776 | bytes 12587008 | tf_op jit(solution)/shard_map/dot_general | solution.py:31
  218.6 18.7 %mlp.2 = (bf16[1024,2048]{1,0:T(8,128)(2,1)}, bf16[1024,2048]{1,0:T(8,128)(2,1)}, bf16[1024,1024]{1,0:T(8,128)(2,1)S(1)}, f32[1024,1024]{1,0:T(8,128)}) custom-call(s32[1]{0:T(128)} %bitcast.10.core_ref, bf16[1024,1024]{1,0:T(8,128)(2,1)S(1)} %add_convert_fusion.1.rows_ref, bf16[1024,1024]{1,0:T(8,128)(2,1)S(1)} %bitcast.132, ...), custom_call_target="tpu_custom_call" | custom-call | flops 1 | bytes 1 | tf_op jit(solution)/shard_map/mlp/pallas_call | solution.py:417
  238.6 9.3 %all-gather.5.cloned.1.call-done.up_ref.down_ref = bf16[1024,6144]{1,0:T(8,128)(2,1)} async-done(((bf16[32,6144]{1,0:T(8,128)(2,1)}), bf16[1024,6144]{1,0:T(8,128)(2,1)}) %all-gather.5.cloned.1.call-update) | async-done | bytes 12582928 | tf_op jit(solution)/shard_map/all_gather | solution.py:951
  249.5 47.7 %mlp.3 = (bf16[1024,2048]{1,0:T(8,128)(2,1)}, bf16[1024,2048]{1,0:T(8,128)(2,1)}, bf16[1024,2048]{1,0:T(8,128)(2,1)}, bf16[1024,2048]{1,0:T(8,128)(2,1)}, bf16[1...) custom-call(s32[1]{0:T(128)} %bitcast.10.core_ref, ...), custom_call_target="tpu_custom_call", output_to_operand_aliasing={{0}: (5, {}), {1}: (6, {})} | custom-call | flops 1 | bytes 1 | tf_op jit(solution)/shard_map/mlp/pallas_call | solution.py:417
  297.5 7.2 %norm_backward.3 = (f32[1024,1024]{1,0:T(8,128)S(1)}, bf16[1024,1024]{1,0:T(8,128)(2,1)S(1)}, f32[8,1024]{1,0:T(8,128)S(1)}) custom-call(f32[1024,1024]{1,0:T(8,128)} %copy-done.36, f32[1,1024]{1,0:T(1,128)S(1)} %get-tuple-element.433.gain_ref, bf16[1024,1024]{1,0:T(8,128)(2,1)} %bitcast.131, f32[1024,1024]{1,0:T(8,128)} %get-tuple-element.230.rest_0_, ...), custom_call_target="tpu_custom_call" | custom-call | flops 1 | bytes 1 | tf_op jit(solution)/shard_map/norm_backward/pallas_call | solution.py:834
  320.8 10.0 %cross_backward.1 = (bf16[1024,1024]{1,0:T(8,128)(2,1)S(1)}, bf16[128,2048]{1,0:T(8,128)(2,1)S(1)}) custom-call(s32[1]{0:T(128)S(6)} %copy.65.limit_ref, bf16[1024,1024]{1,0:T(8,128)(2,1)S(1)} %copy-done.16, bf16[128,2048]{1,0:T(8,128)(2,1)S(1)} %fusion.20.kv_ref, bf16[1024,1024]{1,0:T(8,128)(2,1)S(1)} %copy-done.14, ...), custom_call_target="tpu_custom_call" | custom-call | flops 1 | bytes 1 | tf_op jit(solution)/shard_map/cross_backward/pallas_call | solution.py:316
  342.8 6.0 norm_backward.4
  369.3 17.3 %self_backward.3.sent_ref.kept_ref = bf16[1024,1536]{1,0:T(8,128)(2,1)S(1)} custom-call(bf16[1024,3072]{1,0:T(8,128)(2,1)} %copy-done.1, bf16[1024,1024]{1,0:T(8,128)(2,1)} %get-tuple-element.215.mixed_ref.left_ref, bf16[1024,1024]{1,0:T(8,128)(2,1)S(1)} %convolution_convert_fusion.upstream_ref, f32[8,16,1024]{2,1,0:T(8,128)S(1)} %copy-done.17), custom_call_target="tpu_custom_call" | custom-call | flops 1 | bytes 1 | tf_op jit(solution)/shard_map/self_backward/pallas_call | solution.py:274
  386.7 8.6 %product.10 = (bf16[1024,1280]{1,0:T(8,128)(2,1)S(1)}, bf16[1024,1280]{1,0:T(8,128)(2,1)S(1)}) custom-call(s32[1]{0:T(128)} %bitcast.10.core_ref, bf16[1024,1024]{1,0:T(8,128)(2,1)} %copy-done.4, bf16[1024,1536]{1,0:T(8,128)(2,1)S(1)} %self_backward.3.sent_ref.kept_ref, ...), custom_call_target="tpu_custom_call", output_to_operand_aliasing={{0}: (4, {}), {1}: (5, {})} | custom-call | flops 1 | bytes 1 | tf_op jit(solution)/shard_map/product/pallas_call | solution.py:504
  411.5 7.6 %fusion.15 = f32[1024,1024]{1,0:T(8,128)} fusion(bf16[1024,1536]{1,0:T(8,128)(2,1)S(1)} %copy-done.6, bf16[1024,10368]{1,0:T(8,128)(2,1)} %all-gather.3.cloned.1.call-done.right_ref.up_ref.down_ref), kind=kOutput, calls=%fused_computation.23 | convolution fusion | flops 3221225472 | bytes 10485760 | tf_op jit(solution)/shard_map/dot_general | solution.py:35
  424.1 9.0 %self_backward.4.rest_0_ = bf16[1024,1536]{1,0:T(8,128)(2,1)S(1)} custom-call(bf16[1024,3072]{1,0:T(8,128)(2,1)} %copy-done.1, bf16[1024,1024]{1,0:T(8,128)(2,1)} %get-tuple-element.215.mixed_ref.left_ref, bf16[1024,1024]{1,0:T(8,128)(2,1)S(1)} %copy-done.8, f32[8,16,1024]{2,1,0:T(8,128)S(1)} %copy-done.18), custom_call_target="tpu_custom_call" | custom-call | flops 1 | bytes 1 | tf_op jit(solution)/shard_map/self_backward/pallas_call | solution.py:274
  440.6 8.8 %self_backward.5.sent_ref.kept_ref = bf16[1024,1536]{1,0:T(8,128)(2,1)S(1)} custom-call(bf16[1024,3072]{1,0:T(8,128)(2,1)} %copy-done.1, bf16[1024,1024]{1,0:T(8,128)(2,1)} %get-tuple-element.215.mixed_ref.left_ref, bf16[1024,1024]{1,0:T(8,128)(2,1)S(1)} %copy-done.9, f32[8,16,1024]{2,1,0:T(8,128)S(1)} %copy-done.19, ...), custom_call_target="tpu_custom_call", output_to_operand_aliasing={{}: (4, {})} | custom-call | flops 1 | bytes 1 | tf_op jit(solution)/shard_map/self_backward/pallas_call | solution.py:274
  449.5 7.6 %product.11 = (bf16[1024,768]{1,0:T(8,128)(2,1)S(1)}, bf16[1024,768]{1,0:T(8,128)(2,1)S(1)}) custom-call(s32[1]{0:T(128)} %bitcast.10.core_ref, bf16[1024,1024]{1,0:T(8,128)(2,1)} %copy-done.4, bf16[1024,1536]{1,0:T(8,128)(2,1)S(1)} %self_backward.5.sent_ref.kept_ref, bf16[1024,1536]{1,0:T(8,128)(2,1)S(1)} %self_backward.5.sent_ref.kept_ref), custom_call_target="tpu_custom_call" | custom-call | flops 1 | bytes 1 | tf_op jit(solution)/shard_map/product/pallas_call | solution.py:504
  463.2 5.3 fusion.13
  482.9 7.3 %fusion.31 = f32[1024,1024]{1,0:T(8,128)} fusion(f32[1024,1024]{1,0:T(8,128)} %copy-done.36, bf16[1024,1024]{1,0:T(8,128)(2,1)S(1)} %copy-done.30, bf16[1024,10368]{1,0:T(8,128)(2,1)} %all-gather.3.cloned.1.call-done.right_ref.up_ref.down_ref), kind=kOutput, calls=%fused_computation.35 | convolution fusion | flops 2148532224 | bytes 12582912 | tf_op jit(solution)/shard_map/dot_general | solution.py:35
  490.2 6.6 %norm_backward.5 = (f32[1024,1024]{1,0:T(8,128)}, f32[8,1024]{1,0:T(8,128)S(1)}) custom-call(bf16[1024,1024]{1,0:T(8,128)(2,1)} %bitcast.157, f32[1,1024]{1,0:T(1,128)S(1)} %copy-done.28, f32[1024,1024]{1,0:T(8,128)} %copy-done.20, f32[1024,1024]{1,0:T(8,128)S(1)} %copy-done.12), custom_call_target="tpu_custom_call" | custom-call | flops 1 | bytes 1 | tf_op jit(solution)/shard_map/norm_backward/pallas_call | solution.py:834
  511.2 8.6 %fusion.34 = f32[1024,1024]{1,0:T(8,128)} fusion(f32[1024,1024]{1,0:T(8,128)S(1)} %copy-done.67, bf16[1024,6144]{1,0:T(8,128)(2,1)} %all-gather.5.cloned.1.call-done.up_ref.down_ref, bf16[1024,3072]{1,0:T(8,128)(2,1)S(1)} %bitcast.197), kind=kOutput, calls=%fused_computation.36 | convolution fusion | flops 4296015872 | bytes 16777216 | tf_op jit(solution)/shard_map/dot_general | solution.py:35
  519.7 5.6 collective-permute-done.21
  540.0 5.3 fusion.23
  587.4 7.7 %adam.1 = (f32[8,32,1024]{2,1,0:T(8,128)}, f32[8,32,1024]{2,1,0:T(8,128)}, f32[8,32,1024]{2,1,0:T(8,128)}, bf16[8,32,1024]{2,1,0:T(8,128)(2,1)}, f32[2,32,4096]{...) custom-call(f32[1]{0:T(128)} %bitcast.59.factor_ref, ...), custom_call_target="tpu_custom_call" | custom-call | flops 1 | bytes 1 | tf_op jit(solution)/shard_map/adam/pallas_call | solution.py:911
  (322 shorter events, 197.0 us)
Async XLA Ops:
  7.2 143.1 %all-gather.3.cloned.1.call-start = ((), (), s32[]{:S(2)}) async-start(), calls=%async_computation.3 | async-start | bytes 21897216 | tf_op jit(solution)/shard_map/all_gather | solution.py:950
  11.6 236.3 %all-gather.5.cloned.1.call-start = ((), (), s32[]{:S(2)}) async-start(), calls=%async_computation.4 | async-start | bytes 12976128 | tf_op jit(solution)/shard_map/all_gather | solution.py:951
  12.3 437.2 %reduce-scatter.4.cloned.1.call-start = ((), (), s32[]{:S(2)}) async-start(), calls=%async_computation.5 | async-start | bytes 1310720 | tf_op jit(solution)/shard_map/reduce_scatter | solution.py:976
  297.2 17.4 %collective-permute-start = (bf16[1024,2048]{1,0:T(8,128)(2,1)}, bf16[1024,2048]{1,0:T(8,128)(2,1)}, u32[]{:S(2)}, u32[]{:S(2)}) collective-permute-start(bf16[1024,2048]{1,0:T(8,128)(2,1)} %get-tuple-element.234), channel_id=1, source_target_pairs={{0,1},{1,0},{2,3},{3,2},{4,5},{5,4},{6,7},{7,6},{8,9},{9,8},{10,11... | collective-permute-start | bytes 12582920 | tf_op jit(solution)/shard_map/ppermute | solution.py:581
  318.3 19.6 %collective-permute-start.1 = (bf16[1024,2048]{1,0:T(8,128)(2,1)S(1)}, bf16[1024,2048]{1,0:T(8,128)(2,1)S(1)}, u32[]{:S(2)}, u32[]{:S(2)}) collective-permute-start(bf16[1024,2048]{1,0:T(8,128)(2,1)S(1)} %copy-done.66), channel_id=1, source_target_pairs={{0,1},{1,0},{2,3},{3,2},{4,5},{5,4},{6,7},{7,6},{8,9},{9,8},{10,11... | collective-permute-start | bytes 12582920 | tf_op jit(solution)/shard_map/ppermute | solution.py:581
  318.7 30.1 %collective-permute-start.2 = (bf16[512,1024]{1,0:T(8,128)(2,1)S(1)}, bf16[512,1024]{1,0:T(8,128)(2,1)S(1)}, u32[]{:S(2)}, u32[]{:S(2)}) collective-permute-start(bf16[512,1024]{1,0:T(8,128)(2,1)S(1)} %get-tuple-element.258), channel_id=1, source_target_pairs={{0,2},{1,3},{2,0},{3,1},{4,6},{5,7},{6,4},{7,5},{8,10},{9,11},{10,... | collective-permute-start | bytes 3145736 | tf_op jit(solution)/shard_map/ppermute | solution.py:581
  320.1 28.7 %collective-permute-start.3 = (bf16[512,1024]{1,0:T(8,128)(2,1)S(1)}, bf16[512,1024]{1,0:T(8,128)(2,1)S(1)}, u32[]{:S(2)}, u32[]{:S(2)}) collective-permute-start(bf16[512,1024]{1,0:T(8,128)(2,1)S(1)} %get-tuple-element.259), channel_id=1, source_target_pairs={{0,4},{1,5},{2,6},{3,7},{4,0},{5,1},{6,2},{7,3},{8,12},{9,13},{10,... | collective-permute-start | bytes 3145736 | tf_op jit(solution)/shard_map/ppermute | solution.py:581
  348.8 46.5 %collective-permute-start.8 = (bf16[1024,2048]{1,0:T(8,128)(2,1)S(1)}, bf16[1024,2048]{1,0:T(8,128)(2,1)S(1)}, u32[]{:S(2)}, u32[]{:S(2)}) collective-permute-start(bf16[1024,2048]{1,0:T(8,128)(2,1)S(1)} %get-tuple-element.281), channel_id=1, source_target_pairs={{0,1},{1,0},{2,3},{3,2},{4,5},{5,4},{6,7},{7,6},{8,9},{9,8},{10,11... | collective-permute-start | bytes 12582920 | tf_op jit(solution)/shard_map/ppermute | solution.py:581
  356.1 39.2 %collective-permute-start.6 = (bf16[512,1024]{1,0:T(8,128)(2,1)S(1)}, bf16[512,1024]{1,0:T(8,128)(2,1)S(1)}, u32[]{:S(2)}, u32[]{:S(2)}) collective-permute-start(bf16[512,1024]{1,0:T(8,128)(2,1)S(1)} %get-tuple-element.275), channel_id=1, source_target_pairs={{0,2},{1,3},{2,0},{3,1},{4,6},{5,7},{6,4},{7,5},{8,10},{9,11},{10,... | collective-permute-start | bytes 3145736 | tf_op jit(solution)/shard_map/ppermute | solution.py:581
  357.6 37.7 %collective-permute-start.7 = (bf16[512,1024]{1,0:T(8,128)(2,1)S(1)}, bf16[512,1024]{1,0:T(8,128)(2,1)S(1)}, u32[]{:S(2)}, u32[]{:S(2)}) collective-permute-start(bf16[512,1024]{1,0:T(8,128)(2,1)S(1)} %get-tuple-element.276), channel_id=1, source_target_pairs={{0,4},{1,5},{2,6},{3,7},{4,0},{5,1},{6,2},{7,3},{8,12},{9,13},{10,... | collective-permute-start | bytes 3145736 | tf_op jit(solution)/shard_map/ppermute | solution.py:581
  358.1 37.1 %collective-permute-start.4 = (bf16[256,1024]{1,0:T(8,128)(2,1)S(1)}, bf16[256,1024]{1,0:T(8,128)(2,1)S(1)}, u32[]{:S(2)}, u32[]{:S(2)}) collective-permute-start(bf16[256,1024]{1,0:T(8,128)(2,1)S(1)} %get-tuple-element.273), channel_id=1, source_target_pairs={{0,4},{1,5},{2,6},{3,7},{4,0},{5,1},{6,2},{7,3},{8,12},{9,13},{10,... | collective-permute-start | bytes 1572872 | tf_op jit(solution)/shard_map/ppermute | solution.py:581
  359.6 35.7 %collective-permute-start.5 = (bf16[256,1024]{1,0:T(8,128)(2,1)S(1)}, bf16[256,1024]{1,0:T(8,128)(2,1)S(1)}, u32[]{:S(2)}, u32[]{:S(2)}) collective-permute-start(bf16[256,1024]{1,0:T(8,128)(2,1)S(1)} %get-tuple-element.274), channel_id=1, source_target_pairs={{0,2},{1,3},{2,0},{3,1},{4,6},{5,7},{6,4},{7,5},{8,10},{9,11},{10,... | collective-permute-start | bytes 1572872 | tf_op jit(solution)/shard_map/ppermute | solution.py:581
  395.4 23.8 %collective-permute-start.11 = (bf16[1024,1280]{1,0:T(8,128)(2,1)S(1)}, bf16[1024,1280]{1,0:T(8,128)(2,1)}, u32[]{:S(2)}, u32[]{:S(2)}) collective-permute-start(bf16[1024,1280]{1,0:T(8,128)(2,1)S(1)} %get-tuple-element.295), channel_id=1, source_target_pairs={{0,1},{1,0},{2,3},{3,2},{4,5},{5,4},{6,7},{7,6},{8,9},{9,8},{10,11... | collective-permute-start | bytes 7864328 | tf_op jit(solution)/shard_map/ppermute | solution.py:581
  401.2 17.9 %collective-permute-start.9 = (bf16[256,1024]{1,0:T(8,128)(2,1)}, bf16[256,1024]{1,0:T(8,128)(2,1)}, u32[]{:S(2)}, u32[]{:S(2)}) collective-permute-start(bf16[256,1024]{1,0:T(8,128)(2,1)} %get-tuple-element.293), channel_id=1, source_target_pairs={{0,4},{1,5},{2,6},{3,7},{4,0},{5,1},{6,2},{7,3},{8,12},{9,13},{10,... | collective-permute-start | bytes 1572872 | tf_op jit(solution)/shard_map/ppermute | solution.py:581
  419.1 61.7 %reduce-scatter.6.cloned.1.call-start = ((), (), s32[]{:S(2)}) async-start(), calls=%async_computation.6 | async-start | bytes 1310720 | tf_op jit(solution)/shard_map/reduce_scatter | solution.py:976
  419.2 39.2 %collective-permute-start.12 = (bf16[512,1024]{1,0:T(8,128)(2,1)}, bf16[512,1024]{1,0:T(8,128)(2,1)}, u32[]{:S(2)}, u32[]{:S(2)}) collective-permute-start(bf16[512,1024]{1,0:T(8,128)(2,1)} %copy-done.32), channel_id=1, source_target_pairs={{0,2},{1,3},{2,0},{3,1},{4,6},{5,7},{6,4},{7,5},{8,10},{9,11},{10,... | collective-permute-start | bytes 3145736 | tf_op jit(solution)/shard_map/ppermute | solution.py:581
  420.7 37.7 %collective-permute-start.13 = (bf16[512,1024]{1,0:T(8,128)(2,1)}, bf16[512,1024]{1,0:T(8,128)(2,1)}, u32[]{:S(2)}, u32[]{:S(2)}) collective-permute-start(bf16[512,1024]{1,0:T(8,128)(2,1)} %copy-done.31), channel_id=1, source_target_pairs={{0,4},{1,5},{2,6},{3,7},{4,0},{5,1},{6,2},{7,3},{8,12},{9,13},{10,... | collective-permute-start | bytes 3145736 | tf_op jit(solution)/shard_map/ppermute | solution.py:581
  449.5 77.7 %reduce-scatter.8.cloned.1.call-start = ((), (), s32[]{:S(2)}) async-start(), calls=%async_computation.7 | async-start | bytes 1310720 | tf_op jit(solution)/shard_map/reduce_scatter | solution.py:976
  458.4 22.4 %collective-permute-start.16 = (bf16[1024,768]{1,0:T(8,128)(2,1)S(1)}, bf16[1024,768]{1,0:T(8,128)(2,1)}, u32[]{:S(2)}, u32[]{:S(2)}) collective-permute-start(bf16[1024,768]{1,0:T(8,128)(2,1)S(1)} %get-tuple-element.326), channel_id=1, source_target_pairs={{0,1},{1,0},{2,3},{3,2},{4,5},{5,4},{6,7},{7,6},{8,9},{9,8},{10,11... | collective-permute-start | bytes 4718600 | tf_op jit(solution)/shard_map/ppermute | solution.py:581
  461.2 18.1 %collective-permute-start.14 = (bf16[256,1024]{1,0:T(8,128)(2,1)S(1)}, bf16[256,1024]{1,0:T(8,128)(2,1)S(1)}, u32[]{:S(2)}, u32[]{:S(2)}) collective-permute-start(bf16[256,1024]{1,0:T(8,128)(2,1)S(1)} %get-tuple-element.324), channel_id=1, source_target_pairs={{0,4},{1,5},{2,6},{3,7},{4,0},{5,1},{6,2},{7,3},{8,12},{9,13},{10,... | collective-permute-start | bytes 1572872 | tf_op jit(solution)/shard_map/ppermute | solution.py:581
  480.8 20.9 %collective-permute-start.17 = (bf16[512,640]{1,0:T(8,128)(2,1)S(1)}, bf16[512,640]{1,0:T(8,128)(2,1)}, u32[]{:S(2)}, u32[]{:S(2)}) collective-permute-start(bf16[512,640]{1,0:T(8,128)(2,1)S(1)} %get-tuple-element.338), channel_id=1, source_target_pairs={{0,2},{1,3},{2,0},{3,1},{4,6},{5,7},{6,4},{7,5},{8,10},{9,11},{10,... | collective-permute-start | bytes 1966088 | tf_op jit(solution)/shard_map/ppermute | solution.py:581
  482.2 19.5 %collective-permute-start.18 = (bf16[512,640]{1,0:T(8,128)(2,1)S(1)}, bf16[512,640]{1,0:T(8,128)(2,1)}, u32[]{:S(2)}, u32[]{:S(2)}) collective-permute-start(bf16[512,640]{1,0:T(8,128)(2,1)S(1)} %get-tuple-element.339), channel_id=1, source_target_pairs={{0,4},{1,5},{2,6},{3,7},{4,0},{5,1},{6,2},{7,3},{8,12},{9,13},{10,... | collective-permute-start | bytes 1966088 | tf_op jit(solution)/shard_map/ppermute | solution.py:581
  546.7 39.7 %collective-permute-start.40 = (f32[32,2048]{1,0:T(8,128)S(1)}, f32[32,2048]{1,0:T(8,128)S(1)}, u32[]{:S(2)}, u32[]{:S(2)}) collective-permute-start(f32[32,2048]{1,0:T(8,128)S(1)} %get-tuple-element.420), channel_id=1, source_target_pairs={{0,1},{1,0},{2,3},{3,2},{4,5},{5,4},{6,7},{7,6},{8,9},{9,8},{10,11... | collective-permute-start | bytes 786440 | tf_op jit(solution)/shard_map/ppermute | solution.py:581
  549.1 37.4 %collective-permute-start.41 = (f32[32,1280]{1,0:T(8,128)S(1)}, f32[32,1280]{1,0:T(8,128)S(1)}, u32[]{:S(2)}, u32[]{:S(2)}) collective-permute-start(f32[32,1280]{1,0:T(8,128)S(1)} %get-tuple-element.426), channel_id=1, source_target_pairs={{0,1},{1,0},{2,3},{3,2},{4,5},{5,4},{6,7},{7,6},{8,9},{9,8},{10,11... | collective-permute-start | bytes 491528 | tf_op jit(solution)/shard_map/ppermute | solution.py:581
  (97 other events, 651.1 us)
Sparse Core Ops, SparseCore 0:
  11.7 138.5 all-gather.2
  153.7 94.1 all-gather.4
  419.3 25.5 reduce-scatter.3
  449.6 25.3 reduce-scatter.5
  501.8 25.3 reduce-scatter.7
